TPU v7x, 256 devices: a whole 4x4x8 slice. The times are simulated.
256 devices in a mesh: gx: 16 (over z, x_lo), gz: 16 (over x_hi, y, core).
Axes of the slice: x: 4 (x_hi: 2, x_lo: 2; x = x_hi * 2 + x_lo), y: 4, z: 8, core: 2. Of those that a mesh axis runs over, the one named last changes fastest.
Arguments:
- moments: float32 [6, 2, 1024, 2048], P(None, None, 'gx', 'gz'), may hold values from 0.5 to 2
- scalars: float32 [12, 2, 1024, 2048], P(None, None, 'gx', 'gz'), may hold values from -4 to 4
- velocity: float32 [2, 2, 1024, 2048], P(None, None, 'gx', 'gz'), may hold values from -4 to 4
- diffusivity: float32 [18], replicated, may hold values from 0.05 to 0.5
- nucleation: float32 [2, 1024, 2048], P(None, 'gx', 'gz'), may hold values from 0.2 to 2
- growth: float32 [2, 1024, 2048], P(None, 'gx', 'gz'), may hold values from 0.1 to 1
Outputs:
- new_moments: float32 [6, 2, 1024, 2048], P(None, None, 'gx', 'gz')
- new_scalars: float32 [12, 2, 1024, 2048], P(None, None, 'gx', 'gz')
All inputs are finite; a program needn't handle non-finite values.
Results may differ from a plain program's by a relative error of at most 0.00002.
Values sent between devices are 32-bit elements; how exact they have to be, the bound alone decides.
No kernel may reach another device: no remote copies, remote signals or barrier semaphores. Data moves between devices by JAX's collectives and lax.ppermute only.
A program may use at most 64 MiB of HBM per device.

v0:
```python
import jax
import jax.numpy as jnp
from jax import lax
from jax.sharding import PartitionSpec as P

first_coef = (0.8, -0.2, 4.0 / 105.0, -1.0 / 280.0)
second_coef = (1.6, -0.2, 8.0 / 315.0, -1.0 / 560.0)
centre_coef = -205.0 / 72.0
time_step = 0.25


def with_halo(value, sides, width):
    for axis, dim in sides:
        peers, length = (lax.axis_size(axis), value.shape[dim])
        up = [(i, (i + 1) % peers) for i in range(peers)]
        down = [(j, i) for i, j in up]
        last = lax.slice_in_dim(value, length - width, length, axis=dim)
        initial = lax.slice_in_dim(value, 0, width, axis=dim)
        before = lax.ppermute(last, axis, up)
        after = lax.ppermute(initial, axis, down)
        value = jnp.concatenate([before, value, after], axis=dim)
    return value


def sources(state, nucl, grow):
    precursor = state[6]
    birth = nucl * precursor * precursor
    moms = state[:6]
    earlier = jnp.concatenate([jnp.zeros_like(moms[:1]), moms[:5]], axis=0)
    orders = (jnp.arange(6, dtype=jnp.int32).astype(jnp.float32) / 3.0).reshape(
        (6,) + (1,) * (moms.ndim - 1)
    )
    mom_src = 0.5 * birth + grow * orders * earlier - 0.3 * moms[0] * moms
    return jnp.concatenate([mom_src, (-0.2 * birth)[None], jnp.zeros_like(state[7:])], axis=0)


def region_rhs(centre, along_x, along_z, kappa, nucl, grow):
    width_x = centre.shape[2]
    width_z = centre.shape[3]
    flux_x = along_x[18:19] * along_x[:18]
    flux_z = along_z[19:20] * along_z[:18]
    state_x = along_x[:18]
    state_z = along_z[:18]
    conv = jnp.zeros_like(centre)
    lap = 2.0 * centre_coef * centre
    for m in range(1, 5):
        conv = conv + first_coef[m - 1] * (
            flux_x[:, :, 4 + m : 4 + m + width_x] - flux_x[:, :, 4 - m : 4 - m + width_x]
        )
        conv = conv + first_coef[m - 1] * (
            flux_z[:, :, :, 4 + m : 4 + m + width_z] - flux_z[:, :, :, 4 - m : 4 - m + width_z]
        )
        lap = lap + second_coef[m - 1] * (
            state_x[:, :, 4 + m : 4 + m + width_x]
            + state_x[:, :, 4 - m : 4 - m + width_x]
            + state_z[:, :, :, 4 + m : 4 + m + width_z]
            + state_z[:, :, :, 4 - m : 4 - m + width_z]
        )
    return -conv + kappa.reshape((18, 1, 1, 1)) * lap + sources(centre, nucl, grow)


def body(moments, scalars, velocity, diffusivity, nucleation, growth):

    def section_rate(stacked):
        along_x = with_halo(stacked, (("gx", 2),), 4)
        along_z = with_halo(stacked, (("gz", 3),), 4)
        return region_rhs(stacked[:18], along_x, along_z, diffusivity, nucleation, growth)

    start = jnp.concatenate([moments, scalars, velocity], axis=0)
    first_state = start[:18] + time_step * section_rate(start)
    second_rate = section_rate(jnp.concatenate([first_state, velocity], axis=0))
    result = 0.5 * start[:18] + 0.5 * (first_state + time_step * second_rate)
    return (result[:6], result[6:])


def solution(mesh):
    return jax.shard_map(
        body,
        mesh=mesh,
        in_specs=(
            P(None, None, "gx", "gz"),
            P(None, None, "gx", "gz"),
            P(None, None, "gx", "gz"),
            P(),
            P(None, "gx", "gz"),
            P(None, "gx", "gz"),
        ),
        out_specs=(P(None, None, "gx", "gz"), P(None, None, "gx", "gz")),
        check_vma=False,
    )
```

profile of v0, /device:TPU:25, one launch (start us, length us, event | category | flops | bytes accessed | tf_op | source)
XLA Modules:
  0.0 101.2 jit_solution(1740631533712398923)
XLA Ops:
  4.9 1.9 %fusion.91 = (f32[20,2,64,4]{3,2,1,0:T(8,128)}, f32[20,2,64,4]{3,2,1,0:T(8,128)}) fusion(f32[20,2,64,128]{3,2,1,0:T(8,128)S(1)} %constant_dynamic-update-slice_fusion.2), kind=kLoop, calls=%fused_computation.187 | loop fusion | bytes 163840 | tf_op jit(solution)/shard_map/slice | solution.py:18
  6.8 1.8 %copy.51 = f32[20,2,64,4]{2,0,3,1:T(8,128)S(1)} copy(f32[20,2,64,4]{3,2,1,0:T(8,128)} %get-tuple-element.13) | data formatting | bytes 81920
  8.7 3.0 %collective-permute-start.2 = (f32[20,2,64,4]{2,0,3,1:T(8,128)S(1)}, f32[20,2,64,4]{2,0,3,1:T(8,128)S(1)}, u32[]{:S(2)}, u32[]{:S(2)}) collective-permute-start(f32[20,2,64,4]{2,0,3,1:T(8,128)S(1)} %copy.51), channel_id=1, source_target_pairs={{0,1},{1,2},{2,3},{3,4},{4,5},{5,6},{6,7},{7,8},{8,9},{9,10},{10,1... | collective-permute-start | bytes 122888 | tf_op jit(solution)/shard_map/ppermute | solution.py:19
  11.7 1.8 %copy.52 = f32[20,2,64,4]{2,0,3,1:T(8,128)S(1)} copy(f32[20,2,64,4]{3,2,1,0:T(8,128)} %get-tuple-element.12) | data formatting | bytes 81920
  14.1 5.4 %collective-permute-start.1 = (f32[20,2,4,128]{3,0,2,1:T(8,128)S(1)}, f32[20,2,4,128]{3,0,2,1:T(8,128)S(1)}, u32[]{:S(2)}, u32[]{:S(2)}) collective-permute-start(f32[20,2,4,128]{3,0,2,1:T(8,128)S(1)} %copy.50), channel_id=1, source_target_pairs={{16,0},{32,16},{48,32},{64,48},{80,64},{96,80},{112,96},{128,112},... | collective-permute-start | bytes 245768 | tf_op jit(solution)/shard_map/ppermute | solution.py:20
  19.5 2.4 %collective-permute-done.3 = f32[20,2,64,4]{2,0,3,1:T(8,128)S(1)} collective-permute-done((f32[20,2,64,4]{2,0,3,1:T(8,128)S(1)}, f32[20,2,64,4]{2,0,3,1:T(8,128)S(1)}, u32[]{:S(2)}, u32[]{:S(2)}) %collective-permute-start.3) | collective-permute-done | bytes 40992 | tf_op jit(solution)/shard_map/ppermute | solution.py:20
  21.9 1.6 %copy.32 = f32[20,2,64,4]{3,2,1,0:T(8,128)} copy(f32[20,2,64,4]{2,0,3,1:T(8,128)S(1)} %collective-permute-done.3) | data formatting | bytes 81920 | tf_op jit(solution)/shard_map/ppermute | solution.py:20
  23.5 1.6 %copy.31 = f32[20,2,64,4]{3,2,1,0:T(8,128)} copy(f32[20,2,64,4]{2,0,3,1:T(8,128)S(1)} %collective-permute-done.2) | data formatting | bytes 81920 | tf_op jit(solution)/shard_map/ppermute | solution.py:19
  25.0 1.1 %maximum_bitcast_fusion.1 = f32[2,64,136]{2,1,0:T(8,128)S(1)} fusion(f32[20,2,64,4]{3,2,1,0:T(8,128)} %copy.32, f32[20,2,64,128]{3,2,1,0:T(8,128)S(1)} %constant_dynamic-update-slice_fusion.2, f32[20,2,64,4]{3,2,1,0:T(8,128)} %copy.31), kind=kLoop, calls=%fused_computation.166 | loop fusion | flops 34816 | bytes 1462272 | tf_op jit(solution)/shard_map/mul | solution.py:41
  29.2 7.3 %fusion.15 = f32[18,2,64,128]{3,2,1,0:T(8,128)S(1)} fusion(f32[18,2,64,128]{3,2,1,0:T(8,128)S(1)} %copy-done.7, f32[20,2,64,128]{3,2,1,0:T(8,128)S(1)} %constant_dynamic-update-slice_fusion.2, f32[20,2,4,128]{3,2,1,0:T(4,128)S(1)} %copy.27, f32[20,2,4,128]{3,2,1,0:T(4,128)S(1)} %copy.28, f32[20,2,64,4]{3,2,1,0:T(8,128)S(1)} %copy-done.3, ...), kind=kLoop, calls=%fused_computation.55 | loop fusion | flops 19759104 | bytes 23249040 | tf_op jit(solution)/shard_map/add | solution.py:70
  37.6 1.5 %pad_maximum_fusion.12 = (f32[20,2,64,4]{3,2,1,0:T(8,128)}, f32[20,2,64,4]{3,2,1,0:T(8,128)S(1)}) fusion(f32[2,2,64,128]{3,2,1,0:T(8,128)S(1)} %copy-done.5, f32[18,2,64,128]{3,2,1,0:T(8,128)S(1)} %fusion.15), kind=kLoop, calls=%fused_computation.42 | loop fusion | flops 20480 | bytes 1392640 | tf_op jit(solution)/shard_map/concatenate | solution.py:71
  40.4 4.9 %collective-permute-start.5 = (f32[20,2,4,128]{3,0,2,1:T(8,128)}, f32[20,2,4,128]{3,0,2,1:T(8,128)}, u32[]{:S(2)}, u32[]{:S(2)}) collective-permute-start(f32[20,2,4,128]{3,0,2,1:T(8,128)} %copy.54), channel_id=1, source_target_pairs={{16,0},{32,16},{48,32},{64,48},{80,64},{96,80},{112,96},{128,112},... | collective-permute-start | bytes 245768 | tf_op jit(solution)/shard_map/ppermute | solution.py:20
  45.4 2.6 %copy.56 = f32[20,2,64,4]{2,0,3,1:T(8,128)} copy(f32[20,2,64,4]{3,2,1,0:T(8,128)} %get-tuple-element.10) | data formatting | bytes 81920
  48.0 1.2 %copy.55 = f32[20,2,64,4]{2,0,3,1:T(8,128)} copy(f32[20,2,64,4]{3,2,1,0:T(8,128)S(1)} %get-tuple-element.11) | data formatting | bytes 81920
  49.1 3.1 %collective-permute-start.6 = (f32[20,2,64,4]{2,0,3,1:T(8,128)}, f32[20,2,64,4]{2,0,3,1:T(8,128)}, u32[]{:S(2)}, u32[]{:S(2)}) collective-permute-start(f32[20,2,64,4]{2,0,3,1:T(8,128)} %copy.55), channel_id=1, source_target_pairs={{0,1},{1,2},{2,3},{3,4},{4,5},{5,6},{6,7},{7,8},{8,9},{9,10},{10,1... | collective-permute-start | bytes 122888 | tf_op jit(solution)/shard_map/ppermute | solution.py:19
  53.2 7.0 %collective-permute-done.7 = f32[20,2,64,4]{2,0,3,1:T(8,128)} collective-permute-done((f32[20,2,64,4]{2,0,3,1:T(8,128)}, f32[20,2,64,4]{2,0,3,1:T(8,128)}, u32[]{:S(2)}, u32[]{:S(2)}) %collective-permute-start.7) | collective-permute-done | bytes 40992 | tf_op jit(solution)/shard_map/ppermute | solution.py:20
  60.2 1.4 %copy.44 = f32[20,2,64,4]{3,2,1,0:T(8,128)S(1)} copy(f32[20,2,64,4]{2,0,3,1:T(8,128)} %collective-permute-done.7) | data formatting | bytes 81920 | tf_op jit(solution)/shard_map/ppermute | solution.py:20
  61.5 2.4 %copy.43 = f32[20,2,64,4]{3,2,1,0:T(8,128)} copy(f32[20,2,64,4]{2,0,3,1:T(8,128)} %collective-permute-done.6) | data formatting | bytes 81920 | tf_op jit(solution)/shard_map/ppermute | solution.py:19
  65.3 2.4 %fusion = f32[18,2,64,136]{3,2,1,0:T(8,128)} fusion(f32[20,2,64,4]{3,2,1,0:T(8,128)S(1)} %copy.44, f32[20,2,64,4]{3,2,1,0:T(8,128)S(1)} %copy-done.4, f32[2,2,64,128]{3,2,1,0:T(8,128)S(1)} %copy-done.5, f32[18,2,64,128]{3,2,1,0:T(8,128)S(1)} %copy-done.1, f32[2,64,136]{2,1,0:T(8,128)S(1)} %maximum_bitcast_fusion), kind=kLoop, calls=%fused_computation.21 | loop fusion | flops 1253376 | bytes 2715648 | tf_op jit(solution)/shard_map/mul | solution.py:41
  67.8 3.2 %pad_maximum_fusion = (f32[20,2,64,132]{3,2,1,0:T(8,128)}, f32[20,2,64,132]{3,2,1,0:T(8,128)}) fusion(f32[20,2,64,4]{3,2,1,0:T(8,128)S(1)} %copy.44, f32[2,2,64,128]{3,2,1,0:T(8,128)S(1)} %copy-done.5, f32[18,2,64,128]{3,2,1,0:T(8,128)S(1)} %copy-done.1, f32[20,2,64,4]{3,2,1,0:T(8,128)S(1)} %copy-done.4), kind=kLoop, calls=%fused_computation.18 | loop fusion | flops 1351680 | bytes 4096000 | tf_op jit(solution)/shard_map/concatenate | solution.py:21
  72.9 2.0 %pad_maximum_fusion.6 = (f32[20,2,68,128]{3,2,1,0:T(8,128)}, f32[20,2,68,128]{3,2,1,0:T(8,128)}) fusion(f32[20,2,4,128]{3,2,1,0:T(4,128)S(1)} %copy.40, f32[2,2,64,128]{3,2,1,0:T(8,128)S(1)} %copy-done.5, f32[18,2,64,128]{3,2,1,0:T(8,128)S(1)} %copy-done.1, f32[20,2,4,128]{3,2,1,0:T(4,128)S(1)} %copy.39), kind=kLoop, calls=%fused_computation.27 | loop fusion | flops 1392640 | bytes 4259840 | tf_op jit(solution)/shard_map/concatenate | solution.py:21
  75.5 21.8 %fusion.45 = f32[18,2,64,128]{3,2,1,0:T(8,128)} fusion(f32[18,2,64,128]{3,2,1,0:T(8,128)} %copy-done.6, f32[18,2,64,128]{3,2,1,0:T(8,128)S(1)} %copy-done.1, f32[20,2,64,132]{3,2,1,0:T(8,128)} %get-tuple-element.9, f32[20,2,64,132]{3,2,1,0:T(8,128)} %get-tuple-element.8, f32[20,2,68,128]{3,2,1,0:T(8,128)} %get-tuple-element.5, ...), kind=kLoop, calls=%fused_computation.86 | loop fusion | flops 15630336 | bytes 41746576 | tf_op jit(solution)/shard_map/add | solution.py:72
  97.4 1.8 %slice.514 = f32[6,2,64,128]{3,2,1,0:T(8,128)} slice(f32[18,2,64,128]{3,2,1,0:T(8,128)} %fusion.45), slice={[0:6], [0:2], [0:64], [0:128]} | slice | bytes 786432 | tf_op jit(solution)/shard_map/slice | solution.py:73
  99.1 2.1 %slice.515 = f32[12,2,64,128]{3,2,1,0:T(8,128)} slice(f32[18,2,64,128]{3,2,1,0:T(8,128)} %fusion.45), slice={[6:18], [0:2], [0:64], [0:128]} | slice | bytes 1572864 | tf_op jit(solution)/shard_map/slice | solution.py:73
  (77 shorter events, 14.9 us)
Async XLA Ops:
  0.6 2.0 %copy-start.8 = (f32[6,2,64,128]{3,2,1,0:T(8,128)S(1)}, f32[6,2,64,128]{3,2,1,0:T(8,128)}, u32[]{:S(2)}) copy-start(f32[6,2,64,128]{3,2,1,0:T(8,128)} %param.6) | copy-start | bytes 1179652
  0.6 2.0 %slice-start.1 = ((f32[6,2,64,128]{3,2,1,0:T(8,128)}), f32[5,2,64,128]{3,2,1,0:T(8,128)S(1)}, s32[]{:S(2)}) async-start(f32[6,2,64,128]{3,2,1,0:T(8,128)} %param.6), calls=%async_computation.1 | async-start | bytes 655360 | tf_op jit(solution)/shard_map/slice | solution.py:29
  0.7 3.0 %copy-start.16 = (f32[6]{0:T(128)}, f32[6]{0:T(128)S(1)}, u32[]{:S(2)}) copy-start(f32[6]{0:T(128)S(1)} %convert_multiply_fusion) | copy-start | bytes 76
  1.6 2.0 %copy-start.9 = (f32[12,2,64,128]{3,2,1,0:T(8,128)S(1)}, f32[12,2,64,128]{3,2,1,0:T(8,128)}, u32[]{:S(2)}) copy-start(f32[12,2,64,128]{3,2,1,0:T(8,128)} %param.7) | copy-start | bytes 2359300
  3.6 1.2 %copy-start.5 = (f32[2,2,64,128]{3,2,1,0:T(8,128)S(1)}, f32[2,2,64,128]{3,2,1,0:T(8,128)}, u32[]{:S(2)}) copy-start(f32[2,2,64,128]{3,2,1,0:T(8,128)} %param.8) | copy-start | bytes 393220
  8.7 14.8 %collective-permute-start.2 = (f32[20,2,64,4]{2,0,3,1:T(8,128)S(1)}, f32[20,2,64,4]{2,0,3,1:T(8,128)S(1)}, u32[]{:S(2)}, u32[]{:S(2)}) collective-permute-start(f32[20,2,64,4]{2,0,3,1:T(8,128)S(1)} %copy.51), channel_id=1, source_target_pairs={{0,1},{1,2},{2,3},{3,4},{4,5},{5,6},{6,7},{7,8},{8,9},{9,10},{10,1... | collective-permute-start | bytes 122888 | tf_op jit(solution)/shard_map/ppermute | solution.py:19
  13.5 8.4 %collective-permute-start.3 = (f32[20,2,64,4]{2,0,3,1:T(8,128)S(1)}, f32[20,2,64,4]{2,0,3,1:T(8,128)S(1)}, u32[]{:S(2)}, u32[]{:S(2)}) collective-permute-start(f32[20,2,64,4]{2,0,3,1:T(8,128)S(1)} %copy.52), channel_id=1, source_target_pairs={{1,0},{2,1},{3,2},{4,3},{5,4},{6,5},{7,6},{8,7},{9,8},{10,9},{11,1... | collective-permute-start | bytes 122888 | tf_op jit(solution)/shard_map/ppermute | solution.py:20
  13.7 14.2 %collective-permute-start = (f32[20,2,4,128]{3,0,2,1:T(8,128)S(1)}, f32[20,2,4,128]{3,0,2,1:T(8,128)S(1)}, u32[]{:S(2)}, u32[]{:S(2)}) collective-permute-start(f32[20,2,4,128]{3,0,2,1:T(8,128)S(1)} %copy.49), channel_id=1, source_target_pairs={{0,16},{16,32},{32,48},{48,64},{64,80},{80,96},{96,112},{112,128},... | collective-permute-start | bytes 245768 | tf_op jit(solution)/shard_map/ppermute | solution.py:19
  14.1 13.8 %collective-permute-start.1 = (f32[20,2,4,128]{3,0,2,1:T(8,128)S(1)}, f32[20,2,4,128]{3,0,2,1:T(8,128)S(1)}, u32[]{:S(2)}, u32[]{:S(2)}) collective-permute-start(f32[20,2,4,128]{3,0,2,1:T(8,128)S(1)} %copy.50), channel_id=1, source_target_pairs={{16,0},{32,16},{48,32},{64,48},{80,64},{96,80},{112,96},{128,112},... | collective-permute-start | bytes 245768 | tf_op jit(solution)/shard_map/ppermute | solution.py:20
  19.5 8.6 %copy-start.14 = (f32[18]{0:T(128)}, f32[18]{0:T(128)S(1)}, u32[]{:S(2)}) copy-start(f32[18]{0:T(128)S(1)} %pad.29.clone) | copy-start | bytes 220
  25.0 1.4 %copy-start.2 = (f32[20,2,64,4]{3,2,1,0:T(8,128)S(1)}, f32[20,2,64,4]{3,2,1,0:T(8,128)}, u32[]{:S(2)}) copy-start(f32[20,2,64,4]{3,2,1,0:T(8,128)} %copy.32) | copy-start | bytes 122884
  25.0 1.8 %copy-start.3 = (f32[20,2,64,4]{3,2,1,0:T(8,128)S(1)}, f32[20,2,64,4]{3,2,1,0:T(8,128)}, u32[]{:S(2)}) copy-start(f32[20,2,64,4]{3,2,1,0:T(8,128)} %copy.31) | copy-start | bytes 122884
  27.9 1.3 %copy-start.7 = (f32[18,2,64,128]{3,2,1,0:T(8,128)S(1)}, f32[18,2,64,128]{3,2,1,0:T(8,128)}, u32[]{:S(2)}) copy-start(f32[18,2,64,128]{3,2,1,0:T(8,128)} %copy-done.6) | copy-start | bytes 3538948
  27.9 1.3 %copy-start.12 = (f32[18]{0:T(128)S(1)}, f32[18]{0:T(128)}, u32[]{:S(2)}) copy-start(f32[18]{0:T(128)} %param.9) | copy-start | bytes 220
  29.2 7.3 %copy-start.11 = (f32[2,64,128]{2,1,0:T(8,128)S(1)}, f32[2,64,128]{2,1,0:T(8,128)}, u32[]{:S(2)}) copy-start(f32[2,64,128]{2,1,0:T(8,128)} %param.10) | copy-start | bytes 196612
  40.4 30.6 %collective-permute-start.4 = (f32[20,2,4,128]{3,0,2,1:T(8,128)}, f32[20,2,4,128]{3,0,2,1:T(8,128)}, u32[]{:S(2)}, u32[]{:S(2)}) collective-permute-start(f32[20,2,4,128]{3,0,2,1:T(8,128)} %copy.53), channel_id=1, source_target_pairs={{0,16},{16,32},{32,48},{48,64},{64,80},{80,96},{96,112},{112,128},... | collective-permute-start | bytes 245768 | tf_op jit(solution)/shard_map/ppermute | solution.py:19
  40.4 31.5 %collective-permute-start.5 = (f32[20,2,4,128]{3,0,2,1:T(8,128)}, f32[20,2,4,128]{3,0,2,1:T(8,128)}, u32[]{:S(2)}, u32[]{:S(2)}) collective-permute-start(f32[20,2,4,128]{3,0,2,1:T(8,128)} %copy.54), channel_id=1, source_target_pairs={{16,0},{32,16},{48,32},{64,48},{80,64},{96,80},{112,96},{128,112},... | collective-permute-start | bytes 245768 | tf_op jit(solution)/shard_map/ppermute | solution.py:20
  45.4 6.8 %copy-start.1 = (f32[18,2,64,128]{3,2,1,0:T(8,128)S(1)}, f32[18,2,64,128]{3,2,1,0:T(8,128)}, u32[]{:S(2)}) copy-start(f32[18,2,64,128]{3,2,1,0:T(8,128)} %copy-done) | copy-start | bytes 3538948
  45.4 6.8 %slice-start = ((f32[18,2,64,128]{3,2,1,0:T(8,128)}), f32[5,2,64,128]{3,2,1,0:T(8,128)S(1)}, s32[]{:S(2)}) async-start(f32[18,2,64,128]{3,2,1,0:T(8,128)} %copy-done), calls=%async_computation | async-start | bytes 655360 | tf_op jit(solution)/shard_map/slice | solution.py:29
  45.4 6.8 %copy-start.10 = (f32[2,64,128]{2,1,0:T(8,128)S(1)}, f32[2,64,128]{2,1,0:T(8,128)}, u32[]{:S(2)}) copy-start(f32[2,64,128]{2,1,0:T(8,128)} %param.11) | copy-start | bytes 196612
  45.4 6.9 %copy-start.17 = (f32[6]{0:T(128)S(1)}, f32[6]{0:T(128)}, u32[]{:S(2)}) copy-start(f32[6]{0:T(128)} %copy-done.16) | copy-start | bytes 76
  49.1 12.4 %collective-permute-start.6 = (f32[20,2,64,4]{2,0,3,1:T(8,128)}, f32[20,2,64,4]{2,0,3,1:T(8,128)}, u32[]{:S(2)}, u32[]{:S(2)}) collective-permute-start(f32[20,2,64,4]{2,0,3,1:T(8,128)} %copy.55), channel_id=1, source_target_pairs={{0,1},{1,2},{2,3},{3,4},{4,5},{5,6},{6,7},{7,8},{8,9},{9,10},{10,1... | collective-permute-start | bytes 122888 | tf_op jit(solution)/shard_map/ppermute | solution.py:19
  52.2 8.0 %collective-permute-start.7 = (f32[20,2,64,4]{2,0,3,1:T(8,128)}, f32[20,2,64,4]{2,0,3,1:T(8,128)}, u32[]{:S(2)}, u32[]{:S(2)}) collective-permute-start(f32[20,2,64,4]{2,0,3,1:T(8,128)} %copy.56), channel_id=1, source_target_pairs={{1,0},{2,1},{3,2},{4,3},{5,4},{6,5},{7,6},{8,7},{9,8},{10,9},{11,1... | collective-permute-start | bytes 122888 | tf_op jit(solution)/shard_map/ppermute | solution.py:20
  64.0 1.3 %copy-start.4 = (f32[20,2,64,4]{3,2,1,0:T(8,128)S(1)}, f32[20,2,64,4]{3,2,1,0:T(8,128)}, u32[]{:S(2)}) copy-start(f32[20,2,64,4]{3,2,1,0:T(8,128)} %copy.43) | copy-start | bytes 122884
  (4 other events, 3.4 us)
where the time goes:
time: 102 us; the launch traced here: 101 us
  other arithmetic  46.5 us (46%)
  local copies, waits for them, and re-layouts  27.5 us (27%)
  starting transfers between devices  16.9 us (17%)
  waiting for transfers between devices  9.35 us (9%)
    add x1, other arithmetic, body(): result = 0.5 * start[:18] + 0.5 * (first_state + time_step * second_rate)  21.8 us
    unnamed x45, local copies, waits for them, and re-layouts  12.7 us
    ppermute x4, starting transfers between devices, with_halo(): after = lax.ppermute(initial, axis, down)  10.4 us
    ppermute x4, waiting for transfers between devices, with_halo(): after = lax.ppermute(initial, axis, down)  9.34 us
    add x1, other arithmetic, body(): first_state = start[:18] + time_step * section_rate(start)  7.3 us
    ppermute x4, starting transfers between devices, with_halo(): before = lax.ppermute(last, axis, up)  6.47 us
    mul x4, other arithmetic, region_rhs(): flux_z = along_z[19:20] * along_z[:18]  5.62 us
    concatenate x2, other arithmetic, with_halo(): value = jnp.concatenate([before, value, after], axis=dim)  5.2 us
  transfers between devices with their start and end apart: 8, of which 2 were waited for; matrix products, arithmetic and copies ran while one was open for 23% of the time, Pallas kernels for 0%

commit v1 on v0

v1 whole, which is shorter than its diff:
```python
import jax
import jax.numpy as jnp
from jax import lax
from jax.experimental import pallas as pl
from jax.experimental.pallas import tpu as pltpu
from jax.sharding import PartitionSpec as P

first_coef = (0.8, -0.2, 4.0 / 105.0, -1.0 / 280.0)
second_coef = (1.6, -0.2, 8.0 / 315.0, -1.0 / 560.0)
centre_coef = -205.0 / 72.0
time_step = 0.25

ROWS = 64
F32 = jnp.float32


def lanes(shape=(8, 128)):
    return lax.broadcasted_iota(jnp.int32, shape, len(shape) - 1)


def roll(x, by):
    by = by % 128
    return x if by == 0 else pltpu.roll(x, by, 1)


def plane_ref(refs, p, s):
    mom, sca, vel, nuc, gro = refs
    c, ny = s // 2, s % 2
    if p < 9:
        f = p + 9 * c
        return mom.at[f, ny] if f < 6 else sca.at[f - 6, ny]
    if p == 9:
        return vel.at[c, ny]
    return (nuc, gro)[c].at[ny]


def pack_z(mom, sca, vel, nuc, gro, zl, zr):
    refs = (mom, sca, vel, nuc, gro)
    block = lanes() // 8

    def row(r, _):
        at = pl.ds(pl.multiple_of(r * 8, 8), 8)
        for t in range(3):
            left = right = jnp.zeros((8, 128), F32)
            for j in range(4):
                p = 4 * t + j
                if p > 10:
                    continue
                for s in range(4):
                    b = 4 * s + j
                    tile = plane_ref(refs, p, s)[at, :]
                    left = jnp.where(block == b, roll(tile, 8 * b), left)
                    right = jnp.where(block == b, roll(tile, 8 * b + 8), right)
            zl[t, at, :] = left
            zr[t, at, :] = right
        return _

    lax.fori_loop(0, 8, row, 0)


def pack_x(mom, sca, vel, nuc, gro, up, down):
    for msg, lo, part in ((down, 0, 0), (up, 56, 60)):
        for f in range(18):
            src = mom.at[f] if f < 6 else sca.at[f - 6]
            for ny in range(2):
                msg[2 * f + ny] = src[ny, lo : lo + 8, :]
        for c in range(2):
            for ny in range(2):
                msg[36 + 2 * c + ny] = vel[c, ny, lo : lo + 8, :]
        for ny in range(2):
            msg[40 + ny, 0:4, :] = nuc[ny, part : part + 4, :]
            msg[40 + ny, 4:8, :] = gro[ny, part : part + 4, :]


def edge_packs(zl, zr, from_left, from_right, up_in, down_in, packs, up, down, buf, sems):
    del up_in, down_in
    sub = (lanes() // 8) % 4
    for p in range(11):
        t, j = p // 4, p % 4
        for r in range(0, 64, 8):
            e = roll(from_left[t, r : r + 8, :], -8 * j)
            e = jnp.where(sub == 1, roll(zl[t, r : r + 8, :], 8 - 8 * j), e)
            e = jnp.where(sub == 2, roll(zr[t, r : r + 8, :], 16 - 8 * j), e)
            e = jnp.where(sub == 3, roll(from_right[t, r : r + 8, :], 24 - 8 * j), e)
            packs[p, r : r + 8, :] = e
            if p < 10:
                at = slice(4 * (p % 2), 4 * (p % 2) + 4)
                if r == 0:
                    buf[0, p // 2, at, :] = e[0:4]
                if r == 56:
                    buf[1, p // 2, at, :] = e[4:8]
    copies = [
        pltpu.make_async_copy(buf.at[k], msg.at[pl.ds(42, 5)], sems.at[k])
        for k, msg in enumerate((down, up))
    ]
    for copy in copies:
        copy.start()
    for copy in copies:
        copy.wait()


def transport(q, g, q_at, f_at, kappa, scale):
    k = kappa * scale
    lap = (2.0 * centre_coef) * q
    conv = None
    acc = None
    for m in range(1, 5):
        a, b = first_coef[m - 1] * scale, second_coef[m - 1]
        lap = lap + b * (q_at(m) + q_at(-m))
        c = a * (f_at(-m) - f_at(m))
        conv = c if conv is None else conv + c
        kq = (k * b) * q
        ag = a * g
        z = roll(kq - ag, -m) + roll(kq + ag, m)
        acc = z if acc is None else acc + z
    return k * lap + conv + acc


def correction(q, g, kappa, scale):
    lane = lanes() % 32
    low = lane < 16
    outer = ((lane >= 4) & (lane < 8)) | ((lane >= 24) & (lane < 28))

    def gap(x):
        return jnp.where(outer, x - jnp.where(low, roll(x, -16), roll(x, 16)), 0.0)

    dq, dg = gap(q), gap(g)
    dg = jnp.where(low, dg, -dg)
    k = kappa * scale
    left = right = None
    for m in range(1, 5):
        both = (k * second_coef[m - 1]) * dq + (first_coef[m - 1] * scale) * dg
        one, two = roll(both, m + 16), roll(both, -m)
        left = one if left is None else left + one
        right = two if right is None else right + two
    return jnp.where(lane < 24, right, left)


def unpack(tile, s):
    lane = lanes()
    return jnp.where((lane < 4) | (lane >= 124), roll(tile, 104 - 32 * s), 0.0)


def sources(get, nucl, grow, scale):
    y = get(6)
    birth = nucl * y * y
    first = get(0)
    moms = [first] + [get(k) for k in range(1, 6)]
    half = (0.5 * scale) * birth
    sink = (0.3 * scale) * first
    out = []
    for k in range(6):
        s = half - sink * moms[k]
        if k:
            s = s + (scale * k / 3.0) * grow * moms[k - 1]
        out.append(s)
    return out + [(-0.2 * scale) * birth]


def pack_sources(get, ng, scale):
    low = lanes() < 64
    nucl = jnp.where(low, ng, 0.0)
    grow = jnp.where(low, roll(ng, 64), 0.0)
    y = get(6)
    birth = nucl * y * y
    moms = [get(k) for k in range(6)]
    sink = jnp.where(low, (0.3 * scale) * moms[0], 0.0)
    out = []
    for k in range(6):
        s = (0.5 * scale) * birth - sink * moms[k]
        if k:
            s = s + (scale * k / 3.0) * grow * moms[k - 1]
        out.append(s)
    return out + [(-0.2 * scale) * birth]


def pack_velocity(tile):
    low = lanes() < 64
    other = roll(tile, 64)
    return jnp.where(low, tile, other), jnp.where(low, other, tile)


def pack_kappa(kappa, p):
    return jnp.where(lanes() < 64, kappa[p], kappa[p + 9])


def ds(start, size):
    return slice(start, start + size)


def pack_stage(q, pu, pw, png, kappa, f, cor, dest, rows, base, scale):
    first, last = rows[0], rows[-1] + 8

    def one(p, _):
        kap = pack_kappa(kappa, p)
        lo, hi = max(first - 4, 0), last + 4
        for r in range(lo // 8 * 8, hi, 8):
            f[ds(r, 8), :] = pu[ds(r, 8), :] * q[p, ds(r, 8), :]
        for r in rows:
            v = q[p, ds(r, 8), :]
            g = pw[ds(r, 8), :] * v
            cor[p, ds(r - base, 8), :] = correction(v, g, kap, scale)
            rate = transport(
                v, g, lambda m: q[p, ds(r + m, 8), :], lambda m: f[ds(r + m, 8), :], kap, scale
            )
            dest[p, ds(r - base, 8), :] = v + rate
        return _

    lax.fori_loop(0, 9, one, 0)
    for r in rows:
        src = pack_sources(lambda k: q[k, ds(r, 8), :], png[ds(r, 8), :], scale)
        for k in range(7):
            dest[k, ds(r - base, 8), :] += src[k]


def planes(p):
    for slot in range(4):
        field, ny = p + 9 * (slot // 2), slot % 2
        yield 2 * field + ny, field, ny, slot


def interior(
    kappa, mom, sca, vel, nuc, gro, packs, out_mom, out_sca, edge, pack_edge,
    q, q1, f, pu, pw, pq1, cor, half,
):
    for k in range(18):
        src = mom.at[k] if k < 6 else sca.at[k - 6]
        for ny in range(2):
            q[2 * k + ny] = src[ny]
    for r in range(0, 64, 8):
        pu[ds(r, 8), :], pw[ds(r, 8), :] = pack_velocity(packs[9, ds(r, 8), :])
    dt = time_step

    rows = list(range(4, 60, 8))
    pack_stage(packs, pu, pw, packs.at[10], kappa, f, cor, pq1, rows, 4, dt)

    def one(p, _):
        for i, field, ny, slot in planes(p):
            kap = kappa[field]
            for r in range(0, 64, 8):
                f[ds(r, 8), :] = vel[0, ny, ds(r, 8), :] * q[i, ds(r, 8), :]
            for r in rows:
                v = q[i, ds(r, 8), :]
                g = vel[1, ny, ds(r, 8), :] * v
                rate = transport(
                    v, g, lambda m: q[i, ds(r + m, 8), :], lambda m: f[ds(r + m, 8), :], kap, dt
                )
                q1[i, ds(r - 4, 8), :] = v + rate + unpack(cor[p, ds(r - 4, 8), :], slot)
        return _

    lax.fori_loop(0, 9, one, 0)
    for ny in range(2):
        for r in rows:
            src = sources(
                lambda k: q[2 * k + ny, ds(r, 8), :],
                nuc[ny, ds(r, 8), :], gro[ny, ds(r, 8), :], dt,
            )
            for k in range(7):
                q1[2 * k + ny, ds(r - 4, 8), :] += src[k]
    for i in range(36):
        edge[0, i] = q1[i, 0:8, :]
        edge[1, i] = q1[i, 48:56, :]
    for p in range(9):
        pack_edge[0, p] = pq1[p, 0:8, :]
        pack_edge[1, p] = pq1[p, 48:56, :]

    scale = 0.5 * dt
    rows = list(range(8, 56, 8))

    def two(p, _):
        kap = pack_kappa(kappa, p)
        for r in rows:
            v = pq1[p, ds(r - 4, 8), :]
            cor[p, ds(r, 8), :] = correction(v, pw[ds(r, 8), :] * v, kap, scale)
        for i, field, ny, slot in planes(p):
            kap = kappa[field]
            for r in range(4, 60, 8):
                f[ds(r - 4, 8), :] = vel[0, ny, ds(r, 8), :] * q1[i, ds(r - 4, 8), :]
            for r in rows:
                v = q1[i, ds(r - 4, 8), :]
                g = vel[1, ny, ds(r, 8), :] * v
                rate = transport(
                    v, g, lambda m: q1[i, ds(r - 4 + m, 8), :], lambda m: f[ds(r - 4 + m, 8), :],
                    kap, scale,
                )
                add = unpack(cor[p, ds(r, 8), :], slot)
                half[i, ds(r, 8), :] = 0.5 * (q[i, ds(r, 8), :] + v) + rate + add
        return _

    lax.fori_loop(0, 9, two, 0)
    for ny in range(2):
        for r in rows:
            src = sources(
                lambda k: q1[2 * k + ny, ds(r - 4, 8), :],
                nuc[ny, ds(r, 8), :], gro[ny, ds(r, 8), :], scale,
            )
            for k in range(7):
                half[2 * k + ny, ds(r, 8), :] += src[k]
    for k in range(18):
        dst = out_mom.at[k] if k < 6 else out_sca.at[k - 6]
        for ny in range(2):
            dst[ny, 8:56, :] = half[2 * k + ny, 8:56, :]


def edges(
    kappa, mom, sca, vel, nuc, gro, packs, edge, pack_edge, above, below, in_mom, in_sca, out_mom, out_sca,
    q, q1, f, vq, v1, ng, pq, pu, pw, png, pq1, cor, half,
):
    del in_mom, in_sca
    step = pl.program_id(0)
    own8 = pl.ds(pl.multiple_of(8 * (1 - step), 8), 8)
    far8 = pl.ds(pl.multiple_of(8 * step, 8), 8)
    mid = slice(4, 12)
    dt = time_step

    def take(msg):
        for i in range(36):
            q[i, far8, :] = msg[i]
        for i in range(4):
            vq[i, far8, :] = msg[36 + i]
        for ny in range(2):
            ng[ny, mid, :] = nuc[ny]
            ng[2 + ny, mid, :] = gro[ny]

    @pl.when(step == 0)
    def _():
        take(above)
        for ny in range(2):
            ng[ny, 0:4, :] = above[40 + ny, 0:4, :]
            ng[2 + ny, 0:4, :] = above[40 + ny, 4:8, :]
        for c in range(2):
            for ny in range(2):
                v1[2 * c + ny, 0:4, :] = above[36 + 2 * c + ny, 4:8, :]
                v1[2 * c + ny, 4:16, :] = vel[c, ny, 0:12, :]
        for p in range(10):
            pq[p, 0:4, :] = jnp.zeros((4, 128), F32)
            pq[p, 4:8, :] = above[42 + p // 2, ds(4 * (p % 2), 4), :]

    @pl.when(step == 1)
    def _():
        take(below)
        for ny in range(2):
            ng[ny, 12:16, :] = below[40 + ny, 0:4, :]
            ng[2 + ny, 12:16, :] = below[40 + ny, 4:8, :]
        for c in range(2):
            for ny in range(2):
                v1[2 * c + ny, 0:12, :] = vel[c, ny, 52:64, :]
                v1[2 * c + ny, 12:16, :] = below[36 + 2 * c + ny, 0:4, :]
        for p in range(10):
            pq[p, 8:12, :] = below[42 + p // 2, ds(4 * (p % 2), 4), :]
            pq[p, 12:16, :] = jnp.zeros((4, 128), F32)

    own_at = pl.ds(pl.multiple_of(56 * step, 8), 8)
    for k in range(18):
        src = mom.at[k] if k < 6 else sca.at[k - 6]
        for ny in range(2):
            q[2 * k + ny, own8, :] = src[ny]
            q1[2 * k + ny, own8, :] = edge[0, 2 * k + ny]
    for c in range(2):
        for ny in range(2):
            vq[2 * c + ny, own8, :] = vel[c, ny, own_at, :]
    for p in range(10):
        pq[p, own8, :] = packs[p]
    for p in range(9):
        pq1[p, own8, :] = pack_edge[0, p]
    png[far8, :] = jnp.zeros((8, 128), F32)
    png[own8, :] = packs[10]
    for r in (0, 8):
        pu[ds(r, 8), :], pw[ds(r, 8), :] = pack_velocity(pq[9, ds(r, 8), :])

    def one(p, _):
        kap = pack_kappa(kappa, p)
        for r in (0, 8):
            f[4, ds(r, 8), :] = pu[ds(r, 8), :] * pq[p, ds(r, 8), :]
        v = pq[p, mid, :]
        g = pw[mid, :] * v
        cor = correction(v, g, kap, dt)
        pq1[p, far8, :] = v + transport(
            v, g, lambda m: pq[p, ds(4 + m, 8), :], lambda m: f[4, ds(4 + m, 8), :], kap, dt
        )
        for i, field, ny, slot in planes(p):
            for r in (0, 8):
                f[slot, ds(r, 8), :] = vq[ny, ds(r, 8), :] * q[i, ds(r, 8), :]
            v = q[i, mid, :]
            g = vq[2 + ny, mid, :] * v
            rate = transport(
                v, g, lambda m: q[i, ds(4 + m, 8), :], lambda m: f[slot, ds(4 + m, 8), :],
                kappa[field], dt,
            )
            q1[i, far8, :] = v + rate + unpack(cor, slot)
        return _

    lax.fori_loop(0, 9, one, 0)
    src = pack_sources(lambda k: pq[k, mid, :], png[mid, :], dt)
    for k in range(7):
        pq1[k, far8, :] += src[k]
    for ny in range(2):
        src = sources(lambda k: q[2 * k + ny, mid, :], ng[ny, far8, :], ng[2 + ny, far8, :], dt)
        for k in range(7):
            q1[2 * k + ny, far8, :] += src[k]

    scale = 0.5 * dt

    def two(p, _):
        v = pq1[p, mid, :]
        cor = correction(v, pw[own8, :] * v, pack_kappa(kappa, p), scale)
        for i, field, ny, slot in planes(p):
            for r in (0, 8):
                f[slot, ds(r, 8), :] = v1[ny, ds(r, 8), :] * q1[i, ds(r, 8), :]
            v = q1[i, mid, :]
            g = v1[2 + ny, mid, :] * v
            rate = transport(
                v, g, lambda m: q1[i, ds(4 + m, 8), :], lambda m: f[slot, ds(4 + m, 8), :],
                kappa[field], scale,
            )
            half[i] = 0.5 * (q[i, own8, :] + v) + rate + unpack(cor, slot)
        return _

    lax.fori_loop(0, 9, two, 0)
    for ny in range(2):
        src = sources(lambda k: q1[2 * k + ny, mid, :], ng[ny, mid, :], ng[2 + ny, mid, :], scale)
        for k in range(7):
            half[2 * k + ny] += src[k]
    for k in range(18):
        dst = out_mom.at[k] if k < 6 else out_sca.at[k - 6]
        for ny in range(2):
            dst[ny] = half[2 * k + ny]


def call(kernel, outs, cost, **kw):
    return pl.pallas_call(
        kernel,
        out_shape=[jax.ShapeDtypeStruct(o, F32) for o in outs],
        cost_estimate=pl.CostEstimate(flops=cost, bytes_accessed=cost // 4, transcendentals=0),
        compiler_params=pltpu.CompilerParams(vmem_limit_bytes=24 * 2**20),
        **kw,
    )


def send(value, axis, by):
    peers = lax.axis_size(axis)
    return lax.ppermute(value, axis, [(i, (i + by) % peers) for i in range(peers)])


def body(moments, scalars, velocity, diffusivity, nucleation, growth):
    fields = (moments, scalars, velocity, nucleation, growth)
    vmem = pl.BlockSpec(memory_space=pltpu.VMEM)
    smem = pl.BlockSpec(memory_space=pltpu.SMEM)
    hbm = pl.BlockSpec(memory_space=pl.ANY)
    tiles = lambda *lead: pltpu.VMEM(lead + (128,), F32)

    zl, zr = call(pack_z, [(3, 64, 128)] * 2, 10**6)(*fields)
    from_right = send(zl, "gz", -1)
    from_left = send(zr, "gz", 1)
    up, down = call(pack_x, [(47, 8, 128)] * 2, 10**6)(*fields)
    packs, up, down = call(
        edge_packs,
        [(11, 64, 128), (47, 8, 128), (47, 8, 128)],
        10**6,
        in_specs=[vmem] * 4 + [hbm] * 2,
        out_specs=[vmem, hbm, hbm],
        input_output_aliases={4: 1, 5: 2},
        scratch_shapes=[tiles(2, 5, 8), pltpu.SemaphoreType.DMA((2,))],
    )(zl, zr, from_left, from_right, up, down)
    above = send(up, "gx", 1)
    below = send(down, "gx", -1)
    out_mom, out_sca, edge, pack_edge = call(
        interior,
        [moments.shape, scalars.shape, (2, 36, 8, 128), (2, 9, 8, 128)],
        10**8,
        in_specs=[smem] + [vmem] * 6,
        scratch_shapes=[
            tiles(36, 64), tiles(36, 56), tiles(64), tiles(64), tiles(64), tiles(9, 56), tiles(9, 64), tiles(36, 64),
        ],
    )(diffusivity, *fields, packs)

    def row_block(*lead):
        return pl.BlockSpec(lead + (8, 128), lambda i: (0,) * len(lead) + (7 * i, 0))

    def side_block(*lead):
        return pl.BlockSpec((1,) + lead + (8, 128), lambda i: (i,) + (0,) * (len(lead) + 2))

    def whole(*shape):
        return pl.BlockSpec(shape, lambda i: (0,) * len(shape))

    return tuple(
        call(
            edges,
            [moments.shape, scalars.shape],
            10**8,
            grid=(2,),
            in_specs=[
                smem, row_block(6, 2), row_block(12, 2), whole(2, 2, 64, 128), row_block(2), row_block(2), row_block(11),
                side_block(36), side_block(9), whole(47, 8, 128), whole(47, 8, 128), hbm, hbm,
            ],
            out_specs=[row_block(6, 2), row_block(12, 2)],
            input_output_aliases={11: 0, 12: 1},
            scratch_shapes=[
                tiles(36, 16), tiles(36, 16), tiles(5, 16), tiles(4, 16), tiles(4, 16), tiles(4, 16), tiles(10, 16),
                tiles(16), tiles(16), tiles(16), tiles(9, 16), tiles(8), tiles(36, 8),
            ],
        )(diffusivity, *fields, packs, edge, pack_edge, above, below, out_mom, out_sca)
    )


def solution(mesh):
    return jax.shard_map(
        body,
        mesh=mesh,
        in_specs=(
            P(None, None, "gx", "gz"),
            P(None, None, "gx", "gz"),
            P(None, None, "gx", "gz"),
            P(),
            P(None, "gx", "gz"),
            P(None, "gx", "gz"),
        ),
        out_specs=(P(None, None, "gx", "gz"), P(None, None, "gx", "gz")),
        check_vma=False,
    )
```

time: 102 us -> 46.9 us (0.46)
  the two profiles are of different devices: /device:TPU:25 before, /device:TPU:4 now
where the time goes in v1:
time: 46.9 us; the launch traced here: 46.6 us
  Pallas kernels  23.6 us (50%)
  starting transfers between devices  10 us (21%)
  waiting for transfers between devices  7.63 us (16%)
  local copies, waits for them, and re-layouts  4.72 us (10%)
  between operations  0.67 us (1%)
    pallas_call x1, Pallas kernels, body(): call(interior, [moments.shape, scalars.shape, (2, 36, 8, 128), (2, 9, 8,...  12.1 us
    ppermute x4, starting transfers between devices, send(): lax.ppermute(value, axis, [(i, (i + by) % peers) for i in range(peers)])  10 us
    pallas_call x1, Pallas kernels, body(): call(edges, [moments.shape, scalars.shape], 10 ** 8, grid=(2,), in_specs=...  9.82 us
    ppermute x4, waiting for transfers between devices, send(): lax.ppermute(value, axis, [(i, (i + by) % peers) for i in range(peers)])  7.63 us
    unnamed x16, local copies, waits for them, and re-layouts  4.72 us
    pallas_call x1, Pallas kernels, body(): zl, zr = call(pack_z, [(3, 64, 128)] * 2, 10 ** 6)(*fields)  1.25 us
  transfers between devices with their start and end apart: 4, of which 2 were waited for; matrix products, arithmetic and copies ran while one was open for 0% of the time, Pallas kernels for 26%

profile of v1, /device:TPU:4, one launch (start us, length us, event | category | flops | bytes accessed | tf_op | source)
XLA Modules:
  0.0 46.6 jit_solution(9626738248443643424)
XLA Ops:
  0.6 0.0 copy-start
  0.6 1.1 %copy-done = f32[12,2,64,128]{3,2,1,0:T(8,128)S(1)} copy-done((f32[12,2,64,128]{3,2,1,0:T(8,128)S(1)}, f32[12,2,64,128]{3,2,1,0:T(8,128)}, u32[]{:S(2)}) %copy-start) | copy-done | bytes 786456
  1.8 0.0 copy-start.2
  1.8 1.0 %copy-done.2 = f32[6,2,64,128]{3,2,1,0:T(8,128)S(1)} copy-done((f32[6,2,64,128]{3,2,1,0:T(8,128)S(1)}, f32[6,2,64,128]{3,2,1,0:T(8,128)}, u32[]{:S(2)}) %copy-start.2) | copy-done | bytes 393240
  2.8 0.0 copy-start.4
  2.8 0.9 %copy-done.4 = f32[2,2,64,128]{3,2,1,0:T(8,128)S(1)} copy-done((f32[2,2,64,128]{3,2,1,0:T(8,128)S(1)}, f32[2,2,64,128]{3,2,1,0:T(8,128)}, u32[]{:S(2)}) %copy-start.4) | copy-done | bytes 131096
  3.7 0.0 copy-start.5
  3.7 0.8 %copy-done.5 = f32[2,64,128]{2,1,0:T(8,128)S(1)} copy-done((f32[2,64,128]{2,1,0:T(8,128)S(1)}, f32[2,64,128]{2,1,0:T(8,128)}, u32[]{:S(2)}) %copy-start.5) | copy-done | bytes 65560
  4.5 0.8 %copy-done.6 = f32[2,64,128]{2,1,0:T(8,128)S(1)} copy-done((f32[2,64,128]{2,1,0:T(8,128)S(1)}, f32[2,64,128]{2,1,0:T(8,128)}, u32[]{:S(2)}) %copy-start.6) | copy-done | bytes 65560
  5.3 1.3 %shard_map.77 = (f32[3,64,128]{2,1,0:T(8,128)S(1)}, f32[3,64,128]{2,1,0:T(8,128)S(1)}) custom-call(f32[6,2,64,128]{3,2,1,0:T(8,128)S(1)} %copy-done.2, f32[12,2,64,128]{3,2,1,0:T(8,128)S(1)} %copy-done, f32[2,2,64,128]{3,2,1,0:T(8,128)S(1)} %copy-done.4, f32[2,64,128]{2,1,0:T(8,128)S(1)} %copy-done.5, f32[2,64,128]{2,1,0:T(8,128)S(1)} %copy-done.6), custom_call_target="tpu_custom_call" | custom-call | flops 1000000 | bytes 250000 | tf_op jit(solution)/shard_map/pallas_call | solution.py:452
  6.6 2.5 %collective-permute-start.1 = (f32[3,64,128]{2,1,0:T(8,128)S(1)}, f32[3,64,128]{2,1,0:T(8,128)S(1)}, u32[]{:S(2)}, u32[]{:S(2)}) collective-permute-start(f32[3,64,128]{2,1,0:T(8,128)S(1)} %get-tuple-element.13.zl), channel_id=1, source_target_pairs={{0,15},{1,0},{2,1},{3,2},{4,3},{5,4},{6,5},{7,6},{8,7},{9,8},{10,9... | collective-permute-start | bytes 294920 | tf_op jit(solution)/shard_map/ppermute | solution.py:442
  9.1 0.0 collective-permute-start
  9.1 2.2 %collective-permute-done.1.from_right = f32[3,64,128]{2,1,0:T(8,128)S(1)} collective-permute-done((f32[3,64,128]{2,1,0:T(8,128)S(1)}, f32[3,64,128]{2,1,0:T(8,128)S(1)}, u32[]{:S(2)}, u32[]{:S(2)}) %collective-permute-start.1) | collective-permute-done | bytes 98336 | tf_op jit(solution)/shard_map/ppermute | solution.py:442
  11.3 5.4 %collective-permute-done.from_left = f32[3,64,128]{2,1,0:T(8,128)S(1)} collective-permute-done((f32[3,64,128]{2,1,0:T(8,128)S(1)}, f32[3,64,128]{2,1,0:T(8,128)S(1)}, u32[]{:S(2)}, u32[]{:S(2)}) %collective-permute-start) | collective-permute-done | bytes 98336 | tf_op jit(solution)/shard_map/ppermute | solution.py:442
  16.7 0.4 shard_map.79
  17.2 2.2 %collective-permute-start.2 = (f32[47,8,128]{2,1,0:T(8,128)S(1)}, f32[47,8,128]{2,1,0:T(8,128)S(1)}, u32[]{:S(2)}, u32[]{:S(2)}) collective-permute-start(f32[47,8,128]{2,1,0:T(8,128)S(1)} %get-tuple-element.20), channel_id=1, source_target_pairs={{0,16},{16,32},{32,48},{48,64},{64,80},{80,96},{96,112},{112,128},... | collective-permute-start | bytes 577544 | tf_op jit(solution)/shard_map/ppermute | solution.py:442
  19.3 5.4 %collective-permute-start.3 = (f32[47,8,128]{2,1,0:T(8,128)S(1)}, f32[47,8,128]{2,1,0:T(8,128)S(1)}, u32[]{:S(2)}, u32[]{:S(2)}) collective-permute-start(f32[47,8,128]{2,1,0:T(8,128)S(1)} %get-tuple-element.21), channel_id=1, source_target_pairs={{0,240},{16,0},{32,16},{48,32},{64,48},{80,64},{96,80},{112,96},{1... | collective-permute-start | bytes 577544 | tf_op jit(solution)/shard_map/ppermute | solution.py:442
  24.7 0.0 copy-done.1
  24.7 0.0 copy-done.3
  24.7 0.0 copy-done.7
  24.7 12.1 %shard_map.80 = (f32[6,2,64,128]{3,2,1,0:T(8,128)}, f32[12,2,64,128]{3,2,1,0:T(8,128)}, f32[2,36,8,128]{3,2,1,0:T(8,128)S(1)}, f32[2,9,8,128]{3,2,1,0:T(8,128)S(1)}) custom-call(f32[18]{0:T(128)S(1)} %copy-done.7, f32[6,2,64,128]{3,2,1,0:T(8,128)S(1)} %copy-done.3, f32[12,2,64,128]{3,2,1,0:T(8,128)S(1)} %copy-done.1, f32[2,2,64,128]{3,2,1,0:T(8,128)S(1)} %copy-done.4, ...), custom_call_target="tpu_custom_call" | custom-call | flops 100000000 | bytes 25000000 | tf_op jit(solution)/shard_map/pallas_call | solution.py:467
  36.8 0.0 collective-permute-done.2.above
  36.8 0.0 collective-permute-done.3.below
  36.8 9.8 %shard_map.81 = (f32[6,2,64,128]{3,2,1,0:T(8,128)}, f32[12,2,64,128]{3,2,1,0:T(8,128)}) custom-call(f32[18]{0:T(128)S(1)} %copy-done.7, f32[6,2,64,128]{3,2,1,0:T(8,128)S(1)} %copy-done.3, f32[12,2,64,128]{3,2,1,0:T(8,128)S(1)} %copy-done.1, f32[2,2,64,128]{3,2,1,0:T(8,128)S(1)} %copy-done.4, ...), custom_call_target="tpu_custom_call", output_to_operand_aliasing={{0}: (11, {}), {1}: (12, {})} | custom-call | flops 100000000 | bytes 25000000 | tf_op jit(solution)/shard_map/pallas_call | solution.py:487
  (5 shorter events, 0.0 us)
Async XLA Ops:
  0.6 1.1 %copy-start = (f32[12,2,64,128]{3,2,1,0:T(8,128)S(1)}, f32[12,2,64,128]{3,2,1,0:T(8,128)}, u32[]{:S(2)}) copy-start(f32[12,2,64,128]{3,2,1,0:T(8,128)} %sca.7) | copy-start | bytes 2359300
  1.8 1.0 %copy-start.2 = (f32[6,2,64,128]{3,2,1,0:T(8,128)S(1)}, f32[6,2,64,128]{3,2,1,0:T(8,128)}, u32[]{:S(2)}) copy-start(f32[6,2,64,128]{3,2,1,0:T(8,128)} %mom.7) | copy-start | bytes 1179652
  2.8 0.9 %copy-start.4 = (f32[2,2,64,128]{3,2,1,0:T(8,128)S(1)}, f32[2,2,64,128]{3,2,1,0:T(8,128)}, u32[]{:S(2)}) copy-start(f32[2,2,64,128]{3,2,1,0:T(8,128)} %vel.7) | copy-start | bytes 393220
  3.7 0.8 %copy-start.5 = (f32[2,64,128]{2,1,0:T(8,128)S(1)}, f32[2,64,128]{2,1,0:T(8,128)}, u32[]{:S(2)}) copy-start(f32[2,64,128]{2,1,0:T(8,128)} %nuc.7) | copy-start | bytes 196612
  4.5 0.8 %copy-start.6 = (f32[2,64,128]{2,1,0:T(8,128)S(1)}, f32[2,64,128]{2,1,0:T(8,128)}, u32[]{:S(2)}) copy-start(f32[2,64,128]{2,1,0:T(8,128)} %gro.7) | copy-start | bytes 196612
  6.6 4.7 %collective-permute-start.1 = (f32[3,64,128]{2,1,0:T(8,128)S(1)}, f32[3,64,128]{2,1,0:T(8,128)S(1)}, u32[]{:S(2)}, u32[]{:S(2)}) collective-permute-start(f32[3,64,128]{2,1,0:T(8,128)S(1)} %get-tuple-element.13.zl), channel_id=1, source_target_pairs={{0,15},{1,0},{2,1},{3,2},{4,3},{5,4},{6,5},{7,6},{8,7},{9,8},{10,9... | collective-permute-start | bytes 294920 | tf_op jit(solution)/shard_map/ppermute | solution.py:442
  9.1 15.7 %copy-start.1 = (f32[12,2,64,128]{3,2,1,0:T(8,128)S(1)}, f32[12,2,64,128]{3,2,1,0:T(8,128)}, u32[]{:S(2)}) copy-start(f32[12,2,64,128]{3,2,1,0:T(8,128)} %sca.7) | copy-start | bytes 2359300
  9.1 7.7 %collective-permute-start = (f32[3,64,128]{2,1,0:T(8,128)S(1)}, f32[3,64,128]{2,1,0:T(8,128)S(1)}, u32[]{:S(2)}, u32[]{:S(2)}) collective-permute-start(f32[3,64,128]{2,1,0:T(8,128)S(1)} %get-tuple-element.14.zr), channel_id=1, source_target_pairs={{0,1},{1,2},{2,3},{3,4},{4,5},{5,6},{6,7},{7,8},{8,9},{9,10},{10,1... | collective-permute-start | bytes 294920 | tf_op jit(solution)/shard_map/ppermute | solution.py:442
  16.7 8.0 %copy-start.3 = (f32[6,2,64,128]{3,2,1,0:T(8,128)S(1)}, f32[6,2,64,128]{3,2,1,0:T(8,128)}, u32[]{:S(2)}) copy-start(f32[6,2,64,128]{3,2,1,0:T(8,128)} %mom.7) | copy-start | bytes 1179652
  17.2 19.6 %collective-permute-start.2 = (f32[47,8,128]{2,1,0:T(8,128)S(1)}, f32[47,8,128]{2,1,0:T(8,128)S(1)}, u32[]{:S(2)}, u32[]{:S(2)}) collective-permute-start(f32[47,8,128]{2,1,0:T(8,128)S(1)} %get-tuple-element.20), channel_id=1, source_target_pairs={{0,16},{16,32},{32,48},{48,64},{64,80},{80,96},{96,112},{112,128},... | collective-permute-start | bytes 577544 | tf_op jit(solution)/shard_map/ppermute | solution.py:442
  19.3 5.4 %copy-start.7 = (f32[18]{0:T(128)S(1)}, f32[18]{0:T(128)}, u32[]{:S(2)}) copy-start(f32[18]{0:T(128)} %kappa.3) | copy-start | bytes 220
  19.3 17.5 %collective-permute-start.3 = (f32[47,8,128]{2,1,0:T(8,128)S(1)}, f32[47,8,128]{2,1,0:T(8,128)S(1)}, u32[]{:S(2)}, u32[]{:S(2)}) collective-permute-start(f32[47,8,128]{2,1,0:T(8,128)S(1)} %get-tuple-element.21), channel_id=1, source_target_pairs={{0,240},{16,0},{32,16},{48,32},{64,48},{80,64},{96,80},{112,96},{1... | collective-permute-start | bytes 577544 | tf_op jit(solution)/shard_map/ppermute | solution.py:442

commit v2 on v0

v2 whole, which is shorter than its diff:
```python
import numpy as np

import jax
import jax.numpy as jnp
from jax import lax
from jax.experimental import pallas as pl
from jax.experimental.pallas import tpu as pltpu
from jax.sharding import PartitionSpec as P

first_whole, first_part = (672.0, -168.0, 32.0, -3.0), 840.0
second_whole, second_part = (8064.0, -1008.0, 128.0, -9.0), 5040.0
centre_x, centre_z = -28672.0, -28.0
time_step = 0.25

F32, BF16 = jnp.float32, jnp.bfloat16


def band(targets, sources, centre):
    gap = np.asarray(sources)[None, :] - np.asarray(targets)[:, None]
    second = np.where(gap == 0, centre, 0.0)
    first = np.zeros(gap.shape)
    for m in range(1, 5):
        second = second + second_whole[m - 1] * (abs(gap) == m)
        first = first - first_whole[m - 1] * ((gap == m) * 1.0 - (gap == -m))
    return second, first


def matrices():
    both = lambda pair, axis: np.concatenate([pair[0], pair[0], pair[1], pair[1]], axis=axis).astype(BF16)
    rows, cols = np.arange(64), np.arange(128)
    a_rows = both(band(rows, rows, centre_x), 1)
    place, away = np.arange(32), 1000
    part = np.concatenate([place[:16], away + place[16:]])
    a_edge = both(band(np.concatenate([part[4:12], part[20:28]]), part, centre_x), 1)
    z_main = both(tuple(m.T for m in band(cols, cols, centre_z)), 0)
    slot_col = np.concatenate([np.arange(-8, 8), np.arange(120, 136)])
    beyond = (slot_col < 0) | (slot_col >= 128)
    to_planes = []
    for matrix in band(cols, slot_col, 0.0):
        wide = np.zeros((128, 512))
        for s in range(4):
            wide[32 * s : 32 * s + 32, 128 * s : 128 * s + 128] = (matrix * beyond[None, :]).T
        to_planes.append(wide)
    lane = np.arange(128)
    in_slot = [m.T * (lane[:, None] // 16 == lane[None, :] // 16) for m in band(lane, lane, centre_z)]
    z_pack = both(tuple(np.concatenate([w, o], axis=1) for w, o in zip(to_planes, in_slot)), 0)
    return a_rows, a_edge, z_main, z_pack


def lanes(shape=(8, 128)):
    return lax.broadcasted_iota(jnp.int32, shape, len(shape) - 1)


def roll(x, by):
    by = by % 128
    return x if by == 0 else pltpu.roll(x, by, 1)


def split(x):
    high = x.astype(BF16)
    return high, (x - high.astype(F32)).astype(BF16)


def dot(a, b):
    return jnp.dot(a, b, preferred_element_type=F32)


def plane_of(p, s):
    c, ny = s // 2, s % 2
    return 2 * (p + 9 * c) + ny if p < 9 else 4 * p + s


def pack_z(mom, sca, vel, nuc, gro, zl, zr, fields, sems):
    parts = [
        [(mom, 0, 0, 8), (sca, 6, 18, 8)],
        [(mom, 8, 8, 4), (sca, 0, 12, 4), (sca, 14, 26, 8)],
        [(sca, 4, 16, 2), (sca, 22, 34, 2), (vel, 0, 36, 4), (nuc, 0, 40, 2), (gro, 0, 42, 2)],
    ]
    copies, n = [], 0
    for part in parts:
        copies.append([])
        for src, at, to, size in part:
            copies[-1].append(
                pltpu.make_async_copy(src.at[pl.ds(at, size)], fields.at[pl.ds(to, size)], sems.at[n])
            )
            copies[-1][-1].start()
            n += 1
    pair, odd = lanes() // 16, (lanes() // 8) % 2 == 1
    for t in range(3):
        for copy in copies[t]:
            copy.wait()
        for r in range(0, 64, 8):
            tile = [None, None]
            for j in range(4 if t < 2 else 3):
                for s in range(4):
                    c = 2 * s + j // 2
                    one = roll(fields[plane_of(4 * t + j, s), r : r + 8, :], 16 * c + 8)
                    half = tile[j % 2]
                    tile[j % 2] = one if half is None else jnp.where(pair == c, one, half)
            zr[t, r : r + 8, :] = jnp.where(odd, roll(tile[1], 8), tile[0])
            zl[t, r : r + 8, :] = jnp.where(odd, tile[1], roll(tile[0], -8))


def prepare(mom, sca, vel, nuc, gro, fields, own, up, down):
    for src, to in ((mom, 0), (sca, 12), (vel, 36), (nuc, 40), (gro, 42)):
        for k in range(src.shape[0]):
            fields[to + k] = src[k]
    for msg, lo, part in ((down, 0, 0), (up, 56, 60)):
        for i in range(38):
            msg[i] = fields[i, lo : lo + 8, :]
        for k in range(3):
            for side in range(2):
                i = 38 + side if k == 0 else 39 + k + 2 * side
                msg[38 + k, 4 * side : 4 * side + 4, :] = fields[i, part : part + 4, :]
    sub = lanes() // 8
    for p in range(11):
        for r in range(0, 64, 8):
            e = jnp.zeros((8, 128), F32)
            for s in range(4):
                tile = fields[plane_of(p, s), r : r + 8, :]
                e = jnp.where(sub == 4 * s + 1, roll(tile, 32 * s + 8), e)
                e = jnp.where(sub == 4 * s + 2, roll(tile, 32 * s + 24), e)
            own[p, r : r + 8, :] = e


def corners(from_left, from_right, up_in, down_in, up, down, buf, sems):
    del up_in, down_in
    first = lanes((4, 128)) % 8 < 4
    for k, part in enumerate((0, 60)):
        for t in range(3):
            at = slice(4 * (t % 2), 4 * (t % 2) + 4)
            rows = slice(part, part + 4)
            buf[k, t // 2, at, :] = jnp.where(first, from_right[t, rows, :], from_left[t, rows, :])
        buf[k, 1, 4:8, :] = jnp.zeros((4, 128), F32)
    copies = [
        pltpu.make_async_copy(buf.at[k], msg.at[pl.ds(41, 2)], sems.at[k])
        for k, msg in enumerate((down, up))
    ]
    for copy in copies:
        copy.start()
    for copy in copies:
        copy.wait()


def fill_packs(own, from_left, from_right, packs):
    sub = (lanes((64, 128)) // 8) % 4
    for p in range(11):
        t, j = p // 4, p % 4
        e = jnp.where(sub == 0, roll(from_left[t], -8 * j), own[p])
        packs[p] = jnp.where(sub == 3, roll(from_right[t], 24 - 8 * j), e)


def sources(get, nucl, grow, scale):
    y = get(6)
    birth = nucl * y * y
    moms = [get(k) for k in range(6)]
    half = (0.5 * scale) * birth
    sink = (0.3 * scale) * moms[0]
    out = []
    for k in range(6):
        s = half - sink * moms[k]
        if k:
            s = s + ((scale * k / 3.0) * grow) * moms[k - 1]
        out.append(s)
    return out + [(-0.2 * scale) * birth]


def pack_sources(get, ng, scale):
    low = lanes(ng.shape) < 64
    nucl = jnp.where(low, ng, 0.0)
    grow = jnp.where(low, roll(ng, 64), 0.0)
    y = get(6)
    birth = nucl * y * y
    moms = [get(k) for k in range(6)]
    half = (0.5 * scale) * birth
    sink = jnp.where(low, (0.3 * scale) * moms[0], 0.0)
    out = []
    for k in range(6):
        s = half - sink * moms[k]
        if k:
            s = s + ((scale * k / 3.0) * grow) * moms[k - 1]
        out.append(s)
    return out + [(-0.2 * scale) * birth]


def pack_velocity(tile):
    low = lanes(tile.shape) < 64
    other = roll(tile, 64)
    return jnp.where(low, tile, other), jnp.where(low, other, tile)


def pack_kappa(kappa, p):
    return jnp.where(lanes((1, 128)) < 64, kappa[p], kappa[p + 9])


def planes(p):
    for slot in range(4):
        field, ny = p + 9 * (slot // 2), slot % 2
        yield 2 * field + ny, field, ny, slot


def across(kq, g):
    return jnp.concatenate([*split(kq), *split(g)], axis=1)


def down_rows(kq, f):
    return jnp.concatenate([*split(kq), *split(f)], axis=0)


GROUP = 3


def interior(
    kappa, fields, own, from_left, from_right, a_rows, z_main, z_pack, packs, q1, pq1, half,
    us, ws, pus, pws, el, eo,
):
    def velocities(scale):
        for ny in range(2):
            us[ny] = fields[36 + ny] * (scale / first_part)
            ws[ny] = fields[38 + ny] * (scale / first_part)
        pu, pw = pack_velocity(packs[9])
        pus[...] = pu * (scale / first_part)
        pws[...] = pw * (scale / first_part)

    fill_packs(own, from_left, from_right, packs)
    dt = time_step
    velocities(dt)
    for p in range(9):
        e = packs[p]
        kq = (pack_kappa(kappa, p) * (dt / second_part)) * e
        el[64 * p : 64 * p + 64, :] = across(kq, pws[...] * e)
    eo[...] = dot(el[...], z_pack[...])
    for p in range(9):
        e = packs[p]
        kq = (pack_kappa(kappa, p) * (dt / second_part)) * e
        x = dot(a_rows[...], down_rows(kq, pus[...] * e))
        pq1[p] = e + x + eo[64 * p : 64 * p + 64, 512:640]
    src = pack_sources(lambda k: packs[k], packs[10], dt)
    for k in range(7):
        pq1[k] += src[k]

    def one(p):
        lhs, rhs = [], []
        for i, field, ny, slot in planes(p):
            v = fields[i]
            kq = (kappa[field] * (dt / second_part)) * v
            lhs.append(across(kq, ws[ny] * v))
            rhs.append(down_rows(kq, us[ny] * v))
        z = dot(jnp.concatenate(lhs, axis=0), z_main[...])
        x = [dot(a_rows[...], jnp.concatenate(rhs[c : c + 2], axis=1)) for c in (0, 2)]
        for i, field, ny, slot in planes(p):
            q1[i] = (
                fields[i]
                + z[64 * slot : 64 * slot + 64]
                + x[slot // 2][:, 128 * ny : 128 * ny + 128]
                + eo[pl.ds(64 * p, 64), 128 * slot : 128 * slot + 128]
            )

    def groups(fn):
        def step(i, _):
            for k in range(GROUP):
                fn(i * GROUP + k)
            return _

        if GROUP == 9:
            for p in range(9):
                fn(p)
        else:
            lax.fori_loop(0, 9 // GROUP, step, 0)

    groups(one)
    for ny in range(2):
        src = sources(lambda k: fields[2 * k + ny], fields[40 + ny], fields[42 + ny], dt)
        for k in range(7):
            q1[2 * k + ny] += src[k]

    scale = 0.5 * dt
    velocities(scale)
    for p in range(9):
        e = pq1[p, 8:56, :]
        kq = (pack_kappa(kappa, p) * (scale / second_part)) * e
        el[48 * p : 48 * p + 48, :] = across(kq, pws[8:56, :] * e)
    eo[0:432, 0:512] = dot(el[0:432, :], z_pack[:, 0:512])

    def two(p):
        lhs, rhs = [], []
        for i, field, ny, slot in planes(p):
            v = q1[i]
            kq = (kappa[field] * (scale / second_part)) * v
            mid = v[8:56]
            lhs.append(across(kq[8:56], ws[ny, 8:56, :] * mid))
            rhs.append(down_rows(kq, us[ny] * v))
        z = dot(jnp.concatenate(lhs, axis=0), z_main[...])
        x = [dot(a_rows[8:56, :], jnp.concatenate(rhs[c : c + 2], axis=1)) for c in (0, 2)]
        for i, field, ny, slot in planes(p):
            half[i, 8:56, :] = (
                0.5 * (fields[i, 8:56, :] + q1[i, 8:56, :])
                + z[48 * slot : 48 * slot + 48]
                + x[slot // 2][:, 128 * ny : 128 * ny + 128]
                + eo[pl.ds(48 * p, 48), 128 * slot : 128 * slot + 128]
            )

    groups(two)
    for ny in range(2):
        src = sources(
            lambda k: q1[2 * k + ny, 8:56, :], fields[40 + ny, 8:56, :], fields[42 + ny, 8:56, :], scale
        )
        for k in range(7):
            half[2 * k + ny, 8:56, :] += src[k]


def edges(
    kappa, fields, packs, q1, pq1, half, above, below, a_edge, z_main, z_pack, out_mom, out_sca,
    q, s1, vq, v1, pq, ps1, pvq, el, eo, done, sems,
):
    outs = [(out_mom, 0, 12), (out_sca, 12, 24)]
    copies = [
        pltpu.make_async_copy(
            half.at[pl.ds(at, size), pl.ds(8, 48)], out.at[pl.ds(0, size), pl.ds(8, 48)], sems.at[n]
        )
        for n, (out, at, size) in enumerate(outs)
    ]
    for copy in copies:
        copy.start()
    dt = time_step
    top, low = slice(4, 12), slice(20, 28)
    mid = lambda ref, *at: jnp.concatenate([ref[*at, top, :], ref[*at, low, :]], axis=0)

    for i in range(36):
        q[i, 0:8, :] = above[i]
        q[i, 8:16, :] = fields[i, 0:8, :]
        q[i, 16:24, :] = fields[i, 56:64, :]
        q[i, 24:32, :] = below[i]
        s1[i, 8:16, :] = q1[i, 4:12, :]
        s1[i, 16:24, :] = q1[i, 52:60, :]
    one, two = dt / first_part, 0.5 * dt / first_part
    for i in range(4):
        k = 36 + i
        if i < 2:
            vq[i, 0:8, :] = above[k] * one
            vq[i, 24:32, :] = below[k] * one
        else:
            at = slice(4 * (i % 2), 4 * (i % 2) + 4)
            vq[i, 0:4, :] = vq[i, 28:32, :] = jnp.zeros((4, 128), F32)
            vq[i, 4:8, :] = above[38, at, :] * one
            vq[i, 24:28, :] = below[38, at, :] * one
        vq[i, 8:16, :] = fields[k, 0:8, :] * one
        vq[i, 16:24, :] = fields[k, 56:64, :] * one
        v1[i, 0:4, :] = vq[i, 4:8, :] * 0.5
        v1[i, 4:16, :] = fields[k, 0:12, :] * two
        v1[i, 16:28, :] = fields[k, 52:64, :] * two
        v1[i, 28:32, :] = vq[i, 24:28, :] * 0.5
    zeros = jnp.zeros((4, 128), F32)
    lane = lanes() % 32
    is_left, is_right = (lane >= 4) & (lane < 8), (lane >= 24) & (lane < 28)
    for p in range(10):
        t, j = p // 4, p % 4
        at = slice(4 * (t % 2), 4 * (t % 2) + 4)
        corner = jnp.concatenate([above[41 + t // 2, at, :], below[41 + t // 2, at, :]], axis=0)
        corner = jnp.where(
            is_left, roll(corner, -8 * j), jnp.where(is_right, roll(corner, 24 - 8 * j), 0.0)
        )
        pq[p, 0:4, :] = zeros
        pq[p, 4:8, :] = corner[0:4]
        pq[p, 8:16, :] = packs[p, 0:8, :]
        pq[p, 16:24, :] = packs[p, 56:64, :]
        pq[p, 24:28, :] = corner[4:8]
        pq[p, 28:32, :] = zeros
    for p in range(9):
        ps1[p, 8:16, :] = pq1[p, 4:12, :]
        ps1[p, 16:24, :] = pq1[p, 52:60, :]
    pu, pw = pack_velocity(pq[9])
    pvq[0], pvq[1] = pu * one, pw * one

    def stage(src, vel, scale, put):
        def one(p):
            lhs, rhs = [], []
            for i, field, ny, slot in planes(p):
                k = kappa[field] * (scale / second_part)
                v, m = src[i], mid(src, i)
                lhs.append(across(k * m, mid(vel, 2 + ny) * m))
                rhs.append(down_rows(k * v, vel[ny] * v))
            z = dot(jnp.concatenate(lhs, axis=0), z_main[...])
            x = dot(a_edge[...], jnp.concatenate(rhs, axis=1))
            for i, field, ny, slot in planes(p):
                put(
                    i,
                    z[16 * slot : 16 * slot + 16]
                    + x[:, 128 * slot : 128 * slot + 128]
                    + eo[16 * p : 16 * p + 16, 128 * slot : 128 * slot + 128],
                )

        for p in range(9):
            one(p)

    for p in range(9):
        e, m = pq[p], mid(pq, p)
        k = pack_kappa(kappa, p) * (dt / second_part)
        el[16 * p : 16 * p + 16, :] = across(k * m, mid(pvq, 1) * m)
    eo[...] = dot(el[...], z_pack[...])
    for p in range(9):
        e, m = pq[p], mid(pq, p)
        k = pack_kappa(kappa, p) * (dt / second_part)
        x = dot(a_edge[...], down_rows(k * e, pvq[0] * e))
        new = m + x + eo[16 * p : 16 * p + 16, 512:640]
        ps1[p, 0:8, :] = new[0:8]
        ps1[p, 24:32, :] = new[8:16]
    ng = jnp.concatenate([zeros, packs[10, 0:4, :], packs[10, 60:64, :], zeros], axis=0)
    src = pack_sources(lambda k: mid(pq, k), ng, dt)
    for k in range(7):
        ps1[k, 0:8, :] += src[k][0:8]
        ps1[k, 24:32, :] += src[k][8:16]

    def put_one(i, rate):
        new = mid(q, i) + rate
        s1[i, 0:8, :] = new[0:8]
        s1[i, 24:32, :] = new[8:16]

    stage(q, vq, dt, put_one)
    for ny in range(2):
        near, far = above[39 + ny], below[39 + ny]
        nucl = jnp.concatenate([near[0:4], fields[40 + ny, 0:4, :], fields[40 + ny, 60:64, :], far[0:4]], axis=0)
        grow = jnp.concatenate([near[4:8], fields[42 + ny, 0:4, :], fields[42 + ny, 60:64, :], far[4:8]], axis=0)
        src = sources(lambda k: mid(q, 2 * k + ny), nucl, grow, dt)
        for k in range(7):
            s1[2 * k + ny, 0:8, :] += src[k][0:8]
            s1[2 * k + ny, 24:32, :] += src[k][8:16]

    scale = 0.5 * dt
    for p in range(9):
        m = mid(ps1, p)
        k = pack_kappa(kappa, p) * (scale / second_part)
        el[16 * p : 16 * p + 16, :] = across(k * m, (0.5 * pvq[1, 8:24, :]) * m)
    eo[:, 0:512] = dot(el[...], z_pack[:, 0:512])

    def put_two(i, rate):
        own = jnp.concatenate([fields[i, 0:8, :], fields[i, 56:64, :]], axis=0)
        done[i] = 0.5 * (own + mid(s1, i)) + rate

    stage(s1, v1, scale, put_two)
    for ny in range(2):
        nucl = jnp.concatenate([fields[40 + ny, 0:8, :], fields[40 + ny, 56:64, :]], axis=0)
        grow = jnp.concatenate([fields[42 + ny, 0:8, :], fields[42 + ny, 56:64, :]], axis=0)
        src = sources(lambda k: mid(s1, 2 * k + ny), nucl, grow, scale)
        for k in range(7):
            done[2 * k + ny] += src[k]
    last = [
        pltpu.make_async_copy(
            done.at[pl.ds(at, size), pl.ds(8 * side, 8)],
            out.at[pl.ds(0, size), pl.ds(56 * side, 8)],
            sems.at[2 + 2 * n + side],
        )
        for n, (out, at, size) in enumerate(outs)
        for side in range(2)
    ]
    for copy in last:
        copy.start()
    for copy in copies + last:
        copy.wait()


def call(kernel, outs, cost, mib=24, **kw):
    return pl.pallas_call(
        kernel,
        out_shape=[jax.ShapeDtypeStruct(o, F32) for o in outs],
        cost_estimate=pl.CostEstimate(flops=cost, bytes_accessed=cost // 4, transcendentals=0),
        compiler_params=pltpu.CompilerParams(vmem_limit_bytes=mib * 2**20),
        **kw,
    )


def send(value, axis, by):
    peers = lax.axis_size(axis)
    return lax.ppermute(value, axis, [(i, (i + by) % peers) for i in range(peers)])


def body(moments, scalars, velocity, diffusivity, nucleation, growth):
    vmem = pl.BlockSpec(memory_space=pltpu.VMEM)
    smem = pl.BlockSpec(memory_space=pltpu.SMEM)
    hbm = pl.BlockSpec(memory_space=pltpu.HBM)
    tiles = lambda *lead: pltpu.VMEM(lead + (128,), F32)
    flat = [x.reshape(-1, 64, 128) for x in (moments, scalars, velocity, nucleation, growth)]
    a_rows, a_edge, z_main, z_pack = (jnp.asarray(m) for m in matrices())

    zl, zr = call(
        pack_z,
        [(3, 64, 128), (3, 64, 128)],
        10**6,
        56,
        in_specs=[hbm] * 5,
        out_specs=[vmem] * 2,
        scratch_shapes=[tiles(44, 64), pltpu.SemaphoreType.DMA((10,))],
    )(*flat)
    from_right = send(zl, "gz", -1)
    from_left = send(zr, "gz", 1)
    fields, own, up, down = call(
        prepare, [(44, 64, 128), (11, 64, 128), (43, 8, 128), (43, 8, 128)], 10**6
    )(*flat)
    up, down = call(
        corners,
        [(43, 8, 128), (43, 8, 128)],
        10**6,
        in_specs=[vmem] * 2 + [pl.BlockSpec(memory_space=pl.ANY)] * 2,
        out_specs=[pl.BlockSpec(memory_space=pl.ANY)] * 2,
        input_output_aliases={2: 0, 3: 1},
        scratch_shapes=[tiles(2, 2, 8), pltpu.SemaphoreType.DMA((2,))],
    )(from_left, from_right, up, down)
    above = send(up, "gx", 1)
    below = send(down, "gx", -1)
    packs, q1, pq1, half = call(
        interior,
        [(11, 64, 128), (36, 64, 128), (9, 64, 128), (36, 64, 128)],
        10**8,
        in_specs=[smem] + [vmem] * 7,
        scratch_shapes=[
            tiles(2, 64), tiles(2, 64), tiles(64), tiles(64), pltpu.VMEM((576, 512), BF16), pltpu.VMEM((576, 640), F32),
        ],
    )(diffusivity, fields, own, from_left, from_right, a_rows, z_main, z_pack)
    out_mom, out_sca = call(
        edges,
        [(12, 64, 128), (24, 64, 128)],
        10**8,
        in_specs=[smem] + [vmem] * 10,
        out_specs=[hbm] * 2,
        scratch_shapes=[
            tiles(36, 32), tiles(36, 32), tiles(4, 32), tiles(4, 32), tiles(10, 32), tiles(9, 32), tiles(2, 32),
            pltpu.VMEM((144, 512), BF16), pltpu.VMEM((144, 640), F32), tiles(36, 16), pltpu.SemaphoreType.DMA((6,)),
        ],
    )(diffusivity, fields, packs, q1, pq1, half, above, below, a_edge, z_main, z_pack)
    return out_mom.reshape(moments.shape), out_sca.reshape(scalars.shape)


def solution(mesh):
    return jax.shard_map(
        body,
        mesh=mesh,
        in_specs=(
            P(None, None, "gx", "gz"),
            P(None, None, "gx", "gz"),
            P(None, None, "gx", "gz"),
            P(),
            P(None, "gx", "gz"),
            P(None, "gx", "gz"),
        ),
        out_specs=(P(None, None, "gx", "gz"), P(None, None, "gx", "gz")),
        check_vma=False,
    )
```

time: 102 us -> 27.8 us (0.27)
  other arithmetic: 46.5 us -> 0 us
  local copies, waits for them, and re-layouts: 27.5 us -> 0.05 us
  Pallas kernels: 0 us -> 11 us
  starting transfers between devices: 16.9 us -> 8.78 us
  waiting for transfers between devices: 9.35 us -> 7.03 us
    add x2 -> x0, other arithmetic: 29.1 us -> none  [the longest x1 21.8 us: body(): result = 0.5 * start[:18] + 0.5 * (first_state + time_step * second_rate)]
    unnamed x45 -> x20, local copies, waits for them, and re-layouts: 12.7 us -> 0.05 us
    pallas_call x0 -> x5, Pallas kernels: none -> 11 us  [the longest x1 4.5 us: body(): call(interior, [(11, 64, 128), (36, 64, 128), (9, 64, 128), (36, 64, 128)...]
    ppermute x8 -> x0, local copies, waits for them, and re-layouts: 8.81 us -> none  [the longest x4 4.96 us: with_halo(): before = lax.ppermute(last, axis, up)]
    mul x12 -> x0, other arithmetic: 8.65 us -> none  [the longest x4 5.62 us: region_rhs(): flux_z = along_z[19:20] * along_z[:18]]
    ppermute x8 -> x4, starting transfers between devices: 16.9 us -> 8.78 us  [send(): lax.ppermute(value, axis, [(i, (i + by) % peers) for i in range(peers)])]
    concatenate x3 -> x0, other arithmetic: 6.73 us -> none  [the longest x2 5.2 us: with_halo(): value = jnp.concatenate([before, value, after], axis=dim)]
    slice x8 -> x0, local copies, waits for them, and re-layouts: 5.84 us -> none  [the longest x2 3.85 us: body(): return (result[:6], result[6:])]
  transfers between devices with their start and end apart: 8 -> 4, of which waited for: 2 -> 2; matrix products, arithmetic and copies ran while one was open for 23% -> 0% of each run, Pallas kernels for 0% -> 19%
where the time goes in v2:
time: 27.8 us; the launch traced here: 27.7 us
  Pallas kernels  11 us (40%)
  starting transfers between devices  8.78 us (32%)
  waiting for transfers between devices  7.03 us (25%)
  between operations  0.8 us (3%)
    ppermute x4, starting transfers between devices, send(): lax.ppermute(value, axis, [(i, (i + by) % peers) for i in range(peers)])  8.78 us
    ppermute x4, waiting for transfers between devices, send(): lax.ppermute(value, axis, [(i, (i + by) % peers) for i in range(peers)])  7.03 us
    pallas_call x1, Pallas kernels, body(): call(interior, [(11, 64, 128), (36, 64, 128), (9, 64, 128), (36, 64, 128)...  4.5 us
    pallas_call x1, Pallas kernels, body(): call(pack_z, [(3, 64, 128), (3, 64, 128)], 10 ** 6, 56, in_specs=[hbm] *...  2.86 us
    pallas_call x1, Pallas kernels, body(): call(edges, [(12, 64, 128), (24, 64, 128)], 10 ** 8, in_specs=[smem] + [v...  2.81 us
    pallas_call x1, Pallas kernels, body(): call(prepare, [(44, 64, 128), (11, 64, 128), (43, 8, 128), (43, 8, 128)],...  0.82 us
  transfers between devices with their start and end apart: 4, of which 2 were waited for; matrix products, arithmetic and copies ran while one was open for 0% of the time, Pallas kernels for 19%

profile of v2, /device:TPU:25, one launch (start us, length us, event | category | flops | bytes accessed | tf_op | source)
XLA Modules:
  0.0 27.7 jit_solution(18403854702180592191)
XLA Ops:
  0.6 0.0 copy-start.6
  0.6 0.0 copy-start.5
  0.7 0.0 copy-start.4
  0.7 0.0 copy-start
  0.7 0.0 copy-start.2
  0.7 2.9 %shard_map.114 = (f32[3,64,128]{2,1,0:T(8,128)}, f32[3,64,128]{2,1,0:T(8,128)}) custom-call(f32[12,64,128]{2,1,0:T(8,128)} %bitcast.7, f32[24,64,128]{2,1,0:T(8,128)} %bitcast.5, f32[4,64,128]{2,1,0:T(8,128)} %bitcast.9, f32[2,64,128]{2,1,0:T(8,128)} %nuc.3, f32[2,64,128]{2,1,0:T(8,128)} %gro.3), custom_call_target="tpu_custom_call" | custom-call | flops 1000000 | bytes 250000 | tf_op jit(solution)/shard_map/pallas_call | solution.py:485
  3.5 0.0 copy-start.1
  3.6 0.0 copy-start.3
  3.6 0.0 copy-start.7
  3.6 0.0 copy-start.9
  3.6 3.0 %collective-permute-start = (f32[3,64,128]{2,1,0:T(8,128)}, f32[3,64,128]{2,1,0:T(8,128)S(1)}, u32[]{:S(2)}, u32[]{:S(2)}) collective-permute-start(f32[3,64,128]{2,1,0:T(8,128)} %get-tuple-element.18), channel_id=1, source_target_pairs={{0,1},{1,2},{2,3},{3,4},{4,5},{5,6},{6,7},{7,8},{8,9},{9,10},{10,1... | collective-permute-start | bytes 294920 | tf_op jit(solution)/shard_map/ppermute | solution.py:474
  6.6 0.0 collective-permute-start.1
  6.6 0.0 copy-done.6
  6.7 0.8 %shard_map.113 = (f32[44,64,128]{2,1,0:T(8,128)S(1)}, f32[11,64,128]{2,1,0:T(8,128)S(1)}, f32[43,8,128]{2,1,0:T(8,128)S(1)}, f32[43,8,128]{2,1,0:T(8,128)S(1)}) custom-call(f32[12,64,128]{2,1,0:T(8,128)S(1)} %bitcast.8, f32[24,64,128]{2,1,0:T(8,128)S(1)} %bitcast.6, f32[4,64,128]{2,1,0:T(8,128)S(1)} %bitcast.10, f32[2,64,128]{2,1,0:T(8,128)S(1)} %copy-done.5, ...), custom_call_target="tpu_custom_call" | custom-call | flops 1000000 | bytes 250000 | tf_op jit(solution)/shard_map/pallas_call | solution.py:496
  7.5 1.1 %collective-permute-done.from_left = f32[3,64,128]{2,1,0:T(8,128)S(1)} collective-permute-done((f32[3,64,128]{2,1,0:T(8,128)}, f32[3,64,128]{2,1,0:T(8,128)S(1)}, u32[]{:S(2)}, u32[]{:S(2)}) %collective-permute-start) | collective-permute-done | bytes 98336 | tf_op jit(solution)/shard_map/ppermute | solution.py:474
  8.6 5.9 %collective-permute-done.1.from_right = f32[3,64,128]{2,1,0:T(8,128)S(1)} collective-permute-done((f32[3,64,128]{2,1,0:T(8,128)}, f32[3,64,128]{2,1,0:T(8,128)S(1)}, u32[]{:S(2)}, u32[]{:S(2)}) %collective-permute-start.1) | collective-permute-done | bytes 98336 | tf_op jit(solution)/shard_map/ppermute | solution.py:474
  14.6 0.4 %collective-permute-start.2 = (f32[43,8,128]{2,1,0:T(8,128)S(1)}, f32[43,8,128]{2,1,0:T(8,128)S(1)}, u32[]{:S(2)}, u32[]{:S(2)}) collective-permute-start(f32[43,8,128]{2,1,0:T(8,128)S(1)} %get-tuple-element.26), channel_id=1, source_target_pairs={{0,16},{16,32},{32,48},{48,64},{64,80},{80,96},{96,112},{112,128},... | collective-permute-start | bytes 528392 | tf_op jit(solution)/shard_map/ppermute | solution.py:474
  14.9 5.4 %collective-permute-start.3 = (f32[43,8,128]{2,1,0:T(8,128)S(1)}, f32[43,8,128]{2,1,0:T(8,128)S(1)}, u32[]{:S(2)}, u32[]{:S(2)}) collective-permute-start(f32[43,8,128]{2,1,0:T(8,128)S(1)} %get-tuple-element.27), channel_id=1, source_target_pairs={{0,240},{16,0},{32,16},{48,32},{64,48},{80,64},{96,80},{112,96},{1... | collective-permute-start | bytes 528392 | tf_op jit(solution)/shard_map/ppermute | solution.py:474
  20.3 0.0 copy-done.1
  20.3 0.0 copy-start.8
  20.3 4.5 %shard_map.115 = (f32[11,64,128]{2,1,0:T(8,128)S(1)}, f32[36,64,128]{2,1,0:T(8,128)S(1)}, f32[9,64,128]{2,1,0:T(8,128)S(1)}, f32[36,64,128]{2,1,0:T(8,128)S(1)}) custom-call(f32[18]{0:T(128)S(1)} %copy-done.9, f32[44,64,128]{2,1,0:T(8,128)S(1)} %get-tuple-element.16.fields, f32[11,64,128]{2,1,0:T(8,128)S(1)} %get-tuple-element.17.own, ...), custom_call_target="tpu_custom_call" | custom-call | flops 100000000 | bytes 25000000 | tf_op jit(solution)/shard_map/pallas_call | solution.py:510
  24.8 0.0 collective-permute-done.2.above
  24.9 0.0 collective-permute-done.3.below
  24.9 2.8 %shard_map.117 = (f32[12,64,128]{2,1,0:T(8,128)}, f32[24,64,128]{2,1,0:T(8,128)}) custom-call(f32[18]{0:T(128)S(1)} %copy-done.9, f32[44,64,128]{2,1,0:T(8,128)S(1)} %get-tuple-element.16.fields, f32[11,64,128]{2,1,0:T(8,128)S(1)} %get-tuple-element.20.packs, f32[36,64,128]{2,1,0:T(8,128)S(1)} %get-tuple-element.21.q1, ...), custom_call_target="tpu_custom_call" | custom-call | flops 100000000 | bytes 25000000 | tf_op jit(solution)/shard_map/pallas_call | solution.py:519
  (9 shorter events, 0.1 us)
Async XLA Ops:
  0.6 6.0 %copy-start.6 = (f32[2,64,128]{2,1,0:T(8,128)S(1)}, f32[2,64,128]{2,1,0:T(8,128)}, u32[]{:S(2)}) copy-start(f32[2,64,128]{2,1,0:T(8,128)} %gro.3) | copy-start | bytes 196612
  0.6 6.0 %copy-start.5 = (f32[2,64,128]{2,1,0:T(8,128)S(1)}, f32[2,64,128]{2,1,0:T(8,128)}, u32[]{:S(2)}) copy-start(f32[2,64,128]{2,1,0:T(8,128)} %nuc.3) | copy-start | bytes 196612
  0.7 6.0 %copy-start.4 = (f32[2,2,64,128]{3,2,1,0:T(8,128)S(1)}, f32[2,2,64,128]{3,2,1,0:T(8,128)}, u32[]{:S(2)}) copy-start(f32[2,2,64,128]{3,2,1,0:T(8,128)} %param.12) | copy-start | bytes 393220
  0.7 6.0 %copy-start = (f32[12,2,64,128]{3,2,1,0:T(8,128)S(1)}, f32[12,2,64,128]{3,2,1,0:T(8,128)}, u32[]{:S(2)}) copy-start(f32[12,2,64,128]{3,2,1,0:T(8,128)} %param.11) | copy-start | bytes 2359300
  0.7 6.0 %copy-start.2 = (f32[6,2,64,128]{3,2,1,0:T(8,128)S(1)}, f32[6,2,64,128]{3,2,1,0:T(8,128)}, u32[]{:S(2)}) copy-start(f32[6,2,64,128]{3,2,1,0:T(8,128)} %param.10) | copy-start | bytes 1179652
  3.5 16.8 %copy-start.1 = (bf16[512,640]{1,0:T(8,128)(2,1)S(1)}, bf16[512,640]{1,0:T(8,128)(2,1)}, u32[]{:S(2)}) copy-start(bf16[512,640]{1,0:T(8,128)(2,1)} %constant.11.clone.z_pack) | copy-start | bytes 1966084
  3.6 16.8 %copy-start.3 = (bf16[512,128]{1,0:T(8,128)(2,1)S(1)}, bf16[512,128]{1,0:T(8,128)(2,1)}, u32[]{:S(2)}) copy-start(bf16[512,128]{1,0:T(8,128)(2,1)} %constant.10.clone.z_main) | copy-start | bytes 393220
  3.6 16.8 %copy-start.7 = (bf16[64,256]{1,0:T(8,128)(2,1)S(1)}, bf16[64,256]{1,0:T(8,128)(2,1)}, u32[]{:S(2)}) copy-start(bf16[64,256]{1,0:T(8,128)(2,1)} %constant.8.clone.a_rows) | copy-start | bytes 98308
  3.6 16.7 %copy-start.9 = (f32[18]{0:T(128)S(1)}, f32[18]{0:T(128)}, u32[]{:S(2)}) copy-start(f32[18]{0:T(128)} %kappa.3) | copy-start | bytes 220
  3.6 5.0 %collective-permute-start = (f32[3,64,128]{2,1,0:T(8,128)}, f32[3,64,128]{2,1,0:T(8,128)S(1)}, u32[]{:S(2)}, u32[]{:S(2)}) collective-permute-start(f32[3,64,128]{2,1,0:T(8,128)} %get-tuple-element.18), channel_id=1, source_target_pairs={{0,1},{1,2},{2,3},{3,4},{4,5},{5,6},{6,7},{7,8},{8,9},{9,10},{10,1... | collective-permute-start | bytes 294920 | tf_op jit(solution)/shard_map/ppermute | solution.py:474
  6.6 7.9 %collective-permute-start.1 = (f32[3,64,128]{2,1,0:T(8,128)}, f32[3,64,128]{2,1,0:T(8,128)S(1)}, u32[]{:S(2)}, u32[]{:S(2)}) collective-permute-start(f32[3,64,128]{2,1,0:T(8,128)} %get-tuple-element.19), channel_id=1, source_target_pairs={{0,15},{1,0},{2,1},{3,2},{4,3},{5,4},{6,5},{7,6},{8,7},{9,8},{10,9... | collective-permute-start | bytes 294920 | tf_op jit(solution)/shard_map/ppermute | solution.py:474
  14.6 10.3 %collective-permute-start.2 = (f32[43,8,128]{2,1,0:T(8,128)S(1)}, f32[43,8,128]{2,1,0:T(8,128)S(1)}, u32[]{:S(2)}, u32[]{:S(2)}) collective-permute-start(f32[43,8,128]{2,1,0:T(8,128)S(1)} %get-tuple-element.26), channel_id=1, source_target_pairs={{0,16},{16,32},{32,48},{48,64},{64,80},{80,96},{96,112},{112,128},... | collective-permute-start | bytes 528392 | tf_op jit(solution)/shard_map/ppermute | solution.py:474
  14.9 9.9 %collective-permute-start.3 = (f32[43,8,128]{2,1,0:T(8,128)S(1)}, f32[43,8,128]{2,1,0:T(8,128)S(1)}, u32[]{:S(2)}, u32[]{:S(2)}) collective-permute-start(f32[43,8,128]{2,1,0:T(8,128)S(1)} %get-tuple-element.27), channel_id=1, source_target_pairs={{0,240},{16,0},{32,16},{48,32},{64,48},{80,64},{96,80},{112,96},{1... | collective-permute-start | bytes 528392 | tf_op jit(solution)/shard_map/ppermute | solution.py:474
  20.3 4.5 %copy-start.8 = (bf16[16,128]{1,0:T(8,128)(2,1)S(1)}, bf16[16,128]{1,0:T(8,128)(2,1)}, u32[]{:S(2)}) copy-start(bf16[16,128]{1,0:T(8,128)(2,1)} %constant.9.clone.a_edge) | copy-start | bytes 12292

commit v3 on v2

--- a/solution.py
+++ b/solution.py
@@ -70,7 +70,23 @@
     return 2 * (p + 9 * c) + ny if p < 9 else 4 * p + s
 
 
-def pack_z(mom, sca, vel, nuc, gro, zl, zr, fields, sems):
+def odd_of(axis):
+    return lax.axis_index(axis) % 2
+
+
+def z_messages(fields, r, t):
+    pair, odd = lanes() // 16, (lanes() // 8) % 2 == 1
+    tile = [None, None]
+    for j in range(4 if t < 2 else 3):
+        for s in range(4):
+            c = 2 * s + j // 2
+            one = roll(fields[plane_of(4 * t + j, s), r : r + 8, :], 16 * c + 8)
+            half = tile[j % 2]
+            tile[j % 2] = one if half is None else jnp.where(pair == c, one, half)
+    return jnp.where(odd, tile[1], roll(tile[0], -8)), jnp.where(odd, roll(tile[1], 8), tile[0])
+
+
+def pack_z(mom, sca, vel, nuc, gro, far, near, fields, sems):
     parts = [
         [(mom, 0, 0, 8), (sca, 6, 18, 8)],
         [(mom, 8, 8, 4), (sca, 0, 12, 4), (sca, 14, 26, 8)],
@@ -85,33 +101,31 @@
             )
             copies[-1][-1].start()
             n += 1
-    pair, odd = lanes() // 16, (lanes() // 8) % 2 == 1
+    right = odd_of("gz") == 0
     for t in range(3):
         for copy in copies[t]:
             copy.wait()
         for r in range(0, 64, 8):
-            tile = [None, None]
-            for j in range(4 if t < 2 else 3):
-                for s in range(4):
-                    c = 2 * s + j // 2
-                    one = roll(fields[plane_of(4 * t + j, s), r : r + 8, :], 16 * c + 8)
-                    half = tile[j % 2]
-                    tile[j % 2] = one if half is None else jnp.where(pair == c, one, half)
-            zr[t, r : r + 8, :] = jnp.where(odd, roll(tile[1], 8), tile[0])
-            zl[t, r : r + 8, :] = jnp.where(odd, tile[1], roll(tile[0], -8))
-
-
-def prepare(mom, sca, vel, nuc, gro, fields, own, up, down):
-    for src, to in ((mom, 0), (sca, 12), (vel, 36), (nuc, 40), (gro, 42)):
-        for k in range(src.shape[0]):
-            fields[to + k] = src[k]
-    for msg, lo, part in ((down, 0, 0), (up, 56, 60)):
+            zl, zr = z_messages(fields, r, t)
+            far[t, r : r + 8, :] = jnp.where(right, zl, zr)
+            near[t, r : r + 8, :] = jnp.where(right, zr, zl)
+
+
+def x_messages(fields, z_near, first, second, near):
+    near[...] = z_near[...]
+    odd = odd_of("gx") == 1
+    for k, msg in enumerate((first, second)):
+        low = odd if k == 0 else jnp.logical_not(odd)
+        at = pl.ds(pl.multiple_of(jnp.where(low, 0, 56), 8), 8)
         for i in range(38):
-            msg[i] = fields[i, lo : lo + 8, :]
-        for k in range(3):
-            for side in range(2):
-                i = 38 + side if k == 0 else 39 + k + 2 * side
-                msg[38 + k, 4 * side : 4 * side + 4, :] = fields[i, part : part + 4, :]
+            msg[i] = fields[i, at, :]
+        for n, i in enumerate((38, 39, 40, 42, 41, 43)):
+            tile = fields[i, at, :]
+            tile = jnp.where(low, tile[0:4], tile[4:8])
+            msg[38 + n // 2, 4 * (n % 2) : 4 * (n % 2) + 4, :] = tile
+
+
+def own_packs(fields, own):
     sub = lanes() // 8
     for p in range(11):
         for r in range(0, 64, 8):
@@ -123,31 +137,33 @@
             own[p, r : r + 8, :] = e
 
 
-def corners(from_left, from_right, up_in, down_in, up, down, buf, sems):
-    del up_in, down_in
-    first = lanes((4, 128)) % 8 < 4
-    for k, part in enumerate((0, 60)):
-        for t in range(3):
-            at = slice(4 * (t % 2), 4 * (t % 2) + 4)
-            rows = slice(part, part + 4)
-            buf[k, t // 2, at, :] = jnp.where(first, from_right[t, rows, :], from_left[t, rows, :])
-        buf[k, 1, 4:8, :] = jnp.zeros((4, 128), F32)
-    copies = [
-        pltpu.make_async_copy(buf.at[k], msg.at[pl.ds(41, 2)], sems.at[k])
-        for k, msg in enumerate((down, up))
-    ]
-    for copy in copies:
-        copy.start()
-    for copy in copies:
-        copy.wait()
-
-
-def fill_packs(own, from_left, from_right, packs):
+def corners(near, far, part, first, second):
+    del part
+    right = odd_of("gz") == 0
+    odd = odd_of("gx") == 1
+    inner = lanes((4, 128)) % 8 < 4
+    first[1, 4:8, :] = second[1, 4:8, :] = jnp.zeros((4, 128), F32)
+    for t in range(3):
+        at = slice(4 * (t % 2), 4 * (t % 2) + 4)
+        part = []
+        for rows in (slice(0, 4), slice(60, 64)):
+            from_near, from_far = near[t, rows, :], far[t, rows, :]
+            from_left = jnp.where(right, from_far, from_near)
+            part.append(jnp.where(inner, jnp.where(right, from_near, from_far), from_left))
+        first[t // 2, at, :] = jnp.where(odd, part[0], part[1])
+        second[t // 2, at, :] = jnp.where(odd, part[1], part[0])
+
+
+def fill_packs(own, near, far, packs):
     sub = (lanes((64, 128)) // 8) % 4
-    for p in range(11):
-        t, j = p // 4, p % 4
-        e = jnp.where(sub == 0, roll(from_left[t], -8 * j), own[p])
-        packs[p] = jnp.where(sub == 3, roll(from_right[t], 24 - 8 * j), e)
+    right = odd_of("gz") == 0
+    for t in range(3):
+        from_left = jnp.where(right, far[t], near[t])
+        from_right = jnp.where(right, near[t], far[t])
+        for j in range(4 if t < 2 else 3):
+            p = 4 * t + j
+            e = jnp.where(sub == 0, roll(from_left, -8 * j), own[p])
+            packs[p] = jnp.where(sub == 3, roll(from_right, 24 - 8 * j), e)
 
 
 def sources(get, nucl, grow, scale):
@@ -210,34 +226,25 @@
 GROUP = 3
 
 
-def interior(
-    kappa, fields, own, from_left, from_right, a_rows, z_main, z_pack, packs, q1, pq1, half,
-    us, ws, pus, pws, el, eo,
-):
-    def velocities(scale):
-        for ny in range(2):
-            us[ny] = fields[36 + ny] * (scale / first_part)
-            ws[ny] = fields[38 + ny] * (scale / first_part)
-        pu, pw = pack_velocity(packs[9])
-        pus[...] = pu * (scale / first_part)
-        pws[...] = pw * (scale / first_part)
-
-    fill_packs(own, from_left, from_right, packs)
+def groups(fn):
+    def step(i, _):
+        for k in range(GROUP):
+            fn(i * GROUP + k)
+        return _
+
+    lax.fori_loop(0, 9 // GROUP, step, 0)
+
+
+def plane_velocities(fields, us, ws, scale):
+    for ny in range(2):
+        us[ny] = fields[36 + ny] * (scale / first_part)
+        ws[ny] = fields[38 + ny] * (scale / first_part)
+
+
+def first_stage(kappa, fields, a_rows, z_main, part, own, us, ws):
     dt = time_step
-    velocities(dt)
-    for p in range(9):
-        e = packs[p]
-        kq = (pack_kappa(kappa, p) * (dt / second_part)) * e
-        el[64 * p : 64 * p + 64, :] = across(kq, pws[...] * e)
-    eo[...] = dot(el[...], z_pack[...])
-    for p in range(9):
-        e = packs[p]
-        kq = (pack_kappa(kappa, p) * (dt / second_part)) * e
-        x = dot(a_rows[...], down_rows(kq, pus[...] * e))
-        pq1[p] = e + x + eo[64 * p : 64 * p + 64, 512:640]
-    src = pack_sources(lambda k: packs[k], packs[10], dt)
-    for k in range(7):
-        pq1[k] += src[k]
+    own_packs(fields, own)
+    plane_velocities(fields, us, ws, dt)
 
     def one(p):
         lhs, rhs = [], []
@@ -249,37 +256,46 @@
         z = dot(jnp.concatenate(lhs, axis=0), z_main[...])
         x = [dot(a_rows[...], jnp.concatenate(rhs[c : c + 2], axis=1)) for c in (0, 2)]
         for i, field, ny, slot in planes(p):
-            q1[i] = (
-                fields[i]
-                + z[64 * slot : 64 * slot + 64]
-                + x[slot // 2][:, 128 * ny : 128 * ny + 128]
-                + eo[pl.ds(64 * p, 64), 128 * slot : 128 * slot + 128]
-            )
-
-    def groups(fn):
-        def step(i, _):
-            for k in range(GROUP):
-                fn(i * GROUP + k)
-            return _
-
-        if GROUP == 9:
-            for p in range(9):
-                fn(p)
-        else:
-            lax.fori_loop(0, 9 // GROUP, step, 0)
+            part[i] = fields[i] + z[64 * slot : 64 * slot + 64] + x[slot // 2][:, 128 * ny : 128 * ny + 128]
 
     groups(one)
     for ny in range(2):
         src = sources(lambda k: fields[2 * k + ny], fields[40 + ny], fields[42 + ny], dt)
         for k in range(7):
-            q1[2 * k + ny] += src[k]
-
-    scale = 0.5 * dt
-    velocities(scale)
+            part[2 * k + ny] += src[k]
+
+
+def interior(
+    kappa, fields, part, own, near, far, a_rows, z_main, z_pack, packs, q1, pq1, half,
+    us, ws, pus, pws, el, eo,
+):
+    fill_packs(own, near, far, packs)
+    dt, scale = time_step, 0.5 * time_step
+    pu, pw = pack_velocity(packs[9])
+    pus[...] = pu * (dt / first_part)
+    pws[...] = pw * (dt / first_part)
+    for p in range(9):
+        e = packs[p]
+        kq = (pack_kappa(kappa, p) * (dt / second_part)) * e
+        el[64 * p : 64 * p + 64, :] = across(kq, pws[...] * e)
+    eo[...] = dot(el[...], z_pack[...])
+    for p in range(9):
+        e = packs[p]
+        kq = (pack_kappa(kappa, p) * (dt / second_part)) * e
+        x = dot(a_rows[...], down_rows(kq, pus[...] * e))
+        pq1[p] = e + x + eo[64 * p : 64 * p + 64, 512:640]
+    src = pack_sources(lambda k: packs[k], packs[10], dt)
+    for k in range(7):
+        pq1[k] += src[k]
+    for p in range(9):
+        for i, field, ny, slot in planes(p):
+            q1[i] = part[i] + eo[64 * p : 64 * p + 64, 128 * slot : 128 * slot + 128]
+
+    plane_velocities(fields, us, ws, scale)
     for p in range(9):
         e = pq1[p, 8:56, :]
         kq = (pack_kappa(kappa, p) * (scale / second_part)) * e
-        el[48 * p : 48 * p + 48, :] = across(kq, pws[8:56, :] * e)
+        el[48 * p : 48 * p + 48, :] = across(kq, (0.5 * pws[8:56, :]) * e)
     eo[0:432, 0:512] = dot(el[0:432, :], z_pack[:, 0:512])
 
     def two(p):
@@ -310,7 +326,7 @@
 
 
 def edges(
-    kappa, fields, packs, q1, pq1, half, above, below, a_edge, z_main, z_pack, out_mom, out_sca,
+    kappa, fields, packs, q1, pq1, half, first, second, first_corner, second_corner, a_edge, z_main, z_pack, out_mom, out_sca,
     q, s1, vq, v1, pq, ps1, pvq, el, eo, done, sems,
 ):
     outs = [(out_mom, 0, 12), (out_sca, 12, 24)]
@@ -326,24 +342,27 @@
     top, low = slice(4, 12), slice(20, 28)
     mid = lambda ref, *at: jnp.concatenate([ref[*at, top, :], ref[*at, low, :]], axis=0)
 
+    odd = odd_of("gx") == 1
+    above = lambda i, at=slice(0, 8): jnp.where(odd, first[i, at, :], second[i, at, :])
+    below = lambda i, at=slice(0, 8): jnp.where(odd, second[i, at, :], first[i, at, :])
     for i in range(36):
-        q[i, 0:8, :] = above[i]
+        q[i, 0:8, :] = above(i)
         q[i, 8:16, :] = fields[i, 0:8, :]
         q[i, 16:24, :] = fields[i, 56:64, :]
-        q[i, 24:32, :] = below[i]
+        q[i, 24:32, :] = below(i)
         s1[i, 8:16, :] = q1[i, 4:12, :]
         s1[i, 16:24, :] = q1[i, 52:60, :]
     one, two = dt / first_part, 0.5 * dt / first_part
     for i in range(4):
         k = 36 + i
         if i < 2:
-            vq[i, 0:8, :] = above[k] * one
-            vq[i, 24:32, :] = below[k] * one
+            vq[i, 0:8, :] = above(k) * one
+            vq[i, 24:32, :] = below(k) * one
         else:
             at = slice(4 * (i % 2), 4 * (i % 2) + 4)
             vq[i, 0:4, :] = vq[i, 28:32, :] = jnp.zeros((4, 128), F32)
-            vq[i, 4:8, :] = above[38, at, :] * one
-            vq[i, 24:28, :] = below[38, at, :] * one
+            vq[i, 4:8, :] = above(38, at) * one
+            vq[i, 24:28, :] = below(38, at) * one
         vq[i, 8:16, :] = fields[k, 0:8, :] * one
         vq[i, 16:24, :] = fields[k, 56:64, :] * one
         v1[i, 0:4, :] = vq[i, 4:8, :] * 0.5
@@ -356,7 +375,8 @@
     for p in range(10):
         t, j = p // 4, p % 4
         at = slice(4 * (t % 2), 4 * (t % 2) + 4)
-        corner = jnp.concatenate([above[41 + t // 2, at, :], below[41 + t // 2, at, :]], axis=0)
+        one_c, two_c = first_corner[t // 2, at, :], second_corner[t // 2, at, :]
+        corner = jnp.concatenate([jnp.where(odd, one_c, two_c), jnp.where(odd, two_c, one_c)], axis=0)
         corner = jnp.where(
             is_left, roll(corner, -8 * j), jnp.where(is_right, roll(corner, 24 - 8 * j), 0.0)
         )
@@ -418,7 +438,7 @@
 
     stage(q, vq, dt, put_one)
     for ny in range(2):
-        near, far = above[39 + ny], below[39 + ny]
+        near, far = above(39 + ny), below(39 + ny)
         nucl = jnp.concatenate([near[0:4], fields[40 + ny, 0:4, :], fields[40 + ny, 60:64, :], far[0:4]], axis=0)
         grow = jnp.concatenate([near[4:8], fields[42 + ny, 0:4, :], fields[42 + ny, 60:64, :], far[4:8]], axis=0)
         src = sources(lambda k: mid(q, 2 * k + ny), nucl, grow, dt)
@@ -469,9 +489,10 @@
     )
 
 
-def send(value, axis, by):
+def swap(value, axis, far):
     peers = lax.axis_size(axis)
-    return lax.ppermute(value, axis, [(i, (i + by) % peers) for i in range(peers)])
+    other = lambda i: (((i + far) ^ 1) - far) % peers
+    return lax.ppermute(value, axis, [(i, other(i)) for i in range(peers)])
 
 
 def body(moments, scalars, velocity, diffusivity, nucleation, growth):
@@ -479,54 +500,57 @@
     smem = pl.BlockSpec(memory_space=pltpu.SMEM)
     hbm = pl.BlockSpec(memory_space=pltpu.HBM)
     tiles = lambda *lead: pltpu.VMEM(lead + (128,), F32)
-    flat = [x.reshape(-1, 64, 128) for x in (moments, scalars, velocity, nucleation, growth)]
+    flat = [
+        pltpu.with_memory_space_constraint(x.reshape(-1, 64, 128), pltpu.HBM)
+        for x in (moments, scalars, velocity, nucleation, growth)
+    ]
     a_rows, a_edge, z_main, z_pack = (jnp.asarray(m) for m in matrices())
 
-    zl, zr = call(
+    z_far, z_near, fields = call(
         pack_z,
-        [(3, 64, 128), (3, 64, 128)],
+        [(3, 64, 128), (3, 64, 128), (44, 64, 128)],
         10**6,
-        56,
         in_specs=[hbm] * 5,
-        out_specs=[vmem] * 2,
-        scratch_shapes=[tiles(44, 64), pltpu.SemaphoreType.DMA((10,))],
+        out_specs=[vmem] * 3,
+        scratch_shapes=[pltpu.SemaphoreType.DMA((10,))],
     )(*flat)
-    from_right = send(zl, "gz", -1)
-    from_left = send(zr, "gz", 1)
-    fields, own, up, down = call(
-        prepare, [(44, 64, 128), (11, 64, 128), (43, 8, 128), (43, 8, 128)], 10**6
-    )(*flat)
-    up, down = call(
-        corners,
-        [(43, 8, 128), (43, 8, 128)],
-        10**6,
-        in_specs=[vmem] * 2 + [pl.BlockSpec(memory_space=pl.ANY)] * 2,
-        out_specs=[pl.BlockSpec(memory_space=pl.ANY)] * 2,
-        input_output_aliases={2: 0, 3: 1},
-        scratch_shapes=[tiles(2, 2, 8), pltpu.SemaphoreType.DMA((2,))],
-    )(from_left, from_right, up, down)
-    above = send(up, "gx", 1)
-    below = send(down, "gx", -1)
+    far = swap(z_far, "gz", 1)
+    x_first, x_second, z_near = call(x_messages, [(41, 8, 128), (41, 8, 128), (3, 64, 128)], 10**5)(fields, z_near)
+    near = swap(z_near, "gz", 0)
+    part, own = call(
+        first_stage,
+        [(36, 64, 128), (11, 64, 128)],
+        10**7,
+        in_specs=[smem] + [vmem] * 3,
+        scratch_shapes=[tiles(2, 64), tiles(2, 64)],
+    )(diffusivity, fields, a_rows, z_main)
+    second = swap(x_second, "gx", 1)
+    first = swap(x_first, "gx", 0)
+    c_first, c_second = call(corners, [(2, 8, 128)] * 2, 10**6)(near, far, part)
+    second_corner = swap(c_second, "gx", 1)
+    first_corner = swap(c_first, "gx", 0)
     packs, q1, pq1, half = call(
         interior,
         [(11, 64, 128), (36, 64, 128), (9, 64, 128), (36, 64, 128)],
-        10**8,
-        in_specs=[smem] + [vmem] * 7,
+        10 * 10**8,
+        in_specs=[smem] + [vmem] * 8,
         scratch_shapes=[
             tiles(2, 64), tiles(2, 64), tiles(64), tiles(64), pltpu.VMEM((576, 512), BF16), pltpu.VMEM((576, 640), F32),
         ],
-    )(diffusivity, fields, own, from_left, from_right, a_rows, z_main, z_pack)
+    )(diffusivity, fields, part, own, near, far, a_rows, z_main, z_pack)
     out_mom, out_sca = call(
         edges,
         [(12, 64, 128), (24, 64, 128)],
         10**8,
-        in_specs=[smem] + [vmem] * 10,
+        in_specs=[smem] + [vmem] * 12,
         out_specs=[hbm] * 2,
         scratch_shapes=[
             tiles(36, 32), tiles(36, 32), tiles(4, 32), tiles(4, 32), tiles(10, 32), tiles(9, 32), tiles(2, 32),
             pltpu.VMEM((144, 512), BF16), pltpu.VMEM((144, 640), F32), tiles(36, 16), pltpu.SemaphoreType.DMA((6,)),
         ],
-    )(diffusivity, fields, packs, q1, pq1, half, above, below, a_edge, z_main, z_pack)
+    )(
+            diffusivity, fields, packs, q1, pq1, half, first, second, first_corner, second_corner, a_edge, z_main, z_pack
+        )
     return out_mom.reshape(moments.shape), out_sca.reshape(scalars.shape)
 
 

time: 27.8 us -> 26.8 us (0.964)
  waiting for transfers between devices: 7.03 us -> 0.09 us
  starting transfers between devices: 8.78 us -> 15 us
  Pallas kernels: 11 us -> 10.7 us
    ppermute x4 -> x6, waiting for transfers between devices: 7.03 us -> 0.09 us  [swap(): return lax.ppermute(value, axis, [(i, other(i)) for i in range(peers)])]
    ppermute x4 -> x6, starting transfers between devices: 8.78 us -> 15 us  [swap(): return lax.ppermute(value, axis, [(i, other(i)) for i in range(peers)])]
    pallas_call x1, Pallas kernels: 4.5 us -> 2.95 us  [body(): call(interior, [(11, 64, 128), (36, 64, 128), (9, 64, 128), (36, 64, 128)...]
    pallas_call x3 -> x4, Pallas kernels: 3.72 us -> 4.97 us  [the longest x1 2.75 us: body(): call(first_stage, [(36, 64, 128), (11, 64, 128)], 10 ** 7, in_specs=[smem...]
  transfers between devices with their start and end apart: 4 -> 6, of which waited for: 2 -> 1; matrix products, arithmetic and copies ran while one was open for 0% -> 0% of each run, Pallas kernels for 19% -> 21%
where the time goes in v3:
time: 26.8 us; the launch traced here: 26.6 us
  starting transfers between devices  15 us (56%)
  Pallas kernels  10.7 us (40%)
  between operations  0.75 us (3%)
    ppermute x6, starting transfers between devices, swap(): return lax.ppermute(value, axis, [(i, other(i)) for i in range(peers)])  15 us
    pallas_call x1, Pallas kernels, body(): call(interior, [(11, 64, 128), (36, 64, 128), (9, 64, 128), (36, 64, 128)...  2.95 us
    pallas_call x1, Pallas kernels, body(): call(edges, [(12, 64, 128), (24, 64, 128)], 10 ** 8, in_specs=[smem] + [v...  2.82 us
    pallas_call x1, Pallas kernels, body(): call(first_stage, [(36, 64, 128), (11, 64, 128)], 10 ** 7, in_specs=[smem...  2.75 us
    pallas_call x1, Pallas kernels, body(): call(pack_z, [(3, 64, 128), (3, 64, 128), (44, 64, 128)], 10 ** 6, in_spe...  2.14 us
  transfers between devices with their start and end apart: 6, of which 1 were waited for; matrix products, arithmetic and copies ran while one was open for 0% of the time, Pallas kernels for 21%

profile of v3, /device:TPU:25, one launch (start us, length us, event | category | flops | bytes accessed | tf_op | source)
XLA Modules:
  0.0 26.6 jit_solution(11481355648638387004)
XLA Ops:
  0.6 0.0 copy-start.1
  0.6 0.0 copy-start.2
  0.7 0.0 copy-start.3
  0.7 2.1 %shard_map.113 = (f32[3,64,128]{2,1,0:T(8,128)S(1)}, f32[3,64,128]{2,1,0:T(8,128)S(1)}, f32[44,64,128]{2,1,0:T(8,128)S(1)}) custom-call(f32[12,64,128]{2,1,0:T(8,128)} %bitcast.6, f32[24,64,128]{2,1,0:T(8,128)} %bitcast.5, f32[4,64,128]{2,1,0:T(8,128)} %bitcast.7, f32[2,64,128]{2,1,0:T(8,128)} %nuc.1, f32[2,64,128]{2,1,0:T(8,128)} %gro.1), custom_call_target="tpu_custom_call" | custom-call | flops 1000000 | bytes 250000 | tf_op jit(solution)/shard_map/pallas_call | solution.py:509
  2.8 0.1 shard_map.115
  2.9 0.8 %collective-permute-start = (f32[3,64,128]{2,1,0:T(8,128)S(1)}, f32[3,64,128]{2,1,0:T(8,128)S(1)}, u32[]{:S(2)}, u32[]{:S(2)}) collective-permute-start(f32[3,64,128]{2,1,0:T(8,128)S(1)} %get-tuple-element.22), channel_id=1, source_target_pairs={{0,1},{1,0},{2,3},{3,2},{4,5},{5,4},{6,7},{7,6},{8,9},{9,8},{10,11... | collective-permute-start | bytes 294920 | tf_op jit(solution)/shard_map/ppermute | solution.py:495
  3.7 2.4 %collective-permute-start.1 = (f32[3,64,128]{2,1,0:T(8,128)S(1)}, f32[3,64,128]{2,1,0:T(8,128)S(1)}, u32[]{:S(2)}, u32[]{:S(2)}) collective-permute-start(f32[3,64,128]{2,1,0:T(8,128)S(1)} %get-tuple-element.23), channel_id=1, source_target_pairs={{0,15},{1,2},{2,1},{3,4},{4,3},{5,6},{6,5},{7,8},{8,7},{9,10},{10,... | collective-permute-start | bytes 294920 | tf_op jit(solution)/shard_map/ppermute | solution.py:495
  6.0 0.3 %collective-permute-start.2 = (f32[41,8,128]{2,1,0:T(8,128)S(1)}, f32[41,8,128]{2,1,0:T(8,128)S(1)}, u32[]{:S(2)}, u32[]{:S(2)}) collective-permute-start(f32[41,8,128]{2,1,0:T(8,128)S(1)} %get-tuple-element.28), channel_id=1, source_target_pairs={{0,16},{16,0},{32,48},{48,32},{64,80},{80,64},{96,112},{112,96},{1... | collective-permute-start | bytes 503816 | tf_op jit(solution)/shard_map/ppermute | solution.py:495
  6.4 6.4 %collective-permute-start.3 = (f32[41,8,128]{2,1,0:T(8,128)S(1)}, f32[41,8,128]{2,1,0:T(8,128)S(1)}, u32[]{:S(2)}, u32[]{:S(2)}) collective-permute-start(f32[41,8,128]{2,1,0:T(8,128)S(1)} %get-tuple-element.29), channel_id=1, source_target_pairs={{0,240},{16,32},{32,16},{48,64},{64,48},{80,96},{96,80},{112,128},... | collective-permute-start | bytes 503816 | tf_op jit(solution)/shard_map/ppermute | solution.py:495
  12.8 0.0 copy-done.1
  12.8 0.0 copy-done.2
  12.8 2.7 %shard_map.114 = (f32[36,64,128]{2,1,0:T(8,128)S(1)}, f32[11,64,128]{2,1,0:T(8,128)S(1)}) custom-call(f32[18]{0:T(128)S(1)} %copy-done.3, f32[44,64,128]{2,1,0:T(8,128)S(1)} %get-tuple-element.18.fields, bf16[64,256]{1,0:T(8,128)(2,1)S(1)} %copy-done.2, bf16[512,128]{1,0:T(8,128)(2,1)S(1)} %copy-done.1), custom_call_target="tpu_custom_call" | custom-call | flops 10000000 | bytes 2500000 | tf_op jit(solution)/shard_map/pallas_call | solution.py:520
  15.6 0.0 collective-permute-done.near
  15.6 0.1 collective-permute-done.1.far
  15.7 0.1 collective-permute-start.4
  15.8 5.0 %collective-permute-start.5 = (f32[2,8,128]{2,1,0:T(8,128)S(1)}, f32[2,8,128]{2,1,0:T(8,128)S(1)}, u32[]{:S(2)}, u32[]{:S(2)}) collective-permute-start(f32[2,8,128]{2,1,0:T(8,128)S(1)} %get-tuple-element.31), channel_id=1, source_target_pairs={{0,240},{16,32},{32,16},{48,64},{64,48},{80,96},{96,80},{112,128},... | collective-permute-start | bytes 24584 | tf_op jit(solution)/shard_map/ppermute | solution.py:495
  20.7 0.0 copy-done
  20.7 2.9 %shard_map.116 = (f32[11,64,128]{2,1,0:T(8,128)S(1)}, f32[36,64,128]{2,1,0:T(8,128)S(1)}, f32[9,64,128]{2,1,0:T(8,128)S(1)}, f32[36,64,128]{2,1,0:T(8,128)S(1)}) custom-call(f32[18]{0:T(128)S(1)} %copy-done.3, f32[44,64,128]{2,1,0:T(8,128)S(1)} %get-tuple-element.18.fields, f32[36,64,128]{2,1,0:T(8,128)S(1)} %get-tuple-element.19.part, ...), custom_call_target="tpu_custom_call" | custom-call | flops 1000000000 | bytes 250000000 | tf_op jit(solution)/shard_map/pallas_call | solution.py:532
  23.7 0.0 collective-permute-done.4.first_corner
  23.7 0.0 collective-permute-done.5.second_corner
  23.7 0.0 collective-permute-done.2.first
  23.7 0.0 collective-permute-done.3.second
  23.7 0.0 copy-done.4
  23.8 2.8 %shard_map.118 = (f32[12,64,128]{2,1,0:T(8,128)}, f32[24,64,128]{2,1,0:T(8,128)}) custom-call(f32[18]{0:T(128)S(1)} %copy-done.3, f32[44,64,128]{2,1,0:T(8,128)S(1)} %get-tuple-element.18.fields, f32[11,64,128]{2,1,0:T(8,128)S(1)} %get-tuple-element.24.packs, f32[36,64,128]{2,1,0:T(8,128)S(1)} %get-tuple-element.25.q1, ...), custom_call_target="tpu_custom_call" | custom-call | flops 100000000 | bytes 25000000 | tf_op jit(solution)/shard_map/pallas_call | solution.py:541
  (4 shorter events, 0.0 us)
Async XLA Ops:
  0.6 12.2 %copy-start.1 = (bf16[512,128]{1,0:T(8,128)(2,1)S(1)}, bf16[512,128]{1,0:T(8,128)(2,1)}, u32[]{:S(2)}) copy-start(bf16[512,128]{1,0:T(8,128)(2,1)} %constant.10.clone.z_main) | copy-start | bytes 393220
  0.6 12.2 %copy-start.2 = (bf16[64,256]{1,0:T(8,128)(2,1)S(1)}, bf16[64,256]{1,0:T(8,128)(2,1)}, u32[]{:S(2)}) copy-start(bf16[64,256]{1,0:T(8,128)(2,1)} %constant.8.clone.a_rows) | copy-start | bytes 98308
  0.7 12.2 %copy-start.3 = (f32[18]{0:T(128)S(1)}, f32[18]{0:T(128)}, u32[]{:S(2)}) copy-start(f32[18]{0:T(128)} %kappa.5) | copy-start | bytes 220
  2.9 12.7 %collective-permute-start = (f32[3,64,128]{2,1,0:T(8,128)S(1)}, f32[3,64,128]{2,1,0:T(8,128)S(1)}, u32[]{:S(2)}, u32[]{:S(2)}) collective-permute-start(f32[3,64,128]{2,1,0:T(8,128)S(1)} %get-tuple-element.22), channel_id=1, source_target_pairs={{0,1},{1,0},{2,3},{3,2},{4,5},{5,4},{6,7},{7,6},{8,9},{9,8},{10,11... | collective-permute-start | bytes 294920 | tf_op jit(solution)/shard_map/ppermute | solution.py:495
  3.7 12.0 %collective-permute-start.1 = (f32[3,64,128]{2,1,0:T(8,128)S(1)}, f32[3,64,128]{2,1,0:T(8,128)S(1)}, u32[]{:S(2)}, u32[]{:S(2)}) collective-permute-start(f32[3,64,128]{2,1,0:T(8,128)S(1)} %get-tuple-element.23), channel_id=1, source_target_pairs={{0,15},{1,2},{2,1},{3,4},{4,3},{5,6},{6,5},{7,8},{8,7},{9,10},{10,... | collective-permute-start | bytes 294920 | tf_op jit(solution)/shard_map/ppermute | solution.py:495
  6.0 17.7 %collective-permute-start.2 = (f32[41,8,128]{2,1,0:T(8,128)S(1)}, f32[41,8,128]{2,1,0:T(8,128)S(1)}, u32[]{:S(2)}, u32[]{:S(2)}) collective-permute-start(f32[41,8,128]{2,1,0:T(8,128)S(1)} %get-tuple-element.28), channel_id=1, source_target_pairs={{0,16},{16,0},{32,48},{48,32},{64,80},{80,64},{96,112},{112,96},{1... | collective-permute-start | bytes 503816 | tf_op jit(solution)/shard_map/ppermute | solution.py:495
  6.4 14.4 %copy-start = (bf16[512,640]{1,0:T(8,128)(2,1)S(1)}, bf16[512,640]{1,0:T(8,128)(2,1)}, u32[]{:S(2)}) copy-start(bf16[512,640]{1,0:T(8,128)(2,1)} %constant.11.clone.z_pack) | copy-start | bytes 1966084
  6.4 17.4 %collective-permute-start.3 = (f32[41,8,128]{2,1,0:T(8,128)S(1)}, f32[41,8,128]{2,1,0:T(8,128)S(1)}, u32[]{:S(2)}, u32[]{:S(2)}) collective-permute-start(f32[41,8,128]{2,1,0:T(8,128)S(1)} %get-tuple-element.29), channel_id=1, source_target_pairs={{0,240},{16,32},{32,16},{48,64},{64,48},{80,96},{96,80},{112,128},... | collective-permute-start | bytes 503816 | tf_op jit(solution)/shard_map/ppermute | solution.py:495
  15.7 8.0 %collective-permute-start.4 = (f32[2,8,128]{2,1,0:T(8,128)S(1)}, f32[2,8,128]{2,1,0:T(8,128)S(1)}, u32[]{:S(2)}, u32[]{:S(2)}) collective-permute-start(f32[2,8,128]{2,1,0:T(8,128)S(1)} %get-tuple-element.30), channel_id=1, source_target_pairs={{0,16},{16,0},{32,48},{48,32},{64,80},{80,64},{96,112},{112,96},{1... | collective-permute-start | bytes 24584 | tf_op jit(solution)/shard_map/ppermute | solution.py:495
  15.8 7.9 %collective-permute-start.5 = (f32[2,8,128]{2,1,0:T(8,128)S(1)}, f32[2,8,128]{2,1,0:T(8,128)S(1)}, u32[]{:S(2)}, u32[]{:S(2)}) collective-permute-start(f32[2,8,128]{2,1,0:T(8,128)S(1)} %get-tuple-element.31), channel_id=1, source_target_pairs={{0,240},{16,32},{32,16},{48,64},{64,48},{80,96},{96,80},{112,128},... | collective-permute-start | bytes 24584 | tf_op jit(solution)/shard_map/ppermute | solution.py:495
  20.7 3.0 %copy-start.4 = (bf16[16,128]{1,0:T(8,128)(2,1)S(1)}, bf16[16,128]{1,0:T(8,128)(2,1)}, u32[]{:S(2)}) copy-start(bf16[16,128]{1,0:T(8,128)(2,1)} %constant.9.clone.a_edge) | copy-start | bytes 12292

commit v4 on v3

v4 whole, which is shorter than its diff:
```python
import numpy as np

import jax
import jax.numpy as jnp
from jax import lax
from jax.experimental import pallas as pl
from jax.experimental.pallas import tpu as pltpu
from jax.sharding import PartitionSpec as P

first_whole, first_part = (672.0, -168.0, 32.0, -3.0), 840.0
second_whole, second_part = (8064.0, -1008.0, 128.0, -9.0), 5040.0
centre_x, centre_z = -28672.0, -28.0
time_step = 0.25

F32, BF16 = jnp.float32, jnp.bfloat16


def band(targets, sources, centre):
    gap = np.asarray(sources)[None, :] - np.asarray(targets)[:, None]
    second = np.where(gap == 0, centre, 0.0)
    first = np.zeros(gap.shape)
    for m in range(1, 5):
        second = second + second_whole[m - 1] * (abs(gap) == m)
        first = first - first_whole[m - 1] * ((gap == m) * 1.0 - (gap == -m))
    return second, first


rows_h = [64, 65, 66, 67, -4, -3, -2, -1]
rows_o = [-8, -7, -6, -5, 68, 69, 70, 71]
rows_a = [0, 1, 2, 3, 60, 61, 62, 63]
rows_b = [56, 57, 58, 59, 4, 5, 6, 7]
rows_c = [8, 9, 10, 11, 52, 53, 54, 55]


def matrices():
    both = lambda pair, axis: np.concatenate([pair[0], pair[0], pair[1], pair[1]], axis=axis)
    rows, cols = np.arange(64), np.arange(128)
    a_rows = both(band(rows, rows, centre_x), 1)
    far = band(rows_h + rows_a, rows_h + rows_o, centre_x)
    own = [m * (np.arange(16) < 8)[:, None] for m in band(rows_h + rows_a, rows_a, centre_x)]
    a_one = np.concatenate([both(far, 1), own[0], own[1], own[0], own[1]], axis=1)
    a_two = np.concatenate(
        [both(band(rows_a + rows_b, src, centre_x), 1) for src in (rows_a + rows_b, rows_h + rows_c)], axis=1
    )
    corner = [np.concatenate([m, 0 * m]) for m in band(rows_a, rows_h, centre_x)]
    a_corner = np.concatenate(corner + corner, axis=1)
    z_main = both([m.T for m in band(cols, cols, centre_z)], 0)
    blocks = lambda pair: both([np.kron(np.eye(16), m.T) for m in pair], 0)
    outer = [128, 129, 130, 131, -4, -3, -2, -1]
    z_outer = np.concatenate(
        [blocks(band(outer, np.arange(at, at + 8), centre_z)) for at in (-8, 0, 128, 120)]
    )
    z_inner = blocks(band([124, 125, 126, 127, 0, 1, 2, 3], outer, centre_z))
    return [m.astype(BF16) for m in (a_rows, a_one, a_two, a_corner, z_main, z_outer, z_inner)]


def lanes(shape=(8, 128)):
    return lax.broadcasted_iota(jnp.int32, shape, len(shape) - 1)


def roll(x, by):
    by = by % 128
    return x if by == 0 else pltpu.roll(x, by, 1)


def split(x):
    high = x.astype(BF16)
    return high, (x - high.astype(F32)).astype(BF16)


def dot(a, b):
    return jnp.dot(a, b, preferred_element_type=F32)


def plane_of(p, s):
    c, ny = s // 2, s % 2
    return 2 * (p + 9 * c) + ny if p < 9 else 4 * p + s


def odd_of(axis):
    return lax.axis_index(axis) % 2


def z_messages(fields, r, t):
    pair, odd = lanes() // 16, (lanes() // 8) % 2 == 1
    tile = [None, None]
    for j in range(4 if t < 2 else 3):
        for s in range(4):
            c = 2 * s + j // 2
            one = roll(fields[plane_of(4 * t + j, s), r : r + 8, :], 16 * c + 8)
            half = tile[j % 2]
            tile[j % 2] = one if half is None else jnp.where(pair == c, one, half)
    return jnp.where(odd, tile[1], roll(tile[0], -8)), jnp.where(odd, roll(tile[1], 8), tile[0])


def pack_z(mom, sca, vel, nuc, gro, far, near, fields, sems):
    parts = [
        [(mom, 0, 0, 8), (sca, 6, 18, 8)],
        [(mom, 8, 8, 4), (sca, 0, 12, 4), (sca, 14, 26, 8)],
        [(sca, 4, 16, 2), (sca, 22, 34, 2), (vel, 0, 36, 4), (nuc, 0, 40, 2), (gro, 0, 42, 2)],
    ]
    copies, n = [], 0
    for part in parts:
        copies.append([])
        for src, at, to, size in part:
            copies[-1].append(
                pltpu.make_async_copy(src.at[pl.ds(at, size)], fields.at[pl.ds(to, size)], sems.at[n])
            )
            copies[-1][-1].start()
            n += 1
    right = odd_of("gz") == 0
    for t in range(3):
        for copy in copies[t]:
            copy.wait()
        for r in range(0, 64, 8):
            zl, zr = z_messages(fields, r, t)
            far[t, r : r + 8, :] = jnp.where(right, zl, zr)
            near[t, r : r + 8, :] = jnp.where(right, zr, zl)


def halves(first):
    return (lax.broadcasted_iota(jnp.int32, (8, 128), 0) + 4 * first) % 8 >= 4


def x_messages(fields, z_near, first, second, near):
    near[...] = z_near[...]
    odd = odd_of("gx") == 1
    for k, msg in enumerate((first, second)):
        low = odd if k == 0 else jnp.logical_not(odd)
        at = pl.ds(pl.multiple_of(jnp.where(low, 0, 56), 8), 8)
        for i in range(38):
            msg[i] = fields[i, at, :]
        keep = halves(low.astype(jnp.int32))
        for n, (i, j) in enumerate(((38, 39), (40, 42), (41, 43))):
            msg[38 + n] = jnp.where(keep, fields[i, at, :], pltpu.roll(fields[j, at, :], 4, 0))


def outer_tile(from_left, from_right):
    return jnp.where(lanes(from_left.shape) % 8 >= 4, from_left, from_right)


def sides(near, far):
    right = odd_of("gz") == 0
    return jnp.where(right, far, near), jnp.where(right, near, far)


def corners(near, far, part, first, second):
    del part
    odd = odd_of("gx") == 1
    for k, msg in enumerate((first, second)):
        low = odd if k == 0 else jnp.logical_not(odd)
        at = pl.ds(pl.multiple_of(jnp.where(low, 0, 56), 8), 8)
        keep = halves(low.astype(jnp.int32))
        tile = [outer_tile(*sides(near[t, at, :], far[t, at, :])) for t in range(3)]
        msg[0] = jnp.where(keep, tile[0], pltpu.roll(tile[1], 4, 0))
        msg[1] = jnp.where(keep, tile[2], 0.0)


def spread(tile, j):
    x = jnp.where((lanes(tile.shape) // 8) % 4 == j, tile, 0.0)
    x = x + roll(x, -8 if j % 2 else 8)
    return x + roll(x, -16 if j >= 2 else 16)


def block_velocity(tile):
    x = spread(tile, 1)
    low, other = lanes(tile.shape) < 64, roll(x, 64)
    return jnp.where(low, x, other), jnp.where(low, other, x)


def block_kappa(kappa, t):
    block = lanes((1, 128)) // 8
    out = jnp.zeros((1, 128), F32)
    for j in range(4):
        for c in range(2):
            if 4 * t + j < 9:
                out = jnp.where((block % 4 == j) & (block // 8 == c), kappa[4 * t + j + 9 * c], out)
    return out


def block_sources(tiles, scale):
    shape = tiles[0].shape
    block = lanes(shape) // 8
    low, j = block < 8, block % 4
    ng = spread(tiles[2], 2)
    nucl, grow = jnp.where(low, ng, 0.0), jnp.where(low, roll(ng, 64), 0.0)
    y = spread(tiles[1], 2)
    birth = nucl * y * y
    sink = jnp.where(low, (0.3 * scale) * spread(tiles[0], 0), 0.0)
    before = (roll(tiles[0], 8), jnp.where(j == 0, roll(tiles[0], -24), roll(tiles[1], 8)))
    out = []
    for t in range(2):
        order = (scale / 3.0) * (j + 4 * t).astype(F32)
        out.append((0.5 * scale) * birth + (order * grow) * before[t] - sink * tiles[t])
    out[1] = jnp.where(j < 2, out[1], jnp.where(j == 2, (-0.2 * scale) * birth, 0.0))
    return out


def unpack(tile, b):
    lane = lanes(tile.shape)
    return jnp.where((lane < 4) | (lane >= 124), roll(tile, 124 - 8 * b), 0.0)


def sources(get, nucl, grow, scale):
    y = get(6)
    birth = nucl * y * y
    moms = [get(k) for k in range(6)]
    half = (0.5 * scale) * birth
    sink = (0.3 * scale) * moms[0]
    out = []
    for k in range(6):
        s = half - sink * moms[k]
        if k:
            s = s + ((scale * k / 3.0) * grow) * moms[k - 1]
        out.append(s)
    return out + [(-0.2 * scale) * birth]


def planes(p):
    for slot in range(4):
        field, ny = p + 9 * (slot // 2), slot % 2
        yield 2 * field + ny, field, ny, p // 4, 4 * slot + p % 4


def across(kq, g):
    return jnp.concatenate([*split(kq), *split(g)], axis=1)


def down_rows(kq, f):
    return jnp.concatenate([*split(kq), *split(f)], axis=0)


GROUP = 3


def groups(fn):
    def step(i, _):
        for k in range(GROUP):
            fn(i * GROUP + k)
        return _

    lax.fori_loop(0, 9 // GROUP, step, 0)


def plane_velocities(fields, us, ws, scale):
    for ny in range(2):
        us[ny] = fields[36 + ny] * (scale / first_part)
        ws[ny] = fields[38 + ny] * (scale / first_part)


def first_stage(kappa, fields, a_rows, z_main, part, us, ws):
    dt = time_step
    plane_velocities(fields, us, ws, dt)

    def one(p):
        lhs, rhs = [], []
        for i, field, ny, t, b in planes(p):
            v = fields[i]
            kq = (kappa[field] * (dt / second_part)) * v
            lhs.append(across(kq, ws[ny] * v))
            rhs.append(down_rows(kq, us[ny] * v))
        z = dot(jnp.concatenate(lhs, axis=0), z_main[...])
        x = [dot(a_rows[...], jnp.concatenate(rhs[c : c + 2], axis=1)) for c in (0, 2)]
        for n, (i, field, ny, t, b) in enumerate(planes(p)):
            part[i] = fields[i] + z[64 * n : 64 * n + 64] + x[n // 2][:, 128 * ny : 128 * ny + 128]

    groups(one)
    for ny in range(2):
        src = sources(lambda k: fields[2 * k + ny], fields[40 + ny], fields[42 + ny], dt)
        for k in range(7):
            part[2 * k + ny] += src[k]


def interior(
    kappa, fields, part, z_near, z_far, near, far, a_rows, z_main, z_outer, z_inner, q1, pq1, pws, half,
    us, ws, el, cor,
):
    dt, scale = time_step, 0.5 * time_step
    kap = [block_kappa(kappa, t) for t in range(3)]
    from_left, from_right, to_left, to_right = [], [], [], []
    for t in range(3):
        for pair, one, two in ((sides(near[t], far[t]), from_left, from_right), (sides(z_near[t], z_far[t]), to_left, to_right)):
            one.append(pair[0])
            two.append(pair[1])
    pus, rhs, outer = [], [], []
    for n, side in enumerate((from_left, to_left, from_right, to_right)):
        u, w = block_velocity(side[2])
        w = w * (dt / first_part)
        if n % 2 == 0:
            pus.append(u * (dt / first_part))
            rhs.append(w)
        for t in range(3):
            kq = (kap[t] * (dt / second_part)) * side[t]
            el[64 * t : 64 * t + 64, 512 * n : 512 * n + 512] = across(kq, w * side[t])
    z = dot(el[...], z_outer[...])
    u, w = outer_tile(*pus), outer_tile(*rhs)
    pws[...] = w
    outer = [outer_tile(from_left[t], from_right[t]) for t in range(3)]
    rhs = []
    for t in range(3):
        kq = (kap[t] * (dt / second_part)) * outer[t]
        el[64 * t : 64 * t + 64, 0:512] = across(kq, w * outer[t])
        rhs.append(down_rows(kq, u * outer[t]))
    cor[...] = dot(el[:, 0:512], z_inner[...])
    x = dot(a_rows[...], jnp.concatenate(rhs, axis=1))
    for t in range(3):
        pq1[t] = outer[t] + x[:, 128 * t : 128 * t + 128] + z[64 * t : 64 * t + 64]
    for t, src in enumerate(block_sources(outer, dt)):
        pq1[t] += src
    for p in range(9):
        for i, field, ny, t, b in planes(p):
            q1[i] = part[i] + unpack(cor[64 * t : 64 * t + 64, :], b)

    plane_velocities(fields, us, ws, scale)
    for t in range(3):
        e = pq1[t, 8:56, :]
        el[48 * t : 48 * t + 48, 0:512] = across((kap[t] * (scale / second_part)) * e, (0.5 * pws[8:56, :]) * e)
    cor[0:144, :] = dot(el[0:144, 0:512], z_inner[...])

    def two(p):
        lhs, rhs = [], []
        for i, field, ny, t, b in planes(p):
            v = q1[i]
            kq = (kappa[field] * (scale / second_part)) * v
            mid = v[8:56]
            lhs.append(across(kq[8:56], ws[ny, 8:56, :] * mid))
            rhs.append(down_rows(kq, us[ny] * v))
        z = dot(jnp.concatenate(lhs, axis=0), z_main[...])
        x = [dot(a_rows[8:56, :], jnp.concatenate(rhs[c : c + 2], axis=1)) for c in (0, 2)]
        for n, (i, field, ny, t, b) in enumerate(planes(p)):
            half[i, 8:56, :] = (
                0.5 * (fields[i, 8:56, :] + q1[i, 8:56, :])
                + z[48 * n : 48 * n + 48]
                + x[n // 2][:, 128 * ny : 128 * ny + 128]
                + unpack(cor[48 * t : 48 * t + 48, :], b)
            )

    for p in range(9):
        two(p)
    for ny in range(2):
        src = sources(
            lambda k: q1[2 * k + ny, 8:56, :], fields[40 + ny, 8:56, :], fields[42 + ny, 8:56, :], scale
        )
        for k in range(7):
            half[2 * k + ny, 8:56, :] += src[k]


def edges(
    kappa, fields, q1, pq1, pws, half, first, second, first_corner, second_corner,
    a_one, a_two, a_corner, z_main, z_inner, out_mom, out_sca,
    s1h, s1a, lz, done, sems,
):
    outs = [(out_mom, 0, 12), (out_sca, 12, 24)]
    copies = [
        pltpu.make_async_copy(
            half.at[pl.ds(at, size), pl.ds(8, 48)], out.at[pl.ds(0, size), pl.ds(8, 48)], sems.at[n]
        )
        for n, (out, at, size) in enumerate(outs)
    ]
    for copy in copies:
        copy.start()
    dt, scale = time_step, 0.5 * time_step
    one, two = dt / first_part, scale / first_part
    front = lax.broadcasted_iota(jnp.int32, (8, 128), 0) < 4
    below_first = halves(1 - odd_of("gx"))
    pair = lambda *tiles: jnp.concatenate(tiles, axis=0)
    at_h = lambda a, b, i: jnp.where(below_first, a[i], b[i])
    at_o = lambda a, b, i: jnp.where(below_first, b[i], a[i])
    at_a = lambda ref, *i: jnp.where(front, ref[*i, 0:8, :], ref[*i, 56:64, :])
    at_b = lambda ref, *i: jnp.where(front, ref[*i, 56:64, :], ref[*i, 0:8, :])
    at_c = lambda ref, *i: jnp.where(front, ref[*i, 8:16, :], ref[*i, 48:56, :])
    other_h = lambda a, b, i: pltpu.roll(at_o(a, b, i), 4, 0)

    uh = [at_h(first, second, 36 + ny) for ny in range(2)]
    uo = [at_o(first, second, 36 + ny) for ny in range(2)]
    wh = [at_h(first, second, 38) * one, other_h(first, second, 38) * one]
    ua = [at_a(fields, 36 + ny) for ny in range(2)]
    u_ho = [pair(uh[ny], uo[ny]) * one for ny in range(2)]
    u_hc = [pair(uh[ny], at_c(fields, 36 + ny)) * two for ny in range(2)]
    u_ab = [pair(ua[ny], at_b(fields, 36 + ny)) * two for ny in range(2)]
    w_ab = [pair(at_a(fields, 38 + ny), at_b(fields, 38 + ny)) * two for ny in range(2)]

    kap = [block_kappa(kappa, t) for t in range(3)]
    outer = [
        at_h(first_corner, second_corner, 0),
        other_h(first_corner, second_corner, 0),
        at_h(first_corner, second_corner, 1),
    ]
    u, w = block_velocity(outer[2])
    u, w = u * one, w * one
    rhs, kqs, gs = [], [], []
    for t in range(3):
        kq = (kap[t] * (dt / second_part)) * outer[t]
        rhs.append(pair(*split(pair(kq, u * outer[t]))))
        kqs.append(kq)
        gs.append(w * outer[t])
    zero = jnp.zeros((8, 128), F32)
    cor_h = dot(across(pair(*kqs, zero), pair(*gs, zero)), z_inner[...])
    x = dot(a_corner[...], jnp.concatenate(rhs, axis=1))
    lhs = []
    for t in range(3):
        e = pair(at_a(pq1, t) + x[0:8, 128 * t : 128 * t + 128], at_b(pq1, t))
        w = pair(at_a(pws), at_b(pws)) * 0.5
        lhs.append(across((kap[t] * (scale / second_part)) * e, w * e))
    cor_ab = dot(pair(*lhs), z_inner[...])

    hs = lambda i: at_h(first, second, i)
    for field in range(18):
        k = kappa[field] * (dt / second_part)
        h = [hs(2 * field + ny) for ny in range(2)]
        lz[16 * field : 16 * field + 16, :] = across(pair(k * h[0], k * h[1]), pair(wh[0] * h[0], wh[1] * h[1]))
    z = dot(lz[...], z_main[...])
    for p in range(9):
        rhs = []
        for i, field, ny, t, b in planes(p):
            k = kappa[field] * (dt / second_part)
            ho, a = pair(hs(i), at_o(first, second, i)), at_a(fields, i)
            rhs.append(down_rows(k * ho, u_ho[ny] * ho))
            rhs[-1] = pair(rhs[-1], *split(pair(k * a, (ua[ny] * one) * a)))
        x = dot(a_one[...], jnp.concatenate(rhs, axis=1))
        for n, (i, field, ny, t, b) in enumerate(planes(p)):
            at = 16 * field + 8 * ny
            x_i = x[:, 128 * n : 128 * n + 128]
            s1h[i] = hs(i) + x_i[0:8] + z[at : at + 8] + unpack(cor_h[8 * t : 8 * t + 8], b)
            s1a[i] = at_a(q1, i) + x_i[8:16]
    for ny in range(2):
        src = sources(
            lambda k: hs(2 * k + ny), at_h(first, second, 39 + ny), other_h(first, second, 39 + ny), dt
        )
        for k in range(7):
            s1h[2 * k + ny] += src[k]

    for p in range(9):
        lhs, rhs = [], []
        for i, field, ny, t, b in planes(p):
            k = kappa[field] * (scale / second_part)
            ab, hc = pair(s1a[i], at_b(q1, i)), pair(s1h[i], at_c(q1, i))
            kq = split(k * ab)
            lhs.append(jnp.concatenate([*kq, *split(w_ab[ny] * ab)], axis=1))
            rhs.append(pair(*kq, *split(u_ab[ny] * ab), down_rows(k * hc, u_hc[ny] * hc)))
        z = dot(pair(*lhs), z_main[...])
        x = dot(a_two[...], jnp.concatenate(rhs, axis=1))
        for n, (i, field, ny, t, b) in enumerate(planes(p)):
            own = pair(at_a(fields, i) + s1a[i], at_b(fields, i) + at_b(q1, i))
            done[i] = (
                0.5 * own
                + z[16 * n : 16 * n + 16]
                + x[:, 128 * n : 128 * n + 128]
                + unpack(cor_ab[16 * t : 16 * t + 16], b)
            )
    for ny in range(2):
        nucl = pair(at_a(fields, 40 + ny), at_b(fields, 40 + ny))
        grow = pair(at_a(fields, 42 + ny), at_b(fields, 42 + ny))
        src = sources(lambda k: pair(s1a[2 * k + ny], at_b(q1, 2 * k + ny)), nucl, grow, scale)
        for k in range(7):
            done[2 * k + ny] += src[k]
    for i in range(36):
        a, b = done[i, 0:8, :], done[i, 8:16, :]
        done[i, 0:8, :] = jnp.where(front, a, b)
        done[i, 8:16, :] = jnp.where(front, b, a)
    last = [
        pltpu.make_async_copy(
            done.at[pl.ds(at, size), pl.ds(8 * side, 8)],
            out.at[pl.ds(0, size), pl.ds(56 * side, 8)],
            sems.at[2 + 2 * n + side],
        )
        for n, (out, at, size) in enumerate(outs)
        for side in range(2)
    ]
    for copy in last:
        copy.start()
    for copy in copies + last:
        copy.wait()


def call(kernel, outs, cost, mib=24, **kw):
    return pl.pallas_call(
        kernel,
        out_shape=[jax.ShapeDtypeStruct(o, F32) for o in outs],
        cost_estimate=pl.CostEstimate(flops=cost, bytes_accessed=cost // 4, transcendentals=0),
        compiler_params=pltpu.CompilerParams(vmem_limit_bytes=mib * 2**20),
        **kw,
    )


def swap(value, axis, far):
    peers = lax.axis_size(axis)
    other = lambda i: (((i + far) ^ 1) - far) % peers
    return lax.ppermute(value, axis, [(i, other(i)) for i in range(peers)])


def body(moments, scalars, velocity, diffusivity, nucleation, growth):
    vmem = pl.BlockSpec(memory_space=pltpu.VMEM)
    smem = pl.BlockSpec(memory_space=pltpu.SMEM)
    hbm = pl.BlockSpec(memory_space=pltpu.HBM)
    tiles = lambda *lead: pltpu.VMEM(lead + (128,), F32)
    flat = [
        pltpu.with_memory_space_constraint(x.reshape(-1, 64, 128), pltpu.HBM)
        for x in (moments, scalars, velocity, nucleation, growth)
    ]
    a_rows, a_one, a_two, a_corner, z_main, z_outer, z_inner = (jnp.asarray(m) for m in matrices())

    z_far, z_near, fields = call(
        pack_z,
        [(3, 64, 128), (3, 64, 128), (44, 64, 128)],
        10**6,
        in_specs=[hbm] * 5,
        out_specs=[vmem] * 3,
        scratch_shapes=[pltpu.SemaphoreType.DMA((10,))],
    )(*flat)
    far = swap(z_far, "gz", 1)
    x_first, x_second, z_near = call(x_messages, [(41, 8, 128), (41, 8, 128), (3, 64, 128)], 10**5)(fields, z_near)
    near = swap(z_near, "gz", 0)
    (part,) = call(
        first_stage,
        [(36, 64, 128)],
        10**7,
        in_specs=[smem] + [vmem] * 3,
        scratch_shapes=[tiles(2, 64), tiles(2, 64)],
    )(diffusivity, fields, a_rows, z_main)
    second = swap(x_second, "gx", 1)
    first = swap(x_first, "gx", 0)
    c_first, c_second = call(corners, [(2, 8, 128)] * 2, 10**6)(near, far, part)
    second_corner = swap(c_second, "gx", 1)
    first_corner = swap(c_first, "gx", 0)
    q1, pq1, pws, half = call(
        interior,
        [(36, 64, 128), (3, 64, 128), (64, 128), (36, 64, 128)],
        10 * 10**8,
        in_specs=[smem] + [vmem] * 10,
        scratch_shapes=[tiles(2, 64), tiles(2, 64), pltpu.VMEM((192, 2048), BF16), tiles(192)],
    )(diffusivity, fields, part, z_near, z_far, near, far, a_rows, z_main, z_outer, z_inner)
    out_mom, out_sca = call(
        edges,
        [(12, 64, 128), (24, 64, 128)],
        10**8,
        in_specs=[smem] + [vmem] * 14,
        out_specs=[hbm] * 2,
        scratch_shapes=[
            tiles(36, 8), tiles(36, 8), pltpu.VMEM((288, 512), BF16), tiles(36, 16), pltpu.SemaphoreType.DMA((6,)),
        ],
    )(
        diffusivity, fields, q1, pq1, pws, half, first, second, first_corner, second_corner,
        a_one, a_two, a_corner, z_main, z_inner,
    )
    return out_mom.reshape(moments.shape), out_sca.reshape(scalars.shape)


def solution(mesh):
    return jax.shard_map(
        body,
        mesh=mesh,
        in_specs=(
            P(None, None, "gx", "gz"),
            P(None, None, "gx", "gz"),
            P(None, None, "gx", "gz"),
            P(),
            P(None, "gx", "gz"),
            P(None, "gx", "gz"),
        ),
        out_specs=(P(None, None, "gx", "gz"), P(None, None, "gx", "gz")),
        check_vma=False,
    )
```

time: 26.8 us -> 26.3 us (0.981)
  Pallas kernels: 10.7 us -> 9.54 us
  waiting for transfers between devices: 0.09 us -> 0.88 us
    pallas_call x2, Pallas kernels: 5.7 us -> 4.62 us  [the longest x1 2.68 us: body(): call(interior, [(36, 64, 128), (3, 64, 128), (64, 128), (36, 64, 128)], 1...]
    ppermute x6, waiting for transfers between devices: 0.09 us -> 0.88 us  [swap(): return lax.ppermute(value, axis, [(i, other(i)) for i in range(peers)])]
  transfers between devices with their start and end apart: 6 -> 6, of which waited for: 1 -> 1; matrix products, arithmetic and copies ran while one was open for 0% -> 0% of each run, Pallas kernels for 21% -> 18%
where the time goes in v4:
time: 26.3 us; the launch traced here: 26.2 us
  starting transfers between devices  14.9 us (57%)
  Pallas kernels  9.54 us (36%)
  waiting for transfers between devices  0.88 us (3%)
  between operations  0.81 us (3%)
    ppermute x6, starting transfers between devices, swap(): return lax.ppermute(value, axis, [(i, other(i)) for i in range(peers)])  14.9 us
    pallas_call x1, Pallas kernels, body(): call(edges, [(12, 64, 128), (24, 64, 128)], 10 ** 8, in_specs=[smem] + [v...  2.69 us
    pallas_call x1, Pallas kernels, body(): call(interior, [(36, 64, 128), (3, 64, 128), (64, 128), (36, 64, 128)], 1...  2.68 us
    pallas_call x1, Pallas kernels, body(): call(pack_z, [(3, 64, 128), (3, 64, 128), (44, 64, 128)], 10 ** 6, in_spe...  2.14 us
    pallas_call x1, Pallas kernels, body(): call(first_stage, [(36, 64, 128)], 10 ** 7, in_specs=[smem] + [vmem] * 3,...  1.93 us
    ppermute x6, waiting for transfers between devices, swap(): return lax.ppermute(value, axis, [(i, other(i)) for i in range(peers)])  0.88 us
  transfers between devices with their start and end apart: 6, of which 1 were waited for; matrix products, arithmetic and copies ran while one was open for 0% of the time, Pallas kernels for 18%

profile of v4, /device:TPU:25, one launch (start us, length us, event | category | flops | bytes accessed | tf_op | source)
XLA Modules:
  0.0 26.2 jit_solution(11255421894042086901)
XLA Ops:
  0.6 0.0 copy-start
  0.6 0.0 copy-start.3
  0.7 2.1 %shard_map.140 = (f32[3,64,128]{2,1,0:T(8,128)S(1)}, f32[3,64,128]{2,1,0:T(8,128)S(1)}, f32[44,64,128]{2,1,0:T(8,128)S(1)}) custom-call(f32[12,64,128]{2,1,0:T(8,128)} %bitcast.6, f32[24,64,128]{2,1,0:T(8,128)} %bitcast.5, f32[4,64,128]{2,1,0:T(8,128)} %bitcast.7, f32[2,64,128]{2,1,0:T(8,128)} %nuc.1, f32[2,64,128]{2,1,0:T(8,128)} %gro.1), custom_call_target="tpu_custom_call" | custom-call | flops 1000000 | bytes 250000 | tf_op jit(solution)/shard_map/pallas_call | solution.py:503
  2.8 0.1 shard_map.142
  2.9 0.8 %collective-permute-start = (f32[3,64,128]{2,1,0:T(8,128)S(1)}, f32[3,64,128]{2,1,0:T(8,128)S(1)}, u32[]{:S(2)}, u32[]{:S(2)}) collective-permute-start(f32[3,64,128]{2,1,0:T(8,128)S(1)} %get-tuple-element.18.z_near), channel_id=1, source_target_pairs={{0,1},{1,0},{2,3},{3,2},{4,5},{5,4},{6,7},{7,6},{8,9},{9,8},{10,11... | collective-permute-start | bytes 294920 | tf_op jit(solution)/shard_map/ppermute | solution.py:489
  3.7 2.4 %collective-permute-start.1 = (f32[3,64,128]{2,1,0:T(8,128)S(1)}, f32[3,64,128]{2,1,0:T(8,128)S(1)}, u32[]{:S(2)}, u32[]{:S(2)}) collective-permute-start(f32[3,64,128]{2,1,0:T(8,128)S(1)} %get-tuple-element.19.z_far), channel_id=1, source_target_pairs={{0,15},{1,2},{2,1},{3,4},{4,3},{5,6},{6,5},{7,8},{8,7},{9,10},{10,... | collective-permute-start | bytes 294920 | tf_op jit(solution)/shard_map/ppermute | solution.py:489
  6.0 0.3 %collective-permute-start.2 = (f32[41,8,128]{2,1,0:T(8,128)S(1)}, f32[41,8,128]{2,1,0:T(8,128)S(1)}, u32[]{:S(2)}, u32[]{:S(2)}) collective-permute-start(f32[41,8,128]{2,1,0:T(8,128)S(1)} %get-tuple-element.24), channel_id=1, source_target_pairs={{0,16},{16,0},{32,48},{48,32},{64,80},{80,64},{96,112},{112,96},{1... | collective-permute-start | bytes 503816 | tf_op jit(solution)/shard_map/ppermute | solution.py:489
  6.4 6.4 %collective-permute-start.3 = (f32[41,8,128]{2,1,0:T(8,128)S(1)}, f32[41,8,128]{2,1,0:T(8,128)S(1)}, u32[]{:S(2)}, u32[]{:S(2)}) collective-permute-start(f32[41,8,128]{2,1,0:T(8,128)S(1)} %get-tuple-element.25), channel_id=1, source_target_pairs={{0,240},{16,32},{32,16},{48,64},{64,48},{80,96},{96,80},{112,128},... | collective-permute-start | bytes 503816 | tf_op jit(solution)/shard_map/ppermute | solution.py:489
  12.8 1.9 %shard_map.141.part = f32[36,64,128]{2,1,0:T(8,128)S(1)} custom-call(f32[18]{0:T(128)S(1)} %copy-done.4, f32[44,64,128]{2,1,0:T(8,128)S(1)} %get-tuple-element.16.fields, bf16[64,256]{1,0:T(8,128)(2,1)S(1)} %copy-done.3, bf16[512,128]{1,0:T(8,128)(2,1)S(1)} %copy-done), custom_call_target="tpu_custom_call" | custom-call | flops 10000000 | bytes 2500000 | tf_op jit(solution)/shard_map/pallas_call | solution.py:514
  14.7 0.0 copy-start.1
  14.8 0.0 copy-start.2
  14.8 0.0 collective-permute-done.near
  14.8 0.9 %collective-permute-done.1.far = f32[3,64,128]{2,1,0:T(8,128)S(1)} collective-permute-done((f32[3,64,128]{2,1,0:T(8,128)S(1)}, f32[3,64,128]{2,1,0:T(8,128)S(1)}, u32[]{:S(2)}, u32[]{:S(2)}) %collective-permute-start.1) | collective-permute-done | bytes 98336 | tf_op jit(solution)/shard_map/ppermute | solution.py:489
  15.7 0.1 collective-permute-start.4
  15.8 0.0 copy-start.5
  15.8 0.0 copy-start.6
  15.8 0.0 copy-start.7
  15.8 4.9 %collective-permute-start.5 = (f32[2,8,128]{2,1,0:T(8,128)S(1)}, f32[2,8,128]{2,1,0:T(8,128)S(1)}, u32[]{:S(2)}, u32[]{:S(2)}) collective-permute-start(f32[2,8,128]{2,1,0:T(8,128)S(1)} %get-tuple-element.27), channel_id=1, source_target_pairs={{0,240},{16,32},{32,16},{48,64},{64,48},{80,96},{96,80},{112,128},... | collective-permute-start | bytes 24584 | tf_op jit(solution)/shard_map/ppermute | solution.py:489
  20.8 2.7 %shard_map.143 = (f32[36,64,128]{2,1,0:T(8,128)S(1)}, f32[3,64,128]{2,1,0:T(8,128)S(1)}, f32[64,128]{1,0:T(8,128)S(1)}, f32[36,64,128]{2,1,0:T(8,128)S(1)}) custom-call(f32[18]{0:T(128)S(1)} %copy-done.4, f32[44,64,128]{2,1,0:T(8,128)S(1)} %get-tuple-element.16.fields, f32[36,64,128]{2,1,0:T(8,128)S(1)} %shard_map.141.part, ...), custom_call_target="tpu_custom_call" | custom-call | flops 1000000000 | bytes 250000000 | tf_op jit(solution)/shard_map/pallas_call | solution.py:526
  23.5 0.0 collective-permute-done.4.first_corner
  23.5 0.0 collective-permute-done.5.second_corner
  23.5 0.0 collective-permute-done.2.first
  23.5 0.0 collective-permute-done.3.second
  23.5 2.7 %shard_map.145 = (f32[12,64,128]{2,1,0:T(8,128)}, f32[24,64,128]{2,1,0:T(8,128)}) custom-call(f32[18]{0:T(128)S(1)} %copy-done.4, f32[44,64,128]{2,1,0:T(8,128)S(1)} %get-tuple-element.16.fields, f32[36,64,128]{2,1,0:T(8,128)S(1)} %get-tuple-element.20.q1, f32[3,64,128]{2,1,0:T(8,128)S(1)} %get-tuple-element.21.pq1, f32[64,128]{1,0:T(8,128)S(1)} %get-tuple-element.22.pws, ...), custom_call_target="tpu_custom_call" | custom-call | flops 100000000 | bytes 25000000 | tf_op jit(solution)/shard_map/pallas_call | solution.py:533
  (10 shorter events, 0.0 us)
Async XLA Ops:
  0.6 12.2 %copy-start = (bf16[512,128]{1,0:T(8,128)(2,1)S(1)}, bf16[512,128]{1,0:T(8,128)(2,1)}, u32[]{:S(2)}) copy-start(bf16[512,128]{1,0:T(8,128)(2,1)} %constant.18.clone.z_main) | copy-start | bytes 393220
  0.6 12.2 %copy-start.3 = (bf16[64,256]{1,0:T(8,128)(2,1)S(1)}, bf16[64,256]{1,0:T(8,128)(2,1)}, u32[]{:S(2)}) copy-start(bf16[64,256]{1,0:T(8,128)(2,1)} %constant.14.clone.a_rows) | copy-start | bytes 98308
  0.7 12.2 %copy-start.4 = (f32[18]{0:T(128)S(1)}, f32[18]{0:T(128)}, u32[]{:S(2)}) copy-start(f32[18]{0:T(128)} %kappa.5) | copy-start | bytes 220
  2.9 11.9 %collective-permute-start = (f32[3,64,128]{2,1,0:T(8,128)S(1)}, f32[3,64,128]{2,1,0:T(8,128)S(1)}, u32[]{:S(2)}, u32[]{:S(2)}) collective-permute-start(f32[3,64,128]{2,1,0:T(8,128)S(1)} %get-tuple-element.18.z_near), channel_id=1, source_target_pairs={{0,1},{1,0},{2,3},{3,2},{4,5},{5,4},{6,7},{7,6},{8,9},{9,8},{10,11... | collective-permute-start | bytes 294920 | tf_op jit(solution)/shard_map/ppermute | solution.py:489
  3.7 12.0 %collective-permute-start.1 = (f32[3,64,128]{2,1,0:T(8,128)S(1)}, f32[3,64,128]{2,1,0:T(8,128)S(1)}, u32[]{:S(2)}, u32[]{:S(2)}) collective-permute-start(f32[3,64,128]{2,1,0:T(8,128)S(1)} %get-tuple-element.19.z_far), channel_id=1, source_target_pairs={{0,15},{1,2},{2,1},{3,4},{4,3},{5,6},{6,5},{7,8},{8,7},{9,10},{10,... | collective-permute-start | bytes 294920 | tf_op jit(solution)/shard_map/ppermute | solution.py:489
  6.0 17.4 %collective-permute-start.2 = (f32[41,8,128]{2,1,0:T(8,128)S(1)}, f32[41,8,128]{2,1,0:T(8,128)S(1)}, u32[]{:S(2)}, u32[]{:S(2)}) collective-permute-start(f32[41,8,128]{2,1,0:T(8,128)S(1)} %get-tuple-element.24), channel_id=1, source_target_pairs={{0,16},{16,0},{32,48},{48,32},{64,80},{80,64},{96,112},{112,96},{1... | collective-permute-start | bytes 503816 | tf_op jit(solution)/shard_map/ppermute | solution.py:489
  6.4 17.1 %collective-permute-start.3 = (f32[41,8,128]{2,1,0:T(8,128)S(1)}, f32[41,8,128]{2,1,0:T(8,128)S(1)}, u32[]{:S(2)}, u32[]{:S(2)}) collective-permute-start(f32[41,8,128]{2,1,0:T(8,128)S(1)} %get-tuple-element.25), channel_id=1, source_target_pairs={{0,240},{16,32},{32,16},{48,64},{64,48},{80,96},{96,80},{112,128},... | collective-permute-start | bytes 503816 | tf_op jit(solution)/shard_map/ppermute | solution.py:489
  14.7 6.0 %copy-start.1 = (bf16[512,128]{1,0:T(8,128)(2,1)S(1)}, bf16[512,128]{1,0:T(8,128)(2,1)}, u32[]{:S(2)}) copy-start(bf16[512,128]{1,0:T(8,128)(2,1)} %constant.20.clone.z_inner) | copy-start | bytes 393220
  14.8 6.0 %copy-start.2 = (bf16[2048,128]{1,0:T(8,128)(2,1)S(1)}, bf16[2048,128]{1,0:T(8,128)(2,1)}, u32[]{:S(2)}) copy-start(bf16[2048,128]{1,0:T(8,128)(2,1)} %constant.19.clone.z_outer) | copy-start | bytes 1572868
  15.7 7.8 %collective-permute-start.4 = (f32[2,8,128]{2,1,0:T(8,128)S(1)}, f32[2,8,128]{2,1,0:T(8,128)S(1)}, u32[]{:S(2)}, u32[]{:S(2)}) collective-permute-start(f32[2,8,128]{2,1,0:T(8,128)S(1)} %get-tuple-element.26), channel_id=1, source_target_pairs={{0,16},{16,0},{32,48},{48,32},{64,80},{80,64},{96,112},{112,96},{1... | collective-permute-start | bytes 24584 | tf_op jit(solution)/shard_map/ppermute | solution.py:489
  15.8 7.7 %copy-start.5 = (bf16[16,96]{1,0:T(8,128)(2,1)S(1)}, bf16[16,96]{1,0:T(8,128)(2,1)}, u32[]{:S(2)}) copy-start(bf16[16,96]{1,0:T(8,128)(2,1)} %constant.15.clone.a_one) | copy-start | bytes 9220
  15.8 7.7 %copy-start.6 = (bf16[16,128]{1,0:T(8,128)(2,1)S(1)}, bf16[16,128]{1,0:T(8,128)(2,1)}, u32[]{:S(2)}) copy-start(bf16[16,128]{1,0:T(8,128)(2,1)} %constant.16.clone.a_two) | copy-start | bytes 12292
  15.8 7.7 %copy-start.7 = (bf16[16,32]{1,0:T(8,128)(2,1)S(1)}, bf16[16,32]{1,0:T(8,128)(2,1)}, u32[]{:S(2)}) copy-start(bf16[16,32]{1,0:T(8,128)(2,1)} %constant.17.clone.a_corner) | copy-start | bytes 3076
  15.8 7.7 %collective-permute-start.5 = (f32[2,8,128]{2,1,0:T(8,128)S(1)}, f32[2,8,128]{2,1,0:T(8,128)S(1)}, u32[]{:S(2)}, u32[]{:S(2)}) collective-permute-start(f32[2,8,128]{2,1,0:T(8,128)S(1)} %get-tuple-element.27), channel_id=1, source_target_pairs={{0,240},{16,32},{32,16},{48,64},{64,48},{80,96},{96,80},{112,128},... | collective-permute-start | bytes 24584 | tf_op jit(solution)/shard_map/ppermute | solution.py:489

commit v5 on v4

--- a/solution.py
+++ b/solution.py
@@ -346,7 +346,7 @@
 
 
 def edges(
-    kappa, fields, q1, pq1, pws, half, first, second, first_corner, second_corner,
+    kappa, fields, q1, pq1, pws, half, first, second, second_corner, first_corner,
     a_one, a_two, a_corner, z_main, z_inner, out_mom, out_sca,
     s1h, s1a, lz, done, sems,
 ):
@@ -430,7 +430,24 @@
         for k in range(7):
             s1h[2 * k + ny] += src[k]
 
+    last = [
+        pltpu.make_async_copy(
+            done.at[pl.ds(at, size), pl.ds(8 * side, 8)],
+            out.at[pl.ds(0, size), pl.ds(56 * side, 8)],
+            sems.at[2 + 2 * n + side],
+        )
+        for n, (out, at, size) in enumerate(outs)
+        for side in range(2)
+    ]
+    src = []
+    for ny in range(2):
+        nucl = pair(at_a(fields, 40 + ny), at_b(fields, 40 + ny))
+        grow = pair(at_a(fields, 42 + ny), at_b(fields, 42 + ny))
+        src.append(sources(lambda k: pair(s1a[2 * k + ny], at_b(q1, 2 * k + ny)), nucl, grow, scale))
     for p in range(9):
+        if p == 6:
+            for copy in last[:2]:
+                copy.start()
         lhs, rhs = [], []
         for i, field, ny, t, b in planes(p):
             k = kappa[field] * (scale / second_part)
@@ -442,32 +459,17 @@
         x = dot(a_two[...], jnp.concatenate(rhs, axis=1))
         for n, (i, field, ny, t, b) in enumerate(planes(p)):
             own = pair(at_a(fields, i) + s1a[i], at_b(fields, i) + at_b(q1, i))
-            done[i] = (
+            new = (
                 0.5 * own
                 + z[16 * n : 16 * n + 16]
                 + x[:, 128 * n : 128 * n + 128]
                 + unpack(cor_ab[16 * t : 16 * t + 16], b)
             )
-    for ny in range(2):
-        nucl = pair(at_a(fields, 40 + ny), at_b(fields, 40 + ny))
-        grow = pair(at_a(fields, 42 + ny), at_b(fields, 42 + ny))
-        src = sources(lambda k: pair(s1a[2 * k + ny], at_b(q1, 2 * k + ny)), nucl, grow, scale)
-        for k in range(7):
-            done[2 * k + ny] += src[k]
-    for i in range(36):
-        a, b = done[i, 0:8, :], done[i, 8:16, :]
-        done[i, 0:8, :] = jnp.where(front, a, b)
-        done[i, 8:16, :] = jnp.where(front, b, a)
-    last = [
-        pltpu.make_async_copy(
-            done.at[pl.ds(at, size), pl.ds(8 * side, 8)],
-            out.at[pl.ds(0, size), pl.ds(56 * side, 8)],
-            sems.at[2 + 2 * n + side],
-        )
-        for n, (out, at, size) in enumerate(outs)
-        for side in range(2)
-    ]
-    for copy in last:
+            if field < 7:
+                new = new + src[ny][field]
+            done[i, 0:8, :] = jnp.where(front, new[0:8], new[8:16])
+            done[i, 8:16, :] = jnp.where(front, new[8:16], new[0:8])
+    for copy in last[2:]:
         copy.start()
     for copy in copies + last:
         copy.wait()
@@ -540,7 +542,7 @@
             tiles(36, 8), tiles(36, 8), pltpu.VMEM((288, 512), BF16), tiles(36, 16), pltpu.SemaphoreType.DMA((6,)),
         ],
     )(
-        diffusivity, fields, q1, pq1, pws, half, first, second, first_corner, second_corner,
+        diffusivity, fields, q1, pq1, pws, half, first, second, second_corner, first_corner,
         a_one, a_two, a_corner, z_main, z_inner,
     )
     return out_mom.reshape(moments.shape), out_sca.reshape(scalars.shape)

time: 26.3 us -> 25.5 us (0.970)
  the two profiles are of different devices: /device:TPU:25 before, /device:TPU:121 now
where the time goes in v5:
time: 25.5 us; the launch traced here: 25.3 us
  starting transfers between devices  10.2 us (40%)
  Pallas kernels  9.43 us (37%)
  waiting for transfers between devices  4.83 us (19%)
  between operations  0.81 us (3%)
    ppermute x6, starting transfers between devices, swap(): return lax.ppermute(value, axis, [(i, other(i)) for i in range(peers)])  10.2 us
    ppermute x6, waiting for transfers between devices, swap(): return lax.ppermute(value, axis, [(i, other(i)) for i in range(peers)])  4.83 us
    pallas_call x1, Pallas kernels, body(): call(interior, [(36, 64, 128), (3, 64, 128), (64, 128), (36, 64, 128)], 1...  2.69 us
    pallas_call x1, Pallas kernels, body(): call(edges, [(12, 64, 128), (24, 64, 128)], 10 ** 8, in_specs=[smem] + [v...  2.59 us
    pallas_call x1, Pallas kernels, body(): call(pack_z, [(3, 64, 128), (3, 64, 128), (44, 64, 128)], 10 ** 6, in_spe...  2.14 us
    pallas_call x1, Pallas kernels, body(): call(first_stage, [(36, 64, 128)], 10 ** 7, in_specs=[smem] + [vmem] * 3,...  1.93 us
  transfers between devices with their start and end apart: 6, of which 1 were waited for; matrix products, arithmetic and copies ran while one was open for 0% of the time, Pallas kernels for 18%

profile of v5, /device:TPU:121, one launch (start us, length us, event | category | flops | bytes accessed | tf_op | source)
XLA Modules:
  0.0 25.3 jit_solution(17030324036714417449)
XLA Ops:
  0.6 0.0 copy-start
  0.6 0.0 copy-start.3
  0.7 2.1 %shard_map.140 = (f32[3,64,128]{2,1,0:T(8,128)S(1)}, f32[3,64,128]{2,1,0:T(8,128)S(1)}, f32[44,64,128]{2,1,0:T(8,128)S(1)}) custom-call(f32[12,64,128]{2,1,0:T(8,128)} %bitcast.6, f32[24,64,128]{2,1,0:T(8,128)} %bitcast.5, f32[4,64,128]{2,1,0:T(8,128)} %bitcast.7, f32[2,64,128]{2,1,0:T(8,128)} %nuc.1, f32[2,64,128]{2,1,0:T(8,128)} %gro.1), custom_call_target="tpu_custom_call" | custom-call | flops 1000000 | bytes 250000 | tf_op jit(solution)/shard_map/pallas_call | solution.py:505
  2.8 0.1 shard_map.142
  2.9 0.8 %collective-permute-start = (f32[3,64,128]{2,1,0:T(8,128)S(1)}, f32[3,64,128]{2,1,0:T(8,128)S(1)}, u32[]{:S(2)}, u32[]{:S(2)}) collective-permute-start(f32[3,64,128]{2,1,0:T(8,128)S(1)} %get-tuple-element.18.z_near), channel_id=1, source_target_pairs={{0,1},{1,0},{2,3},{3,2},{4,5},{5,4},{6,7},{7,6},{8,9},{9,8},{10,11... | collective-permute-start | bytes 294920 | tf_op jit(solution)/shard_map/ppermute | solution.py:491
  3.7 2.4 %collective-permute-start.1 = (f32[3,64,128]{2,1,0:T(8,128)S(1)}, f32[3,64,128]{2,1,0:T(8,128)S(1)}, u32[]{:S(2)}, u32[]{:S(2)}) collective-permute-start(f32[3,64,128]{2,1,0:T(8,128)S(1)} %get-tuple-element.19.z_far), channel_id=1, source_target_pairs={{0,15},{1,2},{2,1},{3,4},{4,3},{5,6},{6,5},{7,8},{8,7},{9,10},{10,... | collective-permute-start | bytes 294920 | tf_op jit(solution)/shard_map/ppermute | solution.py:491
  6.0 0.3 %collective-permute-start.2 = (f32[41,8,128]{2,1,0:T(8,128)S(1)}, f32[41,8,128]{2,1,0:T(8,128)S(1)}, u32[]{:S(2)}, u32[]{:S(2)}) collective-permute-start(f32[41,8,128]{2,1,0:T(8,128)S(1)} %get-tuple-element.24), channel_id=1, source_target_pairs={{0,16},{16,0},{32,48},{48,32},{64,80},{80,64},{96,112},{112,96},{1... | collective-permute-start | bytes 503816 | tf_op jit(solution)/shard_map/ppermute | solution.py:491
  6.4 0.7 %collective-permute-start.3 = (f32[41,8,128]{2,1,0:T(8,128)S(1)}, f32[41,8,128]{2,1,0:T(8,128)S(1)}, u32[]{:S(2)}, u32[]{:S(2)}) collective-permute-start(f32[41,8,128]{2,1,0:T(8,128)S(1)} %get-tuple-element.25), channel_id=1, source_target_pairs={{0,240},{16,32},{32,16},{48,64},{64,48},{80,96},{96,80},{112,128},... | collective-permute-start | bytes 503816 | tf_op jit(solution)/shard_map/ppermute | solution.py:491
  7.1 1.9 %shard_map.141.part = f32[36,64,128]{2,1,0:T(8,128)S(1)} custom-call(f32[18]{0:T(128)S(1)} %copy-done.4, f32[44,64,128]{2,1,0:T(8,128)S(1)} %get-tuple-element.16.fields, bf16[64,256]{1,0:T(8,128)(2,1)S(1)} %copy-done.3, bf16[512,128]{1,0:T(8,128)(2,1)S(1)} %copy-done), custom_call_target="tpu_custom_call" | custom-call | flops 10000000 | bytes 2500000 | tf_op jit(solution)/shard_map/pallas_call | solution.py:516
  9.0 0.0 copy-start.1
  9.0 0.0 copy-start.2
  9.0 0.0 collective-permute-done.near
  9.0 4.8 %collective-permute-done.1.far = f32[3,64,128]{2,1,0:T(8,128)S(1)} collective-permute-done((f32[3,64,128]{2,1,0:T(8,128)S(1)}, f32[3,64,128]{2,1,0:T(8,128)S(1)}, u32[]{:S(2)}, u32[]{:S(2)}) %collective-permute-start.1) | collective-permute-done | bytes 98336 | tf_op jit(solution)/shard_map/ppermute | solution.py:491
  13.9 0.1 collective-permute-start.4
  14.0 0.0 copy-start.5
  14.0 0.0 copy-start.6
  14.0 0.0 copy-start.7
  14.0 6.0 %collective-permute-start.5 = (f32[2,8,128]{2,1,0:T(8,128)S(1)}, f32[2,8,128]{2,1,0:T(8,128)S(1)}, u32[]{:S(2)}, u32[]{:S(2)}) collective-permute-start(f32[2,8,128]{2,1,0:T(8,128)S(1)} %get-tuple-element.27), channel_id=1, source_target_pairs={{0,16},{16,0},{32,48},{48,32},{64,80},{80,64},{96,112},{112,96},{1... | collective-permute-start | bytes 24584 | tf_op jit(solution)/shard_map/ppermute | solution.py:491
  20.0 2.7 %shard_map.143 = (f32[36,64,128]{2,1,0:T(8,128)S(1)}, f32[3,64,128]{2,1,0:T(8,128)S(1)}, f32[64,128]{1,0:T(8,128)S(1)}, f32[36,64,128]{2,1,0:T(8,128)S(1)}) custom-call(f32[18]{0:T(128)S(1)} %copy-done.4, f32[44,64,128]{2,1,0:T(8,128)S(1)} %get-tuple-element.16.fields, f32[36,64,128]{2,1,0:T(8,128)S(1)} %shard_map.141.part, ...), custom_call_target="tpu_custom_call" | custom-call | flops 1000000000 | bytes 250000000 | tf_op jit(solution)/shard_map/pallas_call | solution.py:528
  22.7 0.0 collective-permute-done.4.second_corner
  22.7 0.0 collective-permute-done.5.first_corner
  22.7 0.0 collective-permute-done.2.first
  22.7 0.0 collective-permute-done.3.second
  22.7 2.6 %shard_map.145 = (f32[12,64,128]{2,1,0:T(8,128)}, f32[24,64,128]{2,1,0:T(8,128)}) custom-call(f32[18]{0:T(128)S(1)} %copy-done.4, f32[44,64,128]{2,1,0:T(8,128)S(1)} %get-tuple-element.16.fields, f32[36,64,128]{2,1,0:T(8,128)S(1)} %get-tuple-element.20.q1, f32[3,64,128]{2,1,0:T(8,128)S(1)} %get-tuple-element.21.pq1, f32[64,128]{1,0:T(8,128)S(1)} %get-tuple-element.22.pws, ...), custom_call_target="tpu_custom_call" | custom-call | flops 100000000 | bytes 25000000 | tf_op jit(solution)/shard_map/pallas_call | solution.py:535
  (10 shorter events, 0.0 us)
Async XLA Ops:
  0.6 6.4 %copy-start = (bf16[512,128]{1,0:T(8,128)(2,1)S(1)}, bf16[512,128]{1,0:T(8,128)(2,1)}, u32[]{:S(2)}) copy-start(bf16[512,128]{1,0:T(8,128)(2,1)} %constant.18.clone.z_main) | copy-start | bytes 393220
  0.6 6.4 %copy-start.3 = (bf16[64,256]{1,0:T(8,128)(2,1)S(1)}, bf16[64,256]{1,0:T(8,128)(2,1)}, u32[]{:S(2)}) copy-start(bf16[64,256]{1,0:T(8,128)(2,1)} %constant.14.clone.a_rows) | copy-start | bytes 98308
  0.7 6.4 %copy-start.4 = (f32[18]{0:T(128)S(1)}, f32[18]{0:T(128)}, u32[]{:S(2)}) copy-start(f32[18]{0:T(128)} %kappa.5) | copy-start | bytes 220
  2.9 6.1 %collective-permute-start = (f32[3,64,128]{2,1,0:T(8,128)S(1)}, f32[3,64,128]{2,1,0:T(8,128)S(1)}, u32[]{:S(2)}, u32[]{:S(2)}) collective-permute-start(f32[3,64,128]{2,1,0:T(8,128)S(1)} %get-tuple-element.18.z_near), channel_id=1, source_target_pairs={{0,1},{1,0},{2,3},{3,2},{4,5},{5,4},{6,7},{7,6},{8,9},{9,8},{10,11... | collective-permute-start | bytes 294920 | tf_op jit(solution)/shard_map/ppermute | solution.py:491
  3.7 10.2 %collective-permute-start.1 = (f32[3,64,128]{2,1,0:T(8,128)S(1)}, f32[3,64,128]{2,1,0:T(8,128)S(1)}, u32[]{:S(2)}, u32[]{:S(2)}) collective-permute-start(f32[3,64,128]{2,1,0:T(8,128)S(1)} %get-tuple-element.19.z_far), channel_id=1, source_target_pairs={{0,15},{1,2},{2,1},{3,4},{4,3},{5,6},{6,5},{7,8},{8,7},{9,10},{10,... | collective-permute-start | bytes 294920 | tf_op jit(solution)/shard_map/ppermute | solution.py:491
  6.0 16.7 %collective-permute-start.2 = (f32[41,8,128]{2,1,0:T(8,128)S(1)}, f32[41,8,128]{2,1,0:T(8,128)S(1)}, u32[]{:S(2)}, u32[]{:S(2)}) collective-permute-start(f32[41,8,128]{2,1,0:T(8,128)S(1)} %get-tuple-element.24), channel_id=1, source_target_pairs={{0,16},{16,0},{32,48},{48,32},{64,80},{80,64},{96,112},{112,96},{1... | collective-permute-start | bytes 503816 | tf_op jit(solution)/shard_map/ppermute | solution.py:491
  6.4 16.4 %collective-permute-start.3 = (f32[41,8,128]{2,1,0:T(8,128)S(1)}, f32[41,8,128]{2,1,0:T(8,128)S(1)}, u32[]{:S(2)}, u32[]{:S(2)}) collective-permute-start(f32[41,8,128]{2,1,0:T(8,128)S(1)} %get-tuple-element.25), channel_id=1, source_target_pairs={{0,240},{16,32},{32,16},{48,64},{64,48},{80,96},{96,80},{112,128},... | collective-permute-start | bytes 503816 | tf_op jit(solution)/shard_map/ppermute | solution.py:491
  9.0 11.0 %copy-start.1 = (bf16[512,128]{1,0:T(8,128)(2,1)S(1)}, bf16[512,128]{1,0:T(8,128)(2,1)}, u32[]{:S(2)}) copy-start(bf16[512,128]{1,0:T(8,128)(2,1)} %constant.20.clone.z_inner) | copy-start | bytes 393220
  9.0 11.0 %copy-start.2 = (bf16[2048,128]{1,0:T(8,128)(2,1)S(1)}, bf16[2048,128]{1,0:T(8,128)(2,1)}, u32[]{:S(2)}) copy-start(bf16[2048,128]{1,0:T(8,128)(2,1)} %constant.19.clone.z_outer) | copy-start | bytes 1572868
  13.9 8.8 %collective-permute-start.4 = (f32[2,8,128]{2,1,0:T(8,128)S(1)}, f32[2,8,128]{2,1,0:T(8,128)S(1)}, u32[]{:S(2)}, u32[]{:S(2)}) collective-permute-start(f32[2,8,128]{2,1,0:T(8,128)S(1)} %get-tuple-element.26), channel_id=1, source_target_pairs={{0,240},{16,32},{32,16},{48,64},{64,48},{80,96},{96,80},{112,128},... | collective-permute-start | bytes 24584 | tf_op jit(solution)/shard_map/ppermute | solution.py:491
  14.0 8.7 %copy-start.5 = (bf16[16,96]{1,0:T(8,128)(2,1)S(1)}, bf16[16,96]{1,0:T(8,128)(2,1)}, u32[]{:S(2)}) copy-start(bf16[16,96]{1,0:T(8,128)(2,1)} %constant.15.clone.a_one) | copy-start | bytes 9220
  14.0 8.7 %copy-start.6 = (bf16[16,128]{1,0:T(8,128)(2,1)S(1)}, bf16[16,128]{1,0:T(8,128)(2,1)}, u32[]{:S(2)}) copy-start(bf16[16,128]{1,0:T(8,128)(2,1)} %constant.16.clone.a_two) | copy-start | bytes 12292
  14.0 8.7 %copy-start.7 = (bf16[16,32]{1,0:T(8,128)(2,1)S(1)}, bf16[16,32]{1,0:T(8,128)(2,1)}, u32[]{:S(2)}) copy-start(bf16[16,32]{1,0:T(8,128)(2,1)} %constant.17.clone.a_corner) | copy-start | bytes 3076
  14.0 8.7 %collective-permute-start.5 = (f32[2,8,128]{2,1,0:T(8,128)S(1)}, f32[2,8,128]{2,1,0:T(8,128)S(1)}, u32[]{:S(2)}, u32[]{:S(2)}) collective-permute-start(f32[2,8,128]{2,1,0:T(8,128)S(1)} %get-tuple-element.27), channel_id=1, source_target_pairs={{0,16},{16,0},{32,48},{48,32},{64,80},{80,64},{96,112},{112,96},{1... | collective-permute-start | bytes 24584 | tf_op jit(solution)/shard_map/ppermute | solution.py:491

commit v6 on v5

--- a/solution.py
+++ b/solution.py
@@ -81,8 +81,8 @@
     return lax.axis_index(axis) % 2
 
 
-def z_messages(fields, r, t):
-    pair, odd = lanes() // 16, (lanes() // 8) % 2 == 1
+def z_tiles(fields, r, t):
+    pair = lanes() // 16
     tile = [None, None]
     for j in range(4 if t < 2 else 3):
         for s in range(4):
@@ -90,7 +90,7 @@
             one = roll(fields[plane_of(4 * t + j, s), r : r + 8, :], 16 * c + 8)
             half = tile[j % 2]
             tile[j % 2] = one if half is None else jnp.where(pair == c, one, half)
-    return jnp.where(odd, tile[1], roll(tile[0], -8)), jnp.where(odd, roll(tile[1], 8), tile[0])
+    return tile
 
 
 def pack_z(mom, sca, vel, nuc, gro, far, near, fields, sems):
@@ -109,13 +109,15 @@
             copies[-1][-1].start()
             n += 1
     right = odd_of("gz") == 0
+    odd = (lanes() // 8) % 2 == 1
     for t in range(3):
         for copy in copies[t]:
             copy.wait()
-        for r in range(0, 64, 8):
-            zl, zr = z_messages(fields, r, t)
-            far[t, r : r + 8, :] = jnp.where(right, zl, zr)
-            near[t, r : r + 8, :] = jnp.where(right, zr, zl)
+        made = [z_tiles(fields, r, t) for r in range(0, 64, 8)]
+        for n, (one, two) in enumerate(made):
+            zl, zr = jnp.where(odd, two, roll(one, -8)), jnp.where(odd, roll(two, 8), one)
+            far[t, 8 * n : 8 * n + 8, :] = jnp.where(right, zl, zr)
+            near[t, 8 * n : 8 * n + 8, :] = jnp.where(right, zr, zl)
 
 
 def halves(first):
@@ -128,11 +130,8 @@
     for k, msg in enumerate((first, second)):
         low = odd if k == 0 else jnp.logical_not(odd)
         at = pl.ds(pl.multiple_of(jnp.where(low, 0, 56), 8), 8)
-        for i in range(38):
+        for i in range(36):
             msg[i] = fields[i, at, :]
-        keep = halves(low.astype(jnp.int32))
-        for n, (i, j) in enumerate(((38, 39), (40, 42), (41, 43))):
-            msg[38 + n] = jnp.where(keep, fields[i, at, :], pltpu.roll(fields[j, at, :], 4, 0))
 
 
 def outer_tile(from_left, from_right):
@@ -144,7 +143,7 @@
     return jnp.where(right, far, near), jnp.where(right, near, far)
 
 
-def corners(near, far, part, first, second):
+def corners(near, far, part, fields, first, second):
     del part
     odd = odd_of("gx") == 1
     for k, msg in enumerate((first, second)):
@@ -154,6 +153,10 @@
         tile = [outer_tile(*sides(near[t, at, :], far[t, at, :])) for t in range(3)]
         msg[0] = jnp.where(keep, tile[0], pltpu.roll(tile[1], 4, 0))
         msg[1] = jnp.where(keep, tile[2], 0.0)
+        for i in range(2):
+            msg[2 + i] = fields[36 + i, at, :]
+        for n, (i, j) in enumerate(((38, 39), (40, 42), (41, 43))):
+            msg[4 + n] = jnp.where(keep, fields[i, at, :], pltpu.roll(fields[j, at, :], 4, 0))
 
 
 def spread(tile, j):
@@ -371,9 +374,9 @@
     at_c = lambda ref, *i: jnp.where(front, ref[*i, 8:16, :], ref[*i, 48:56, :])
     other_h = lambda a, b, i: pltpu.roll(at_o(a, b, i), 4, 0)
 
-    uh = [at_h(first, second, 36 + ny) for ny in range(2)]
-    uo = [at_o(first, second, 36 + ny) for ny in range(2)]
-    wh = [at_h(first, second, 38) * one, other_h(first, second, 38) * one]
+    uh = [at_h(first_corner, second_corner, 2 + ny) for ny in range(2)]
+    uo = [at_o(first_corner, second_corner, 2 + ny) for ny in range(2)]
+    wh = [at_h(first_corner, second_corner, 4) * one, other_h(first_corner, second_corner, 4) * one]
     ua = [at_a(fields, 36 + ny) for ny in range(2)]
     u_ho = [pair(uh[ny], uo[ny]) * one for ny in range(2)]
     u_hc = [pair(uh[ny], at_c(fields, 36 + ny)) * two for ny in range(2)]
@@ -425,7 +428,7 @@
             s1a[i] = at_a(q1, i) + x_i[8:16]
     for ny in range(2):
         src = sources(
-            lambda k: hs(2 * k + ny), at_h(first, second, 39 + ny), other_h(first, second, 39 + ny), dt
+            lambda k: hs(2 * k + ny), at_h(first_corner, second_corner, 5 + ny), other_h(first_corner, second_corner, 5 + ny), dt
         )
         for k in range(7):
             s1h[2 * k + ny] += src[k]
@@ -511,7 +514,7 @@
         scratch_shapes=[pltpu.SemaphoreType.DMA((10,))],
     )(*flat)
     far = swap(z_far, "gz", 1)
-    x_first, x_second, z_near = call(x_messages, [(41, 8, 128), (41, 8, 128), (3, 64, 128)], 10**5)(fields, z_near)
+    x_first, x_second, z_near = call(x_messages, [(36, 8, 128), (36, 8, 128), (3, 64, 128)], 10**5)(fields, z_near)
     near = swap(z_near, "gz", 0)
     (part,) = call(
         first_stage,
@@ -522,7 +525,7 @@
     )(diffusivity, fields, a_rows, z_main)
     second = swap(x_second, "gx", 1)
     first = swap(x_first, "gx", 0)
-    c_first, c_second = call(corners, [(2, 8, 128)] * 2, 10**6)(near, far, part)
+    c_first, c_second = call(corners, [(7, 8, 128)] * 2, 10**6)(near, far, part, fields)
     second_corner = swap(c_second, "gx", 1)
     first_corner = swap(c_first, "gx", 0)
     q1, pq1, pws, half = call(

time: 25.5 us -> 24.8 us (0.973)
  the two profiles are of different devices: /device:TPU:121 before, /device:TPU:0 now
where the time goes in v6:
time: 24.8 us; the launch traced here: 24.7 us
  starting transfers between devices  11.4 us (46%)
  Pallas kernels  9.26 us (37%)
  waiting for transfers between devices  2.37 us (10%)
  local copies, waits for them, and re-layouts  0.84 us (3%)
  between operations  0.8 us (3%)
    ppermute x6, starting transfers between devices, swap(): return lax.ppermute(value, axis, [(i, other(i)) for i in range(peers)])  11.4 us
    pallas_call x1, Pallas kernels, body(): call(interior, [(36, 64, 128), (3, 64, 128), (64, 128), (36, 64, 128)], 1...  2.67 us
    pallas_call x1, Pallas kernels, body(): call(edges, [(12, 64, 128), (24, 64, 128)], 10 ** 8, in_specs=[smem] + [v...  2.59 us
    ppermute x6, waiting for transfers between devices, swap(): return lax.ppermute(value, axis, [(i, other(i)) for i in range(peers)])  2.37 us
    pallas_call x1, Pallas kernels, body(): call(pack_z, [(3, 64, 128), (3, 64, 128), (44, 64, 128)], 10 ** 6, in_spe...  1.97 us
    pallas_call x1, Pallas kernels, body(): call(first_stage, [(36, 64, 128)], 10 ** 7, in_specs=[smem] + [vmem] * 3,...  1.94 us
    unnamed x16, local copies, waits for them, and re-layouts  0.84 us
  transfers between devices with their start and end apart: 6, of which 1 were waited for; matrix products, arithmetic and copies ran while one was open for 0% of the time, Pallas kernels for 19%

profile of v6, /device:TPU:0, one launch (start us, length us, event | category | flops | bytes accessed | tf_op | source)
XLA Modules:
  0.0 24.7 jit_solution(9070522780563945382)
XLA Ops:
  0.6 0.0 copy-start
  0.6 0.0 copy-start.3
  0.7 2.0 %shard_map.140 = (f32[3,64,128]{2,1,0:T(8,128)S(1)}, f32[3,64,128]{2,1,0:T(8,128)S(1)}, f32[44,64,128]{2,1,0:T(8,128)S(1)}) custom-call(f32[12,64,128]{2,1,0:T(8,128)} %bitcast.6, f32[24,64,128]{2,1,0:T(8,128)} %bitcast.5, f32[4,64,128]{2,1,0:T(8,128)} %bitcast.7, f32[2,64,128]{2,1,0:T(8,128)} %nuc.1, f32[2,64,128]{2,1,0:T(8,128)} %gro.1), custom_call_target="tpu_custom_call" | custom-call | flops 1000000 | bytes 250000 | tf_op jit(solution)/shard_map/pallas_call | solution.py:508
  2.6 0.1 shard_map.142
  2.7 0.1 collective-permute-start
  2.8 3.8 %collective-permute-start.1 = (f32[3,64,128]{2,1,0:T(8,128)S(1)}, f32[3,64,128]{2,1,0:T(8,128)S(1)}, u32[]{:S(2)}, u32[]{:S(2)}) collective-permute-start(f32[3,64,128]{2,1,0:T(8,128)S(1)} %get-tuple-element.19.z_far), channel_id=1, source_target_pairs={{0,15},{1,2},{2,1},{3,4},{4,3},{5,6},{6,5},{7,8},{8,7},{9,10},{10,... | collective-permute-start | bytes 294920 | tf_op jit(solution)/shard_map/ppermute | solution.py:494
  6.6 0.6 %collective-permute-start.2 = (f32[36,8,128]{2,1,0:T(8,128)S(1)}, f32[36,8,128]{2,1,0:T(8,128)S(1)}, u32[]{:S(2)}, u32[]{:S(2)}) collective-permute-start(f32[36,8,128]{2,1,0:T(8,128)S(1)} %get-tuple-element.24), channel_id=1, source_target_pairs={{0,16},{16,0},{32,48},{48,32},{64,80},{80,64},{96,112},{112,96},{1... | collective-permute-start | bytes 442376 | tf_op jit(solution)/shard_map/ppermute | solution.py:494
  7.2 6.7 %collective-permute-start.3 = (f32[36,8,128]{2,1,0:T(8,128)S(1)}, f32[36,8,128]{2,1,0:T(8,128)S(1)}, u32[]{:S(2)}, u32[]{:S(2)}) collective-permute-start(f32[36,8,128]{2,1,0:T(8,128)S(1)} %get-tuple-element.25), channel_id=1, source_target_pairs={{0,240},{16,32},{32,16},{48,64},{64,48},{80,96},{96,80},{112,128},... | collective-permute-start | bytes 442376 | tf_op jit(solution)/shard_map/ppermute | solution.py:494
  14.0 1.9 %shard_map.141.part = f32[36,64,128]{2,1,0:T(8,128)S(1)} custom-call(f32[18]{0:T(128)S(1)} %copy-done.4, f32[44,64,128]{2,1,0:T(8,128)S(1)} %get-tuple-element.16.fields, bf16[64,256]{1,0:T(8,128)(2,1)S(1)} %copy-done.3, bf16[512,128]{1,0:T(8,128)(2,1)S(1)} %copy-done), custom_call_target="tpu_custom_call" | custom-call | flops 10000000 | bytes 2500000 | tf_op jit(solution)/shard_map/pallas_call | solution.py:519
  15.9 0.0 copy-start.1
  15.9 0.0 copy-start.2
  16.0 0.0 collective-permute-done.1.far
  16.0 0.1 collective-permute-start.4
  16.1 0.0 copy-start.6
  16.1 0.0 copy-start.7
  16.1 0.1 collective-permute-start.5
  16.2 0.6 %copy-done.1 = bf16[512,128]{1,0:T(8,128)(2,1)S(1)} copy-done((bf16[512,128]{1,0:T(8,128)(2,1)S(1)}, bf16[512,128]{1,0:T(8,128)(2,1)}, u32[]{:S(2)}) %copy-start.1) | copy-done | bytes 131096
  16.8 0.2 copy-done.2
  17.0 2.7 %shard_map.143 = (f32[36,64,128]{2,1,0:T(8,128)S(1)}, f32[3,64,128]{2,1,0:T(8,128)S(1)}, f32[64,128]{1,0:T(8,128)S(1)}, f32[36,64,128]{2,1,0:T(8,128)S(1)}) custom-call(f32[18]{0:T(128)S(1)} %copy-done.4, f32[44,64,128]{2,1,0:T(8,128)S(1)} %get-tuple-element.16.fields, f32[36,64,128]{2,1,0:T(8,128)S(1)} %shard_map.141.part, ...), custom_call_target="tpu_custom_call" | custom-call | flops 1000000000 | bytes 250000000 | tf_op jit(solution)/shard_map/pallas_call | solution.py:531
  19.7 2.4 %collective-permute-done.4.second_corner = f32[7,8,128]{2,1,0:T(8,128)S(1)} collective-permute-done((f32[7,8,128]{2,1,0:T(8,128)S(1)}, f32[7,8,128]{2,1,0:T(8,128)S(1)}, u32[]{:S(2)}, u32[]{:S(2)}) %collective-permute-start.4) | collective-permute-done | bytes 28704 | tf_op jit(solution)/shard_map/ppermute | solution.py:494
  22.1 0.0 collective-permute-done.5.first_corner
  22.1 0.0 collective-permute-done.2.first
  22.1 0.0 collective-permute-done.3.second
  22.1 2.6 %shard_map.145 = (f32[12,64,128]{2,1,0:T(8,128)}, f32[24,64,128]{2,1,0:T(8,128)}) custom-call(f32[18]{0:T(128)S(1)} %copy-done.4, f32[44,64,128]{2,1,0:T(8,128)S(1)} %get-tuple-element.16.fields, f32[36,64,128]{2,1,0:T(8,128)S(1)} %get-tuple-element.20.q1, f32[3,64,128]{2,1,0:T(8,128)S(1)} %get-tuple-element.21.pq1, f32[64,128]{1,0:T(8,128)S(1)} %get-tuple-element.22.pws, ...), custom_call_target="tpu_custom_call" | custom-call | flops 100000000 | bytes 25000000 | tf_op jit(solution)/shard_map/pallas_call | solution.py:538
  (10 shorter events, 0.1 us)
Async XLA Ops:
  0.6 13.3 %copy-start = (bf16[512,128]{1,0:T(8,128)(2,1)S(1)}, bf16[512,128]{1,0:T(8,128)(2,1)}, u32[]{:S(2)}) copy-start(bf16[512,128]{1,0:T(8,128)(2,1)} %constant.18.clone.z_main) | copy-start | bytes 393220
  0.6 13.3 %copy-start.3 = (bf16[64,256]{1,0:T(8,128)(2,1)S(1)}, bf16[64,256]{1,0:T(8,128)(2,1)}, u32[]{:S(2)}) copy-start(bf16[64,256]{1,0:T(8,128)(2,1)} %constant.14.clone.a_rows) | copy-start | bytes 98308
  0.7 13.3 %copy-start.4 = (f32[18]{0:T(128)S(1)}, f32[18]{0:T(128)}, u32[]{:S(2)}) copy-start(f32[18]{0:T(128)} %kappa.5) | copy-start | bytes 220
  2.7 13.2 %collective-permute-start = (f32[3,64,128]{2,1,0:T(8,128)S(1)}, f32[3,64,128]{2,1,0:T(8,128)S(1)}, u32[]{:S(2)}, u32[]{:S(2)}) collective-permute-start(f32[3,64,128]{2,1,0:T(8,128)S(1)} %get-tuple-element.18.z_near), channel_id=1, source_target_pairs={{0,1},{1,0},{2,3},{3,2},{4,5},{5,4},{6,7},{7,6},{8,9},{9,8},{10,11... | collective-permute-start | bytes 294920 | tf_op jit(solution)/shard_map/ppermute | solution.py:494
  2.8 13.2 %collective-permute-start.1 = (f32[3,64,128]{2,1,0:T(8,128)S(1)}, f32[3,64,128]{2,1,0:T(8,128)S(1)}, u32[]{:S(2)}, u32[]{:S(2)}) collective-permute-start(f32[3,64,128]{2,1,0:T(8,128)S(1)} %get-tuple-element.19.z_far), channel_id=1, source_target_pairs={{0,15},{1,2},{2,1},{3,4},{4,3},{5,6},{6,5},{7,8},{8,7},{9,10},{10,... | collective-permute-start | bytes 294920 | tf_op jit(solution)/shard_map/ppermute | solution.py:494
  6.6 15.4 %collective-permute-start.2 = (f32[36,8,128]{2,1,0:T(8,128)S(1)}, f32[36,8,128]{2,1,0:T(8,128)S(1)}, u32[]{:S(2)}, u32[]{:S(2)}) collective-permute-start(f32[36,8,128]{2,1,0:T(8,128)S(1)} %get-tuple-element.24), channel_id=1, source_target_pairs={{0,16},{16,0},{32,48},{48,32},{64,80},{80,64},{96,112},{112,96},{1... | collective-permute-start | bytes 442376 | tf_op jit(solution)/shard_map/ppermute | solution.py:494
  7.2 14.8 %collective-permute-start.3 = (f32[36,8,128]{2,1,0:T(8,128)S(1)}, f32[36,8,128]{2,1,0:T(8,128)S(1)}, u32[]{:S(2)}, u32[]{:S(2)}) collective-permute-start(f32[36,8,128]{2,1,0:T(8,128)S(1)} %get-tuple-element.25), channel_id=1, source_target_pairs={{0,240},{16,32},{32,16},{48,64},{64,48},{80,96},{96,80},{112,128},... | collective-permute-start | bytes 442376 | tf_op jit(solution)/shard_map/ppermute | solution.py:494
  15.9 0.9 %copy-start.1 = (bf16[512,128]{1,0:T(8,128)(2,1)S(1)}, bf16[512,128]{1,0:T(8,128)(2,1)}, u32[]{:S(2)}) copy-start(bf16[512,128]{1,0:T(8,128)(2,1)} %constant.20.clone.z_inner) | copy-start | bytes 393220
  15.9 1.1 %copy-start.2 = (bf16[2048,128]{1,0:T(8,128)(2,1)S(1)}, bf16[2048,128]{1,0:T(8,128)(2,1)}, u32[]{:S(2)}) copy-start(bf16[2048,128]{1,0:T(8,128)(2,1)} %constant.19.clone.z_outer) | copy-start | bytes 1572868
  16.0 6.1 %collective-permute-start.4 = (f32[7,8,128]{2,1,0:T(8,128)S(1)}, f32[7,8,128]{2,1,0:T(8,128)S(1)}, u32[]{:S(2)}, u32[]{:S(2)}) collective-permute-start(f32[7,8,128]{2,1,0:T(8,128)S(1)} %get-tuple-element.26), channel_id=1, source_target_pairs={{0,240},{16,32},{32,16},{48,64},{64,48},{80,96},{96,80},{112,128},... | collective-permute-start | bytes 86024 | tf_op jit(solution)/shard_map/ppermute | solution.py:494
  16.1 6.0 %copy-start.5 = (bf16[16,96]{1,0:T(8,128)(2,1)S(1)}, bf16[16,96]{1,0:T(8,128)(2,1)}, u32[]{:S(2)}) copy-start(bf16[16,96]{1,0:T(8,128)(2,1)} %constant.15.clone.a_one) | copy-start | bytes 9220
  16.1 6.0 %copy-start.6 = (bf16[16,128]{1,0:T(8,128)(2,1)S(1)}, bf16[16,128]{1,0:T(8,128)(2,1)}, u32[]{:S(2)}) copy-start(bf16[16,128]{1,0:T(8,128)(2,1)} %constant.16.clone.a_two) | copy-start | bytes 12292
  16.1 6.0 %copy-start.7 = (bf16[16,32]{1,0:T(8,128)(2,1)S(1)}, bf16[16,32]{1,0:T(8,128)(2,1)}, u32[]{:S(2)}) copy-start(bf16[16,32]{1,0:T(8,128)(2,1)} %constant.17.clone.a_corner) | copy-start | bytes 3076
  16.1 5.9 %collective-permute-start.5 = (f32[7,8,128]{2,1,0:T(8,128)S(1)}, f32[7,8,128]{2,1,0:T(8,128)S(1)}, u32[]{:S(2)}, u32[]{:S(2)}) collective-permute-start(f32[7,8,128]{2,1,0:T(8,128)S(1)} %get-tuple-element.27), channel_id=1, source_target_pairs={{0,16},{16,0},{32,48},{48,32},{64,80},{80,64},{96,112},{112,96},{1... | collective-permute-start | bytes 86024 | tf_op jit(solution)/shard_map/ppermute | solution.py:494

commit v7 on v6

--- a/solution.py
+++ b/solution.py
@@ -124,8 +124,7 @@
     return (lax.broadcasted_iota(jnp.int32, (8, 128), 0) + 4 * first) % 8 >= 4
 
 
-def x_messages(fields, z_near, first, second, near):
-    near[...] = z_near[...]
+def x_messages(fields, first, second):
     odd = odd_of("gx") == 1
     for k, msg in enumerate((first, second)):
         low = odd if k == 0 else jnp.logical_not(odd)
@@ -276,7 +275,7 @@
 
 def interior(
     kappa, fields, part, z_near, z_far, near, far, a_rows, z_main, z_outer, z_inner, q1, pq1, pws, half,
-    us, ws, el, cor,
+    us, ws, el, cor, cor_two,
 ):
     dt, scale = time_step, 0.5 * time_step
     kap = [block_kappa(kappa, t) for t in range(3)]
@@ -310,20 +309,17 @@
         pq1[t] = outer[t] + x[:, 128 * t : 128 * t + 128] + z[64 * t : 64 * t + 64]
     for t, src in enumerate(block_sources(outer, dt)):
         pq1[t] += src
-    for p in range(9):
-        for i, field, ny, t, b in planes(p):
-            q1[i] = part[i] + unpack(cor[64 * t : 64 * t + 64, :], b)
-
     plane_velocities(fields, us, ws, scale)
     for t in range(3):
         e = pq1[t, 8:56, :]
         el[48 * t : 48 * t + 48, 0:512] = across((kap[t] * (scale / second_part)) * e, (0.5 * pws[8:56, :]) * e)
-    cor[0:144, :] = dot(el[0:144, 0:512], z_inner[...])
+    cor_two[...] = dot(el[0:144, 0:512], z_inner[...])
 
     def two(p):
         lhs, rhs = [], []
         for i, field, ny, t, b in planes(p):
-            v = q1[i]
+            v = part[i] + unpack(cor[64 * t : 64 * t + 64, :], b)
+            q1[i] = v
             kq = (kappa[field] * (scale / second_part)) * v
             mid = v[8:56]
             lhs.append(across(kq[8:56], ws[ny, 8:56, :] * mid))
@@ -335,7 +331,7 @@
                 0.5 * (fields[i, 8:56, :] + q1[i, 8:56, :])
                 + z[48 * n : 48 * n + 48]
                 + x[n // 2][:, 128 * ny : 128 * ny + 128]
-                + unpack(cor[48 * t : 48 * t + 48, :], b)
+                + unpack(cor_two[48 * t : 48 * t + 48, :], b)
             )
 
     for p in range(9):
@@ -514,7 +510,7 @@
         scratch_shapes=[pltpu.SemaphoreType.DMA((10,))],
     )(*flat)
     far = swap(z_far, "gz", 1)
-    x_first, x_second, z_near = call(x_messages, [(36, 8, 128), (36, 8, 128), (3, 64, 128)], 10**5)(fields, z_near)
+    x_first, x_second = call(x_messages, [(36, 8, 128), (36, 8, 128)], 10**5)(fields)
     near = swap(z_near, "gz", 0)
     (part,) = call(
         first_stage,
@@ -533,7 +529,7 @@
         [(36, 64, 128), (3, 64, 128), (64, 128), (36, 64, 128)],
         10 * 10**8,
         in_specs=[smem] + [vmem] * 10,
-        scratch_shapes=[tiles(2, 64), tiles(2, 64), pltpu.VMEM((192, 2048), BF16), tiles(192)],
+        scratch_shapes=[tiles(2, 64), tiles(2, 64), pltpu.VMEM((192, 2048), BF16), tiles(192), tiles(144)],
     )(diffusivity, fields, part, z_near, z_far, near, far, a_rows, z_main, z_outer, z_inner)
     out_mom, out_sca = call(
         edges,

time: 24.8 us -> 24.9 us (level)
  no operation moved by 1% of the time
where the time goes in v7:
time: 24.9 us; the launch traced here: 24.8 us
  starting transfers between devices  11.5 us (46%)
  Pallas kernels  9.28 us (37%)
  waiting for transfers between devices  2.35 us (9%)
  local copies, waits for them, and re-layouts  0.84 us (3%)
  between operations  0.79 us (3%)
    ppermute x6, starting transfers between devices, swap(): return lax.ppermute(value, axis, [(i, other(i)) for i in range(peers)])  11.5 us
    pallas_call x1, Pallas kernels, body(): call(interior, [(36, 64, 128), (3, 64, 128), (64, 128), (36, 64, 128)], 1...  2.69 us
    pallas_call x1, Pallas kernels, body(): call(edges, [(12, 64, 128), (24, 64, 128)], 10 ** 8, in_specs=[smem] + [v...  2.6 us
    ppermute x6, waiting for transfers between devices, swap(): return lax.ppermute(value, axis, [(i, other(i)) for i in range(peers)])  2.35 us
    pallas_call x1, Pallas kernels, body(): call(pack_z, [(3, 64, 128), (3, 64, 128), (44, 64, 128)], 10 ** 6, in_spe...  1.97 us
    pallas_call x1, Pallas kernels, body(): call(first_stage, [(36, 64, 128)], 10 ** 7, in_specs=[smem] + [vmem] * 3,...  1.95 us
    unnamed x16, local copies, waits for them, and re-layouts  0.84 us
  transfers between devices with their start and end apart: 6, of which 1 were waited for; matrix products, arithmetic and copies ran while one was open for 0% of the time, Pallas kernels for 19%

profile of v7, /device:TPU:0, one launch (start us, length us, event | category | flops | bytes accessed | tf_op | source)
XLA Modules:
  0.0 24.8 jit_solution(15303358508562757153)
XLA Ops:
  0.6 0.0 copy-start
  0.6 0.0 copy-start.3
  0.7 2.0 %shard_map.140 = (f32[3,64,128]{2,1,0:T(8,128)S(1)}, f32[3,64,128]{2,1,0:T(8,128)S(1)}, f32[44,64,128]{2,1,0:T(8,128)S(1)}) custom-call(f32[12,64,128]{2,1,0:T(8,128)} %bitcast.6, f32[24,64,128]{2,1,0:T(8,128)} %bitcast.5, f32[4,64,128]{2,1,0:T(8,128)} %bitcast.7, f32[2,64,128]{2,1,0:T(8,128)} %nuc.1, f32[2,64,128]{2,1,0:T(8,128)} %gro.1), custom_call_target="tpu_custom_call" | custom-call | flops 1000000 | bytes 250000 | tf_op jit(solution)/shard_map/pallas_call | solution.py:504
  2.6 0.1 collective-permute-start
  2.7 3.8 %collective-permute-start.1 = (f32[3,64,128]{2,1,0:T(8,128)S(1)}, f32[3,64,128]{2,1,0:T(8,128)S(1)}, u32[]{:S(2)}, u32[]{:S(2)}) collective-permute-start(f32[3,64,128]{2,1,0:T(8,128)S(1)} %get-tuple-element.17.z_far), channel_id=1, source_target_pairs={{0,15},{1,2},{2,1},{3,4},{4,3},{5,6},{6,5},{7,8},{8,7},{9,10},{10,... | collective-permute-start | bytes 294920 | tf_op jit(solution)/shard_map/ppermute | solution.py:490
  6.6 0.7 %collective-permute-start.2 = (f32[36,8,128]{2,1,0:T(8,128)S(1)}, f32[36,8,128]{2,1,0:T(8,128)S(1)}, u32[]{:S(2)}, u32[]{:S(2)}) collective-permute-start(f32[36,8,128]{2,1,0:T(8,128)S(1)} %get-tuple-element.22), channel_id=1, source_target_pairs={{0,16},{16,0},{32,48},{48,32},{64,80},{80,64},{96,112},{112,96},{1... | collective-permute-start | bytes 442376 | tf_op jit(solution)/shard_map/ppermute | solution.py:490
  7.3 6.7 %collective-permute-start.3 = (f32[36,8,128]{2,1,0:T(8,128)S(1)}, f32[36,8,128]{2,1,0:T(8,128)S(1)}, u32[]{:S(2)}, u32[]{:S(2)}) collective-permute-start(f32[36,8,128]{2,1,0:T(8,128)S(1)} %get-tuple-element.23), channel_id=1, source_target_pairs={{0,240},{16,32},{32,16},{48,64},{64,48},{80,96},{96,80},{112,128},... | collective-permute-start | bytes 442376 | tf_op jit(solution)/shard_map/ppermute | solution.py:490
  14.0 2.0 %shard_map.141.part = f32[36,64,128]{2,1,0:T(8,128)S(1)} custom-call(f32[18]{0:T(128)S(1)} %copy-done.4, f32[44,64,128]{2,1,0:T(8,128)S(1)} %get-tuple-element.15.fields, bf16[64,256]{1,0:T(8,128)(2,1)S(1)} %copy-done.3, bf16[512,128]{1,0:T(8,128)(2,1)S(1)} %copy-done), custom_call_target="tpu_custom_call" | custom-call | flops 10000000 | bytes 2500000 | tf_op jit(solution)/shard_map/pallas_call | solution.py:515
  16.0 0.0 copy-start.1
  16.0 0.0 copy-start.2
  16.0 0.0 collective-permute-done.near
  16.0 0.0 collective-permute-done.1.far
  16.1 0.1 collective-permute-start.4
  16.2 0.0 copy-start.5
  16.2 0.0 copy-start.6
  16.2 0.0 copy-start.7
  16.2 0.1 collective-permute-start.5
  16.3 0.6 %copy-done.1 = bf16[512,128]{1,0:T(8,128)(2,1)S(1)} copy-done((bf16[512,128]{1,0:T(8,128)(2,1)S(1)}, bf16[512,128]{1,0:T(8,128)(2,1)}, u32[]{:S(2)}) %copy-start.1) | copy-done | bytes 131096
  16.9 0.2 copy-done.2
  17.1 2.7 %shard_map.142 = (f32[36,64,128]{2,1,0:T(8,128)S(1)}, f32[3,64,128]{2,1,0:T(8,128)S(1)}, f32[64,128]{1,0:T(8,128)S(1)}, f32[36,64,128]{2,1,0:T(8,128)S(1)}) custom-call(f32[18]{0:T(128)S(1)} %copy-done.4, f32[44,64,128]{2,1,0:T(8,128)S(1)} %get-tuple-element.15.fields, f32[36,64,128]{2,1,0:T(8,128)S(1)} %shard_map.141.part, ...), custom_call_target="tpu_custom_call" | custom-call | flops 1000000000 | bytes 250000000 | tf_op jit(solution)/shard_map/pallas_call | solution.py:527
  19.8 2.3 %collective-permute-done.4.second_corner = f32[7,8,128]{2,1,0:T(8,128)S(1)} collective-permute-done((f32[7,8,128]{2,1,0:T(8,128)S(1)}, f32[7,8,128]{2,1,0:T(8,128)S(1)}, u32[]{:S(2)}, u32[]{:S(2)}) %collective-permute-start.4) | collective-permute-done | bytes 28704 | tf_op jit(solution)/shard_map/ppermute | solution.py:490
  22.2 0.0 collective-permute-done.2.first
  22.2 0.0 collective-permute-done.3.second
  22.2 2.6 %shard_map.145 = (f32[12,64,128]{2,1,0:T(8,128)}, f32[24,64,128]{2,1,0:T(8,128)}) custom-call(f32[18]{0:T(128)S(1)} %copy-done.4, f32[44,64,128]{2,1,0:T(8,128)S(1)} %get-tuple-element.15.fields, f32[36,64,128]{2,1,0:T(8,128)S(1)} %get-tuple-element.18.q1, f32[3,64,128]{2,1,0:T(8,128)S(1)} %get-tuple-element.19.pq1, f32[64,128]{1,0:T(8,128)S(1)} %get-tuple-element.20.pws, ...), custom_call_target="tpu_custom_call" | custom-call | flops 100000000 | bytes 25000000 | tf_op jit(solution)/shard_map/pallas_call | solution.py:534
  (10 shorter events, 0.1 us)
Async XLA Ops:
  0.6 13.4 %copy-start = (bf16[512,128]{1,0:T(8,128)(2,1)S(1)}, bf16[512,128]{1,0:T(8,128)(2,1)}, u32[]{:S(2)}) copy-start(bf16[512,128]{1,0:T(8,128)(2,1)} %constant.18.clone.z_main) | copy-start | bytes 393220
  0.6 13.4 %copy-start.3 = (bf16[64,256]{1,0:T(8,128)(2,1)S(1)}, bf16[64,256]{1,0:T(8,128)(2,1)}, u32[]{:S(2)}) copy-start(bf16[64,256]{1,0:T(8,128)(2,1)} %constant.14.clone.a_rows) | copy-start | bytes 98308
  0.7 13.4 %copy-start.4 = (f32[18]{0:T(128)S(1)}, f32[18]{0:T(128)}, u32[]{:S(2)}) copy-start(f32[18]{0:T(128)} %kappa.5) | copy-start | bytes 220
  2.6 13.4 %collective-permute-start = (f32[3,64,128]{2,1,0:T(8,128)S(1)}, f32[3,64,128]{2,1,0:T(8,128)S(1)}, u32[]{:S(2)}, u32[]{:S(2)}) collective-permute-start(f32[3,64,128]{2,1,0:T(8,128)S(1)} %get-tuple-element.16.z_near), channel_id=1, source_target_pairs={{0,1},{1,0},{2,3},{3,2},{4,5},{5,4},{6,7},{7,6},{8,9},{9,8},{10,11... | collective-permute-start | bytes 294920 | tf_op jit(solution)/shard_map/ppermute | solution.py:490
  2.7 13.3 %collective-permute-start.1 = (f32[3,64,128]{2,1,0:T(8,128)S(1)}, f32[3,64,128]{2,1,0:T(8,128)S(1)}, u32[]{:S(2)}, u32[]{:S(2)}) collective-permute-start(f32[3,64,128]{2,1,0:T(8,128)S(1)} %get-tuple-element.17.z_far), channel_id=1, source_target_pairs={{0,15},{1,2},{2,1},{3,4},{4,3},{5,6},{6,5},{7,8},{8,7},{9,10},{10,... | collective-permute-start | bytes 294920 | tf_op jit(solution)/shard_map/ppermute | solution.py:490
  6.6 15.5 %collective-permute-start.2 = (f32[36,8,128]{2,1,0:T(8,128)S(1)}, f32[36,8,128]{2,1,0:T(8,128)S(1)}, u32[]{:S(2)}, u32[]{:S(2)}) collective-permute-start(f32[36,8,128]{2,1,0:T(8,128)S(1)} %get-tuple-element.22), channel_id=1, source_target_pairs={{0,16},{16,0},{32,48},{48,32},{64,80},{80,64},{96,112},{112,96},{1... | collective-permute-start | bytes 442376 | tf_op jit(solution)/shard_map/ppermute | solution.py:490
  7.3 14.9 %collective-permute-start.3 = (f32[36,8,128]{2,1,0:T(8,128)S(1)}, f32[36,8,128]{2,1,0:T(8,128)S(1)}, u32[]{:S(2)}, u32[]{:S(2)}) collective-permute-start(f32[36,8,128]{2,1,0:T(8,128)S(1)} %get-tuple-element.23), channel_id=1, source_target_pairs={{0,240},{16,32},{32,16},{48,64},{64,48},{80,96},{96,80},{112,128},... | collective-permute-start | bytes 442376 | tf_op jit(solution)/shard_map/ppermute | solution.py:490
  16.0 0.9 %copy-start.1 = (bf16[512,128]{1,0:T(8,128)(2,1)S(1)}, bf16[512,128]{1,0:T(8,128)(2,1)}, u32[]{:S(2)}) copy-start(bf16[512,128]{1,0:T(8,128)(2,1)} %constant.20.clone.z_inner) | copy-start | bytes 393220
  16.0 1.1 %copy-start.2 = (bf16[2048,128]{1,0:T(8,128)(2,1)S(1)}, bf16[2048,128]{1,0:T(8,128)(2,1)}, u32[]{:S(2)}) copy-start(bf16[2048,128]{1,0:T(8,128)(2,1)} %constant.19.clone.z_outer) | copy-start | bytes 1572868
  16.1 6.1 %collective-permute-start.4 = (f32[7,8,128]{2,1,0:T(8,128)S(1)}, f32[7,8,128]{2,1,0:T(8,128)S(1)}, u32[]{:S(2)}, u32[]{:S(2)}) collective-permute-start(f32[7,8,128]{2,1,0:T(8,128)S(1)} %get-tuple-element.24), channel_id=1, source_target_pairs={{0,240},{16,32},{32,16},{48,64},{64,48},{80,96},{96,80},{112,128},... | collective-permute-start | bytes 86024 | tf_op jit(solution)/shard_map/ppermute | solution.py:490
  16.2 6.0 %copy-start.5 = (bf16[16,96]{1,0:T(8,128)(2,1)S(1)}, bf16[16,96]{1,0:T(8,128)(2,1)}, u32[]{:S(2)}) copy-start(bf16[16,96]{1,0:T(8,128)(2,1)} %constant.15.clone.a_one) | copy-start | bytes 9220
  16.2 6.0 %copy-start.6 = (bf16[16,128]{1,0:T(8,128)(2,1)S(1)}, bf16[16,128]{1,0:T(8,128)(2,1)}, u32[]{:S(2)}) copy-start(bf16[16,128]{1,0:T(8,128)(2,1)} %constant.16.clone.a_two) | copy-start | bytes 12292
  16.2 6.0 %copy-start.7 = (bf16[16,32]{1,0:T(8,128)(2,1)S(1)}, bf16[16,32]{1,0:T(8,128)(2,1)}, u32[]{:S(2)}) copy-start(bf16[16,32]{1,0:T(8,128)(2,1)} %constant.17.clone.a_corner) | copy-start | bytes 3076
  16.2 5.9 %collective-permute-start.5 = (f32[7,8,128]{2,1,0:T(8,128)S(1)}, f32[7,8,128]{2,1,0:T(8,128)S(1)}, u32[]{:S(2)}, u32[]{:S(2)}) collective-permute-start(f32[7,8,128]{2,1,0:T(8,128)S(1)} %get-tuple-element.25), channel_id=1, source_target_pairs={{0,16},{16,0},{32,48},{48,32},{64,80},{80,64},{96,112},{112,96},{1... | collective-permute-start | bytes 86024 | tf_op jit(solution)/shard_map/ppermute | solution.py:490
